TPU v7x, 32 devices: a whole 2x2x4 slice. The times are simulated.
32 devices in a mesh: dp: 8 (over z, x), tensor: 4 (over y, core).
Axes of the slice: x: 2, y: 2, z: 4, core: 2. Of those that a mesh axis runs over, the one named last changes fastest.
Arguments:
- latent_tokens: bfloat16 [8, 1024, 1152], P('dp', None, 'tensor'), may hold values from -6 to 6
- timesteps: int32 [8], P('dp'), may hold values from 0 to 999, as said below
- labels: int32 [8], P('dp'), may hold values from 0 to 999
- class_table: bfloat16 [1000, 1152], replicated, may hold values from -6 to 6
- ada_weight: bfloat16 [1152, 6, 1152], P(None, None, 'tensor'), may hold values from -0.1875 to 0.1875
- ada_bias: bfloat16 [6, 1152], P(None, 'tensor'), may hold values from -4 to 4
- query_key_value_weight: bfloat16 [1152, 3, 1152], P(None, None, 'tensor'), may hold values from -0.1875 to 0.1875
- gate_weight: bfloat16 [1152, 16], P(None, 'tensor'), may hold values from -0.1875 to 0.1875
- gate_bias: bfloat16 [16], P('tensor'), may hold values from 1 to 7
- conv_weight: bfloat16 [3, 3, 1152], P(None, None, 'tensor'), may hold values from -5 to 5
- out_weight: bfloat16 [1152, 1152], P('tensor'), may hold values from -0.0014648438 to 0.0014648438
- up_weight: bfloat16 [1152, 4608], P(None, 'tensor'), may hold values from -0.23570226 to 0.23570226
- down_weight: bfloat16 [4608, 1152], P('tensor'), may hold values from -0.09375 to 0.09375
- cotangent: bfloat16 [8, 1024, 1152], P('dp', None, 'tensor'), may hold values from -6 to 6
Outputs:
- layer_out: bfloat16 [8, 1024, 1152], P('dp', None, 'tensor')
- grad_tokens: float32 [8, 1024, 1152], P('dp', None, 'tensor')
- grad_class: float32 [1000, 1152], P(None, 'dp')
- grad_ada_w: float32 [1152, 6, 1152], P('dp', None, 'tensor')
- grad_ada_b: float32 [6, 1152], P(None, 'tensor')
- grad_qkv: float32 [1152, 3, 1152], P('dp', None, 'tensor')
- grad_gate_w: float32 [1152, 16], P('dp', 'tensor')
- grad_gate_b: float32 [16], P('tensor')
- grad_conv: float32 [3, 3, 1152], P(None, None, 'tensor')
- grad_out_w: float32 [1152, 1152], P('tensor', 'dp')
- grad_up: float32 [1152, 4608], P('dp', 'tensor')
- grad_down: float32 [4608, 1152], P('tensor', 'dp')
Inputs may be any that keep to these rules, and one draw needn't show every extreme that they name: `timesteps`: timesteps per latent, smaller ones more common; every draw holds both ends of the range.
All inputs are finite; a program needn't handle non-finite values.
Results may differ from a plain program's by a relative error of at most 0.012.
The roundings to bfloat16 on the way count: a program that leaves them out, or rounds other values in their place, can miss the bound.
Values may be sent and summed in bfloat16 or wider, within the bound.
A program may use at most 192 MiB of HBM per device.

v0:
```python
from functools import partial
import math

import jax
import jax.numpy as jnp
from jax import lax
from jax.sharding import PartitionSpec as P

MODEL_DIM = 1152
HD = 72
NCLASS = 1000
GRID = 32
CH = 64


TOP_PRECISION = lax.Precision.HIGHEST
norm_eps = 1e-06


def embed_time(time_steps, model_width):
    half_width = model_width // 2
    frequency = jnp.exp(-math.log(10000.0) * jnp.arange(half_width, dtype=jnp.float32) / half_width)
    angles = time_steps.astype(jnp.float32)[:, None] * frequency[None, :]
    return jnp.concatenate([jnp.cos(angles), jnp.sin(angles)], axis=1)


def span_pass(running_state, block):
    query_matrix, key_matrix, value_matrix, log_forget = block
    block_len = log_forget.shape[1]
    decay_factors = jnp.cumsum(log_forget, axis=1)
    causal_mask = (jnp.arange(block_len)[:, None] >= jnp.arange(block_len)[None, :])[None]
    decay_gap = jnp.where(causal_mask, decay_factors[:, :, None] - decay_factors[:, None, :], 0.0)
    score_matrix = jnp.einsum("mkd,mld->mkl", query_matrix, key_matrix, precision=TOP_PRECISION)
    weighted_values = jnp.where(causal_mask, jnp.exp(decay_gap), 0.0) * score_matrix
    within_block_part = jnp.einsum(
        "dps,dsh->dph", weighted_values, value_matrix, precision=TOP_PRECISION
    )
    across_block_part = jnp.einsum(
        "ugm,ump->ugp",
        query_matrix * jnp.exp(decay_factors)[:, :, None],
        running_state,
        precision=TOP_PRECISION,
    )
    final_decay = decay_factors[:, -1:]
    carried = key_matrix * jnp.exp(final_decay - decay_factors)[:, :, None]
    running_state = running_state * jnp.exp(final_decay)[:, :, None] + jnp.einsum(
        "nje,njf->nef", carried, value_matrix, precision=TOP_PRECISION
    )
    return (running_state, within_block_part + across_block_part)


def gated_scan(query_matrix, key_matrix, value_matrix, log_forget, span):
    latents, length, head_count, head_dim = query_matrix.shape
    blocks = length // span

    def arrange(array):
        return (
            array.reshape(latents, blocks, span, head_count, head_dim)
            .transpose(1, 0, 3, 2, 4)
            .reshape(blocks, latents * head_count, span, head_dim)
        )

    log_blocks = (
        log_forget.reshape(latents, blocks, span, head_count)
        .transpose(1, 0, 3, 2)
        .reshape(blocks, latents * head_count, span)
    )
    initial = jnp.zeros((latents * head_count, head_dim, head_dim), query_matrix.dtype)
    _, results = lax.scan(
        jax.checkpoint(span_pass),
        initial,
        (arrange(query_matrix), arrange(key_matrix), arrange(value_matrix), log_blocks),
    )
    results = results.reshape(blocks, latents, head_count, span, head_dim).transpose(1, 0, 3, 2, 4)
    return results.reshape(latents, length, head_count * head_dim)


def depthwise(field, kernel, grid_side):
    latents = field.shape[0]
    channels = field.shape[2]
    image = field.reshape(latents, grid_side, grid_side, channels)
    padded = jnp.pad(image, ((0, 0), (1, 1), (1, 1), (0, 0)))
    summed = jnp.zeros_like(image)
    for row_off in range(3):
        for col_off in range(3):
            summed = (
                summed
                + padded[:, row_off : row_off + grid_side, col_off : col_off + grid_side, :]
                * kernel[row_off, col_off]
            )
    return summed.reshape(latents, grid_side * grid_side, channels)


def mixer_rows(query_matrix, key_matrix, value_matrix, log_forget, kernel, span, grid_side):
    recurrent = gated_scan(query_matrix, key_matrix, value_matrix, log_forget, span)
    return depthwise(recurrent, kernel, grid_side)


def tanh_gelu(inputs):
    return jax.nn.gelu(inputs, approximate=True)


def moments(rows, model_width):
    totals = lax.psum((jnp.sum(rows, axis=-1), jnp.sum(rows * rows, axis=-1)), "tensor")
    mean_row = totals[0][..., None] / model_width
    var_row = totals[1][..., None] / model_width - mean_row * mean_row
    return (mean_row, lax.rsqrt(var_row + norm_eps))


def share_rows(local_rows):
    return lax.all_gather(local_rows, "tensor", axis=2, tiled=True)


def branch_total(partial_rows):
    return lax.psum_scatter(partial_rows, "tensor", scatter_dimension=1, tiled=True)


def spread_grads(local_grads):
    return lax.all_gather(local_grads, "tensor", axis=2, tiled=True)


def input_total(partial_rows):
    return lax.psum_scatter(partial_rows, "tensor", scatter_dimension=1, tiled=True)


def norm_back(grad_normed, normalized, inv_std, scale_row, model_width):
    scaled = grad_normed * (1.0 + scale_row)
    totals = lax.psum((jnp.sum(scaled, axis=-1), jnp.sum(scaled * normalized, axis=-1)), "tensor")
    return inv_std * (
        scaled
        - totals[0][..., None] / model_width
        - normalized * totals[1][..., None] / model_width
    )


def shards(
    latent_tokens,
    timesteps,
    labels,
    class_table,
    ada_weight,
    ada_bias,
    query_key_value_weight,
    gate_weight,
    gate_bias,
    conv_weight,
    out_weight,
    up_weight,
    down_weight,
    cotangent,
):
    latents, length, part_width = latent_tokens.shape
    row_count = latents * length
    heads_here = gate_weight.shape[1]
    onehot = labels[:, None] == jnp.arange(NCLASS, dtype=jnp.int32)[None, :]
    cond = jnp.dot(
        onehot.astype(jnp.bfloat16), class_table, preferred_element_type=jnp.float32
    ) + embed_time(timesteps, MODEL_DIM)
    silu_value, silu_pull = jax.vjp(jax.nn.silu, cond)
    silu_cond = silu_value.astype(jnp.bfloat16)
    ada_flat = ada_weight.reshape(MODEL_DIM, 6 * part_width)
    mods = (
        jnp.dot(silu_cond, ada_flat, preferred_element_type=jnp.float32).reshape(
            latents, 6, part_width
        )
        + ada_bias.astype(jnp.float32)[None]
    )
    shift_one = mods[:, 0:1]
    scale_one = mods[:, 1:2]
    gate_one = mods[:, 2:3]
    shift_two = mods[:, 3:4]
    scale_two = mods[:, 4:5]
    gate_two = mods[:, 5:6]
    tokens_value = latent_tokens.astype(jnp.float32)
    mean_one, std_inv_one = moments(tokens_value, MODEL_DIM)
    unit_one = (tokens_value - mean_one) * std_inv_one
    first_normalized = share_rows((unit_one * (1.0 + scale_one) + shift_one).astype(jnp.bfloat16))
    rows_one = first_normalized.reshape(row_count, MODEL_DIM)
    qkv_flat = query_key_value_weight.reshape(MODEL_DIM, 3 * part_width)
    projected_rows = jnp.dot(rows_one, qkv_flat, preferred_element_type=jnp.float32).astype(
        jnp.bfloat16
    )
    forget_logit = jnp.dot(
        rows_one, gate_weight, preferred_element_type=jnp.float32
    ) + gate_bias.astype(jnp.float32)

    def head_view(columns):
        return columns.astype(jnp.float32).reshape(latents, length, heads_here, HD)

    query_matrix = head_view(projected_rows[:, :part_width]) * HD ** (-0.5)
    key_matrix = head_view(projected_rows[:, part_width : 2 * part_width])
    value_matrix = head_view(projected_rows[:, 2 * part_width :])
    log_forget = jax.nn.log_sigmoid(forget_logit).reshape(latents, length, heads_here)
    mixed_out, mixer_pull = jax.vjp(
        partial(mixer_rows, span=CH, grid_side=GRID),
        query_matrix,
        key_matrix,
        value_matrix,
        log_forget,
        conv_weight.astype(jnp.float32),
    )
    mixer_low = mixed_out.reshape(row_count, part_width).astype(jnp.bfloat16)
    attn_out = branch_total(
        jnp.dot(mixer_low, out_weight, preferred_element_type=jnp.float32)
    ).reshape(latents, length, part_width)
    after_attn = tokens_value + gate_one * attn_out
    mean_two, std_inv_two = moments(after_attn, MODEL_DIM)
    unit_two = (after_attn - mean_two) * std_inv_two
    normed_two = share_rows((unit_two * (1.0 + scale_two) + shift_two).astype(jnp.bfloat16))
    rows_two = normed_two.reshape(row_count, MODEL_DIM)
    up_rows = jnp.dot(rows_two, up_weight, preferred_element_type=jnp.float32)
    act_rows, gelu_pull = jax.vjp(tanh_gelu, up_rows)
    act_low = act_rows.astype(jnp.bfloat16)
    mlp_out = branch_total(
        jnp.dot(act_low, down_weight, preferred_element_type=jnp.float32)
    ).reshape(latents, length, part_width)
    layer_out = (after_attn + gate_two * mlp_out).astype(jnp.bfloat16)
    grad_result = cotangent.astype(jnp.float32)
    grad_gate_two = jnp.sum(grad_result * mlp_out, axis=1)
    grad_mlp = spread_grads((grad_result * gate_two).astype(jnp.bfloat16)).reshape(
        row_count, MODEL_DIM
    )
    grad_down = jnp.einsum("rf,rd->fd", act_low, grad_mlp, preferred_element_type=jnp.float32)
    grad_act = jnp.einsum("rd,fd->rf", grad_mlp, down_weight, preferred_element_type=jnp.float32)
    grad_up_rows = gelu_pull(grad_act)[0].astype(jnp.bfloat16)
    grad_up = jnp.einsum("rd,rf->df", rows_two, grad_up_rows, preferred_element_type=jnp.float32)
    grad_normed_two = input_total(
        jnp.einsum("rf,df->rd", grad_up_rows, up_weight, preferred_element_type=jnp.float32)
    ).reshape(latents, length, part_width)
    grad_shift_two = jnp.sum(grad_normed_two, axis=1)
    grad_scale_two = jnp.sum(grad_normed_two * unit_two, axis=1)
    grad_after = grad_result + norm_back(
        grad_normed_two, unit_two, std_inv_two, scale_two, MODEL_DIM
    )
    grad_gate_one = jnp.sum(grad_after * attn_out, axis=1)
    grad_attn = spread_grads((grad_after * gate_one).astype(jnp.bfloat16)).reshape(
        row_count, MODEL_DIM
    )
    grad_out_w = jnp.einsum("rp,rd->pd", mixer_low, grad_attn, preferred_element_type=jnp.float32)
    grad_mixed = jnp.einsum(
        "rd,pd->rp", grad_attn, out_weight, preferred_element_type=jnp.float32
    ).reshape(latents, length, part_width)
    grad_query, grad_key, grad_value, grad_log, grad_conv = mixer_pull(grad_mixed)
    grad_projected = (
        jnp.concatenate([grad_query * HD ** (-0.5), grad_key, grad_value], axis=2)
        .reshape(row_count, 3 * part_width)
        .astype(jnp.bfloat16)
    )
    grad_forget = (grad_log.reshape(row_count, heads_here) * jax.nn.sigmoid(-forget_logit)).astype(
        jnp.bfloat16
    )
    grad_qkv = jnp.einsum(
        "rd,rc->dc", rows_one, grad_projected, preferred_element_type=jnp.float32
    ).reshape(MODEL_DIM, 3, part_width)
    grad_gate_w = jnp.einsum("rd,rh->dh", rows_one, grad_forget, preferred_element_type=jnp.float32)
    grad_gate_b = jnp.sum(grad_forget.astype(jnp.float32), axis=0)
    grad_normed_one = input_total(
        jnp.einsum("rc,dc->rd", grad_projected, qkv_flat, preferred_element_type=jnp.float32)
        + jnp.einsum("rh,dh->rd", grad_forget, gate_weight, preferred_element_type=jnp.float32)
    ).reshape(latents, length, part_width)
    grad_shift_one = jnp.sum(grad_normed_one, axis=1)
    grad_scale_one = jnp.sum(grad_normed_one * unit_one, axis=1)
    grad_tokens = grad_after + norm_back(
        grad_normed_one, unit_one, std_inv_one, scale_one, MODEL_DIM
    )
    grad_mods = jnp.stack(
        [
            grad_shift_one,
            grad_scale_one,
            grad_gate_one,
            grad_shift_two,
            grad_scale_two,
            grad_gate_two,
        ],
        axis=1,
    ).astype(jnp.bfloat16)
    mods_flat = grad_mods.reshape(latents, 6 * part_width)
    grad_ada_b = jnp.sum(grad_mods.astype(jnp.float32), axis=0)
    grad_silu = lax.psum(
        jnp.einsum("bc,dc->bd", mods_flat, ada_flat, preferred_element_type=jnp.float32), "tensor"
    )
    grad_cond = silu_pull(grad_silu)[0]
    grad_ada_w = jnp.einsum(
        "bd,bc->dc", silu_cond, mods_flat, preferred_element_type=jnp.float32
    ).reshape(MODEL_DIM, 6, part_width)
    grad_class = jnp.dot(onehot.astype(jnp.float32).T, grad_cond, precision=TOP_PRECISION)
    grad_class, grad_ada_w = (
        lax.psum_scatter(grad_class, "dp", scatter_dimension=1, tiled=True),
        lax.psum_scatter(grad_ada_w, "dp", scatter_dimension=0, tiled=True),
    )
    grad_qkv, grad_gate_w, grad_out_w, grad_up, grad_down = (
        lax.psum_scatter(grad_qkv, "dp", scatter_dimension=0, tiled=True),
        lax.psum_scatter(grad_gate_w, "dp", scatter_dimension=0, tiled=True),
        lax.psum_scatter(grad_out_w, "dp", scatter_dimension=1, tiled=True),
        lax.psum_scatter(grad_up, "dp", scatter_dimension=0, tiled=True),
        lax.psum_scatter(grad_down, "dp", scatter_dimension=1, tiled=True),
    )
    grad_ada_b, grad_gate_b, grad_conv = lax.psum((grad_ada_b, grad_gate_b, grad_conv), "dp")
    return (
        layer_out,
        grad_tokens,
        grad_class,
        grad_ada_w,
        grad_ada_b,
        grad_qkv,
        grad_gate_w,
        grad_gate_b,
        grad_conv,
        grad_out_w,
        grad_up,
        grad_down,
    )


def solution(mesh):
    in_specs = (
        P("dp", None, "tensor"),
        P("dp"),
        P("dp"),
        P(),
        P(None, None, "tensor"),
        P(None, "tensor"),
        P(None, None, "tensor"),
        P(None, "tensor"),
        P("tensor"),
        P(None, None, "tensor"),
        P("tensor", None),
        P(None, "tensor"),
        P("tensor", None),
        P("dp", None, "tensor"),
    )
    out_specs = (
        P("dp", None, "tensor"),
        P("dp", None, "tensor"),
        P(None, "dp"),
        P("dp", None, "tensor"),
        P(None, "tensor"),
        P("dp", None, "tensor"),
        P("dp", "tensor"),
        P("tensor"),
        P(None, None, "tensor"),
        P("tensor", "dp"),
        P("dp", "tensor"),
        P("tensor", "dp"),
    )
    return jax.shard_map(shards, mesh=mesh, in_specs=in_specs, out_specs=out_specs, check_vma=False)
```

profile of v0, /device:TPU:0, one launch (start us, length us, event | category | flops | bytes accessed | tf_op | source)
XLA Modules:
  0.0 1475.0 jit_solution(13348404259358902451)
XLA Ops:
  15.3 8.5 all-reduce.24
  25.8 23.7 %all-gather.5.cloned.1.call-done = bf16[1,1024,1152]{1,2,0:T(8,128)(2,1)} async-done(((bf16[1,1024,288]{1,2,0:T(8,128)(2,1)}), bf16[1,1024,1152]{1,2,0:T(8,128)(2,1)}) %all-gather.5.cloned.1.call-update) | async-done | bytes 2359312 | tf_op jit(solution)/shard_map/all_gather | solution.py:111
  78.2 114.2 %while.42 = (s32[]{:T(128)}, f32[4,72,72]{2,1,0:T(8,128)S(1)}, f32[16,4,64,72]{3,2,1,0:T(8,128)}, f32[16,4,72,72]{3,2,1,0:T(8,128)}, f32[16,4,64]{2,1,0:T(4,128)...) while((s32[]{:T(128)}, f32[4,72,72]{2,1,0:T(8,128)S(1)}, ...), condition=%wide.region_6.7_spmd.clone.clone, body=%wide.region_4.6_spmd.clone.clone.sunk | while | flops 60402944 | bytes 1701095 | solution.py:69
  202.0 8.5 add_convert_fusion
  215.0 47.9 %reduce-scatter.14.cloned.1.call-done = f32[1024,288]{0,1:T(8,128)} async-done(((f32[1024,1152]{0,1:T(8,128)}), f32[1024,288]{0,1:T(8,128)}) %reduce-scatter.14.cloned.1.call-update) | async-done | bytes 1179664 | tf_op jit(solution)/shard_map/reduce_scatter | solution.py:115
  265.5 5.8 all-reduce.23
  276.1 23.0 %all-gather.7.cloned.1.call-done = bf16[1,1024,1152]{1,2,0:T(8,128)(2,1)} async-done(((bf16[1,1024,288]{1,2,0:T(8,128)(2,1)}), bf16[1,1024,1152]{1,2,0:T(8,128)(2,1)}) %all-gather.7.cloned.1.call-update) | async-done | bytes 2359312 | tf_op jit(solution)/shard_map/all_gather | solution.py:111
  299.1 7.3 fusion.83
  306.5 18.8 %all-gather.9.cloned.1.call-done = bf16[1,1024,1152]{1,2,0:T(8,128)(2,1)} async-done(((bf16[1,1024,288]{1,2,0:T(8,128)(2,1)}), bf16[1,1024,1152]{1,2,0:T(8,128)(2,1)}) %all-gather.9.cloned.1.call-update) | async-done | bytes 2359312 | tf_op jit(solution)/shard_map/all_gather | solution.py:119
  325.3 9.2 fusion.66
  336.0 4.9 fusion.136
  342.6 8.4 fusion.126
  351.1 37.8 %reduce-scatter.18.cloned.1.call-done = f32[1024,288]{0,1:T(8,128)} async-done(((f32[1024,1152]{0,1:T(8,128)}), f32[1024,288]{0,1:T(8,128)}) %reduce-scatter.18.cloned.1.call-update) | async-done | bytes 1179664 | tf_op jit(solution)/shard_map/reduce_scatter | solution.py:123
  392.0 5.9 all-reduce.22
  397.9 41.3 %reduce-scatter.16.cloned.1.call-done = f32[1024,288]{0,1:T(8,128)} async-done(((f32[1024,1152]{0,1:T(8,128)}), f32[1024,288]{0,1:T(8,128)}) %reduce-scatter.16.cloned.1.call-update) | async-done | bytes 1179664 | tf_op jit(solution)/shard_map/reduce_scatter | solution.py:115
  445.4 22.8 %all-gather.11.cloned.1.call-done = bf16[1,1024,1152]{1,2,0:T(8,128)(2,1)} async-done(((bf16[1,1024,288]{1,2,0:T(8,128)(2,1)}), bf16[1,1024,1152]{1,2,0:T(8,128)(2,1)}) %all-gather.11.cloned.1.call-update) | async-done | bytes 2359312 | tf_op jit(solution)/shard_map/all_gather | solution.py:119
  484.0 168.7 %while.41 = (s32[]{:T(128)}, f32[4,72,72]{2,1,0:T(8,128)S(1)}, f32[16,4,64,72]{3,2,1,0:T(8,128)}, bf16[16,4,64,72]{3,2,1,0:T(8,128)(2,1)S(1)}, bf16[16,4,64,72]{...) while((s32[]{:T(128)}, f32[4,72,72]{2,1,0:T(8,128)S(1)}, ...), condition=%wide.region_27.28_spmd.clone, body=%wide.region_18.27_spmd.clone.sunk | while | flops 135152128 | bytes 4529631 | solution.py:69
  679.5 9.6 fusion.75
  689.1 8.0 fusion.81
  701.8 6.7 fusion.69
  708.7 15.5 %reduce-scatter.20.cloned.1.call-done = f32[1024,288]{0,1:T(8,128)} async-done(((f32[1024,1152]{0,1:T(8,128)}), f32[1024,288]{0,1:T(8,128)}) %reduce-scatter.20.cloned.1.call-update) | async-done | bytes 1179664 | tf_op jit(solution)/shard_map/reduce_scatter | solution.py:123
  729.1 10.5 all-reduce.21
  742.5 5.0 broadcast_multiply_fusion
  750.8 8.1 multiply_reduce_fusion.12
  761.5 28.1 %reduce-scatter.34.cloned.1.call-done = f32[144,4]{1,0:T(8,128)} async-done(((f32[1152,4]{1,0:T(8,128)}), f32[144,4]{1,0:T(8,128)}) %reduce-scatter.34.cloned.1.call-update) | async-done | bytes 2320
  791.2 70.6 %all-reduce.20 = (f32[6,288]{1,0:T(8,128)}, f32[4]{0:T(128)}, f32[3,3,288]{2,1,0:T(4,128)}) all-reduce(bf16[6,288]{1,0:T(8,128)(2,1)S(1)} %stack.48, f32[4]{0:T(128)S(1)} %get-tuple-element.618, f32[3,3,288]{2,1,0:T(4,128)S(1)} %pad_add_fusion.7), channel_id=1, replica_groups=mesh['dp'=8,'tensor'=4] {'dp'}, use_global_device_ids=true, to_apply=%region_42.43 | all-reduce | flops 4324 | bytes 31136 | tf_op jit(solution)/shard_map/psum | solution.py:298
  865.1 33.3 %reduce-scatter.32.cloned.1.call-done = f32[1152,144]{0,1:T(8,128)} async-done(((f32[1152,1152]{0,1:T(8,128)}), f32[1152,144]{0,1:T(8,128)}) %reduce-scatter.32.cloned.1.call-update) | async-done | bytes 663568 | tf_op jit(solution)/shard_map/reduce_scatter | solution.py:296
  898.4 108.1 %reduce-scatter.30.cloned.1.call-done = f32[144,1152]{1,0:T(8,128)} async-done(((f32[1152,1152]{1,0:T(8,128)}), f32[144,1152]{1,0:T(8,128)}) %reduce-scatter.30.cloned.1.call-update) | async-done | bytes 663568 | tf_op jit(solution)/shard_map/reduce_scatter | solution.py:295
  1006.5 70.1 %reduce-scatter.28.cloned.1.call-done = f32[288,144]{0,1:T(8,128)} async-done(((f32[288,1152]{0,1:T(8,128)}), f32[288,144]{0,1:T(8,128)}) %reduce-scatter.28.cloned.1.call-update) | async-done | bytes 165904 | tf_op jit(solution)/shard_map/reduce_scatter | solution.py:294
  1076.6 107.3 %reduce-scatter.26.cloned.1.call-done = f32[144,3,288]{2,0,1:T(8,128)} async-done(((f32[1152,3,288]{2,0,1:T(8,128)}), f32[144,3,288]{2,0,1:T(8,128)}) %reduce-scatter.26.cloned.1.call-update) | async-done | bytes 497680 | tf_op jit(solution)/shard_map/reduce_scatter | solution.py:292
  1183.9 99.7 %reduce-scatter.22.cloned.1.call-done = f32[1000,144]{0,1:T(8,128)} async-done(((f32[1000,1152]{0,1:T(8,128)}), f32[1000,144]{0,1:T(8,128)}) %reduce-scatter.22.cloned.1.call-update) | async-done | bytes 576016 | tf_op jit(solution)/shard_map/reduce_scatter | solution.py:288
  1283.6 184.6 %reduce-scatter.24.cloned.1.call-done = f32[144,6,288]{2,0,1:T(8,128)} async-done(((f32[1152,6,288]{2,0,1:T(8,128)}), f32[144,6,288]{2,0,1:T(8,128)}) %reduce-scatter.24.cloned.1.call-update) | async-done | bytes 995344 | tf_op jit(solution)/shard_map/reduce_scatter | solution.py:289
  (769 shorter events, 417.5 us)
Async XLA Ops:
  7.2 291.9 %copy-start = (bf16[1152,1152]{1,0:T(8,128)(2,1)S(1)}, bf16[1152,1152]{1,0:T(8,128)(2,1)}, u32[]{:S(2)}) copy-start(bf16[1152,1152]{1,0:T(8,128)(2,1)} %param.29) | copy-start | bytes 7962628
  7.2 42.3 %all-gather.5.cloned.1.call-start = ((), (), s32[]{:S(2)}) async-start(), calls=%async_computation.11 | async-start | bytes 2949120 | tf_op jit(solution)/shard_map/all_gather | solution.py:111
  11.0 3.5 copy-start.28
  11.0 4.2 copy-start.4
  14.5 10.6 copy-start.31
  14.5 10.6 copy-start.26
  25.0 237.9 %reduce-scatter.14.cloned.1.call-start = ((), (), s32[]{:S(2)}) async-start(), calls=%async_computation.12 | async-start | bytes 5898240 | tf_op jit(solution)/shard_map/reduce_scatter | solution.py:115
  198.6 3.3 copy-start.20
  198.6 3.3 copy-start.21
  198.6 3.3 copy-start.22
  198.7 3.3 copy-start.23
  198.7 3.3 copy-start.24
  201.9 9.4 copy-start.15
  214.9 48.0 %copy-start.25 = (f32[288]{0:T(512)S(1)}, f32[288]{0:T(512)}, u32[]{:S(2)}) copy-start(f32[288]{0:T(512)} %get-tuple-element.561) | copy-start | bytes 3460
  214.9 56.5 %copy-start.27 = (f32[288]{0:T(512)S(1)}, f32[288]{0:T(512)}, u32[]{:S(2)}) copy-start(f32[288]{0:T(512)} %get-tuple-element.557) | copy-start | bytes 3460
  214.9 84.2 %all-gather.7.cloned.1.call-start = ((), (), s32[]{:S(2)}) async-start(), calls=%async_computation.13 | async-start | bytes 2949120 | tf_op jit(solution)/shard_map/all_gather | solution.py:111
  273.8 51.5 %all-gather.9.cloned.1.call-start = ((), (), s32[]{:S(2)}) async-start(), calls=%async_computation.15 | async-start | bytes 2949120 | tf_op jit(solution)/shard_map/all_gather | solution.py:119
  275.9 113.0 %reduce-scatter.18.cloned.1.call-start = ((), (), s32[]{:S(2)}) async-start(), calls=%async_computation.16 | async-start | bytes 5898240 | tf_op jit(solution)/shard_map/reduce_scatter | solution.py:123
  340.9 98.3 %reduce-scatter.16.cloned.1.call-start = ((), (), s32[]{:S(2)}) async-start(), calls=%async_computation.14 | async-start | bytes 5898240 | tf_op jit(solution)/shard_map/reduce_scatter | solution.py:115
  351.1 39.3 %copy-start.3 = (f32[1,1024,288]{1,2,0:T(8,128)S(1)}, f32[1,1024,288]{1,2,0:T(8,128)}, u32[]{:S(2)}) copy-start(f32[1,1024,288]{1,2,0:T(8,128)} %get-tuple-element.625) | copy-start | bytes 3538948
  351.1 117.2 %all-gather.11.cloned.1.call-start = ((), (), s32[]{:S(2)}) async-start(), calls=%async_computation.17 | async-start | bytes 2949120 | tf_op jit(solution)/shard_map/all_gather | solution.py:119
  444.1 280.1 %reduce-scatter.20.cloned.1.call-start = ((), (), s32[]{:S(2)}) async-start(), calls=%async_computation.18 | async-start | bytes 5898240 | tf_op jit(solution)/shard_map/reduce_scatter | solution.py:123
  444.4 23.9 %copy-start.10 = (bf16[16,4,64,72]{3,2,1,0:T(8,128)(2,1)}, bf16[16,4,64,72]{3,2,1,0:T(8,128)(2,1)S(1)}, u32[]{:S(2)}) copy-start(bf16[16,4,64,72]{3,2,1,0:T(8,128)(2,1)S(1)} %fusion.133) | copy-start | bytes 1769476
  676.2 113.5 %reduce-scatter.34.cloned.1.call-start = ((), (), s32[]{:S(2)}) async-start(), calls=%async_computation.25 | async-start | bytes 663552
  679.4 218.9 %reduce-scatter.32.cloned.1.call-start = ((), (), s32[]{:S(2)}) async-start(), calls=%async_computation.24 | async-start | bytes 5971968 | tf_op jit(solution)/shard_map/reduce_scatter | solution.py:296
  689.1 317.4 %reduce-scatter.30.cloned.1.call-start = ((), (), s32[]{:S(2)}) async-start(), calls=%async_computation.23 | async-start | bytes 5971968 | tf_op jit(solution)/shard_map/reduce_scatter | solution.py:295
  697.1 379.5 %reduce-scatter.28.cloned.1.call-start = ((), (), s32[]{:S(2)}) async-start(), calls=%async_computation.22 | async-start | bytes 1990656 | tf_op jit(solution)/shard_map/reduce_scatter | solution.py:294
  701.7 482.2 %reduce-scatter.26.cloned.1.call-start = ((), (), s32[]{:S(2)}) async-start(), calls=%async_computation.21 | async-start | bytes 5971968 | tf_op jit(solution)/shard_map/reduce_scatter | solution.py:292
  708.5 575.1 %reduce-scatter.22.cloned.1.call-start = ((), (), s32[]{:S(2)}) async-start(), calls=%async_computation.19 | async-start | bytes 5308416 | tf_op jit(solution)/shard_map/reduce_scatter | solution.py:288
  742.3 725.8 %reduce-scatter.24.cloned.1.call-start = ((), (), s32[]{:S(2)}) async-start(), calls=%async_computation.20 | async-start | bytes 11943936 | tf_op jit(solution)/shard_map/reduce_scatter | solution.py:289
  750.8 8.2 copy-start.2
  861.8 606.3 %copy-start.1 = (bf16[1152,1152]{1,0:T(8,128)(2,1)S(1)}, bf16[1152,1152]{1,0:T(8,128)(2,1)}, u32[]{:S(2)}) copy-start(bf16[1152,1152]{1,0:T(8,128)(2,1)} %param.29) | copy-start | bytes 7962628
  (16 other events, 33.3 us)
Sparse Core Ops, SparseCore 0:
  25.1 24.3 all-gather.4
  215.0 47.8 reduce-scatter.13
  273.9 25.2 all-gather.6
  301.2 24.0 all-gather.8
  341.0 47.8 reduce-scatter.17
  391.3 47.8 reduce-scatter.15
  444.2 24.0 all-gather.10
  676.3 47.8 reduce-scatter.19
  727.5 62.1 reduce-scatter.33
  794.1 104.2 reduce-scatter.31
  902.5 103.9 reduce-scatter.29
  1010.8 65.7 reduce-scatter.27
  1080.8 103.0 reduce-scatter.25
  1188.4 95.1 reduce-scatter.21
  1288.0 180.0 reduce-scatter.23
where the time goes:
time: 1480 us; the launch traced here: 1470 us
  waiting for transfers between devices  862 us (58%)
  matrix products  265 us (18%)
  local copies, waits for them, and re-layouts  132 us (9%)
  blocking collectives  101 us (7%)
  other arithmetic  94.3 us (6%)
  between operations  16.4 us (1%)
    reduce_scatter x1, waiting for transfers between devices, shards(): lax.psum_scatter(grad_ada_w, 'dp', scatter_dimension=0, tiled=True)  185 us
    reduce_scatter x1, waiting for transfers between devices, shards(): lax.psum_scatter(grad_up, 'dp', scatter_dimension=0, tiled=True)  108 us
    reduce_scatter x1, waiting for transfers between devices, shards(): lax.psum_scatter(grad_qkv, 'dp', scatter_dimension=0, tiled=True)  107 us
    reduce_scatter x1, waiting for transfers between devices, shards(): lax.psum_scatter(grad_class, 'dp', scatter_dimension=1, tiled=True)  99.7 us
    reduce_scatter x2, waiting for transfers between devices, branch_total(): lax.psum_scatter(partial_rows, 'tensor', scatter_dimension=1, tiled=True)  89.2 us
    psum x1, blocking collectives, shards(): lax.psum((grad_ada_b, grad_gate_b, grad_conv), 'dp')  70.6 us
    reduce_scatter x1, waiting for transfers between devices, shards(): lax.psum_scatter(grad_out_w, 'dp', scatter_dimension=1, tiled=True)  70.1 us
    reduce_scatter x2, waiting for transfers between devices, input_total(): lax.psum_scatter(partial_rows, 'tensor', scatter_dimension=1, tiled=True)  53.3 us
  transfers between devices with their start and end apart: 15, of which 15 were waited for; matrix products, arithmetic and copies ran while one was open for 6% of the time, Pallas kernels for 0%

commit v1 on v0

--- a/solution.py
+++ b/solution.py
@@ -275,27 +275,69 @@
         axis=1,
     ).astype(jnp.bfloat16)
     mods_flat = grad_mods.reshape(latents, 6 * part_width)
-    grad_ada_b = jnp.sum(grad_mods.astype(jnp.float32), axis=0)
-    grad_silu = lax.psum(
-        jnp.einsum("bc,dc->bd", mods_flat, ada_flat, preferred_element_type=jnp.float32), "tensor"
-    )
-    grad_cond = silu_pull(grad_silu)[0]
+    grad_silu = jnp.einsum("bc,dc->bd", mods_flat, ada_flat, preferred_element_type=jnp.float32)
+    shard_count = lax.psum(1, "dp")
+    shard_at = lax.axis_index("dp")
+    own_width = MODEL_DIM // shard_count
+    small = jnp.concatenate(
+        [
+            mods_flat.astype(jnp.float32).reshape(latents * 6 * part_width),
+            lax.psum(grad_silu, "tensor").reshape(latents * MODEL_DIM),
+            cond.reshape(latents * MODEL_DIM),
+            grad_gate_w.reshape(MODEL_DIM * heads_here),
+            grad_gate_b,
+            grad_conv.reshape(9 * part_width),
+        ]
+    )
+    every = lax.all_gather(small, "dp", axis=0, tiled=False)
+    every_labels = lax.all_gather(labels, "dp", axis=0, tiled=True)
+    all_latents = every_labels.shape[0]
+    sizes = [
+        latents * 6 * part_width,
+        latents * MODEL_DIM,
+        latents * MODEL_DIM,
+        MODEL_DIM * heads_here,
+        heads_here,
+        9 * part_width,
+    ]
+    starts = [sum(sizes[:index]) for index in range(len(sizes) + 1)]
+    every_mods, every_silu, every_cond, every_gate_w, every_gate_b, every_conv = (
+        every[:, low:high] for low, high in zip(starts[:-1], starts[1:])
+    )
+    every_mods = every_mods.reshape(all_latents, 6 * part_width)
+    grad_ada_b = jnp.sum(every_mods, axis=0).reshape(6, part_width)
+    grad_gate_b = jnp.sum(every_gate_b, axis=0)
+    grad_conv = jnp.sum(every_conv, axis=0).reshape(3, 3, part_width)
+
+    def own_columns(rows):
+        rows = rows.reshape(all_latents, MODEL_DIM)
+        return lax.dynamic_slice_in_dim(rows, shard_at * own_width, own_width, axis=1)
+
+    own_silu, own_pull = jax.vjp(jax.nn.silu, own_columns(every_cond))
+    own_cond = own_pull(own_columns(every_silu))[0]
     grad_ada_w = jnp.einsum(
-        "bd,bc->dc", silu_cond, mods_flat, preferred_element_type=jnp.float32
-    ).reshape(MODEL_DIM, 6, part_width)
-    grad_class = jnp.dot(onehot.astype(jnp.float32).T, grad_cond, precision=TOP_PRECISION)
-    grad_class, grad_ada_w = (
-        lax.psum_scatter(grad_class, "dp", scatter_dimension=1, tiled=True),
-        lax.psum_scatter(grad_ada_w, "dp", scatter_dimension=0, tiled=True),
-    )
-    grad_qkv, grad_gate_w, grad_out_w, grad_up, grad_down = (
-        lax.psum_scatter(grad_qkv, "dp", scatter_dimension=0, tiled=True),
-        lax.psum_scatter(grad_gate_w, "dp", scatter_dimension=0, tiled=True),
-        lax.psum_scatter(grad_out_w, "dp", scatter_dimension=1, tiled=True),
-        lax.psum_scatter(grad_up, "dp", scatter_dimension=0, tiled=True),
-        lax.psum_scatter(grad_down, "dp", scatter_dimension=1, tiled=True),
-    )
-    grad_ada_b, grad_gate_b, grad_conv = lax.psum((grad_ada_b, grad_gate_b, grad_conv), "dp")
+        "bd,bc->dc",
+        own_silu.astype(jnp.bfloat16),
+        every_mods.astype(jnp.bfloat16),
+        preferred_element_type=jnp.float32,
+    ).reshape(own_width, 6, part_width)
+    every_onehot = every_labels[:, None] == jnp.arange(NCLASS, dtype=jnp.int32)[None, :]
+    grad_class = jnp.dot(every_onehot.astype(jnp.float32).T, own_cond, precision=TOP_PRECISION)
+    own_gate_w = lax.dynamic_slice_in_dim(
+        every_gate_w.reshape(shard_count, MODEL_DIM, heads_here), shard_at * own_width, own_width, axis=1
+    )
+    grad_gate_w = jnp.sum(own_gate_w, axis=0)
+
+    def dp_total(partial, axis):
+        low = partial.astype(jnp.bfloat16)
+        return lax.psum_scatter(low, "dp", scatter_dimension=axis, tiled=True).astype(jnp.float32)
+
+    grad_qkv, grad_out_w, grad_up, grad_down = (
+        dp_total(grad_qkv, 0),
+        dp_total(grad_out_w, 1),
+        dp_total(grad_up, 0),
+        dp_total(grad_down, 1),
+    )
     return (
         layer_out,
         grad_tokens,

time: 1480 us -> 962 us (0.65)
  waiting for transfers between devices: 862 us -> 391 us
  blocking collectives: 101 us -> 41.8 us
  local copies, waits for them, and re-layouts: 132 us -> 147 us
    reduce_scatter x6 -> x4, waiting for transfers between devices: 603 us -> 72.6 us  [dp_total(): lax.psum_scatter(low, 'dp', scatter_dimension=axis, tiled=True)]
    psum x1 -> x0, blocking collectives: 70.6 us -> none  [shards(): lax.psum((grad_ada_b, grad_gate_b, grad_conv), 'dp')]
    unnamed x16 -> x14, waiting for transfers between devices: 28.3 us -> 70.9 us
    reduce_scatter x2, waiting for transfers between devices: 53.3 us -> 85.3 us  [input_total(): lax.psum_scatter(partial_rows, 'tensor', scatter_dimension=1, tiled=True)]
    all_gather x2, waiting for transfers between devices: 41.7 us -> 26.3 us  [spread_grads(): return lax.all_gather(local_grads, 'tensor', axis=2, tiled=True)]
  transfers between devices with their start and end apart: 15 -> 13, of which waited for: 15 -> 11; matrix products, arithmetic and copies ran while one was open for 6% -> 29% of each run, Pallas kernels for 0% -> 0%
where the time goes in v1:
time: 962 us; the launch traced here: 955 us
  waiting for transfers between devices  391 us (41%)
  matrix products  262 us (27%)
  local copies, waits for them, and re-layouts  147 us (15%)
  other arithmetic  92.3 us (10%)
  blocking collectives  41.8 us (4%)
  between operations  16.9 us (2%)
    reduce_scatter x2, waiting for transfers between devices, branch_total(): lax.psum_scatter(partial_rows, 'tensor', scatter_dimension=1, tiled=True)  89.2 us
    reduce_scatter x2, waiting for transfers between devices, input_total(): lax.psum_scatter(partial_rows, 'tensor', scatter_dimension=1, tiled=True)  85.3 us
    reduce_scatter x4, waiting for transfers between devices, dp_total(): lax.psum_scatter(low, 'dp', scatter_dimension=axis, tiled=True)  72.6 us
    unnamed x14, waiting for transfers between devices  70.9 us
    dot_general x64, matrix products, span_pass(): jnp.einsum('mkd,mld->mkl', query_matrix, key_matrix, precision=TOP_PRECIS...  50.4 us
    all_gather x2, waiting for transfers between devices, share_rows(): return lax.all_gather(local_rows, 'tensor', axis=2, tiled=True)  46.4 us
    squeeze x80, local copies, waits for them, and re-layouts, gated_scan(): lax.scan(jax.checkpoint(span_pass), initial, (arrange(query_matrix), arra...  46 us
    dot_general x48, matrix products, span_pass(): jnp.einsum('ugm,ump->ugp', query_matrix * jnp.exp(decay_factors)[:, :, No...  46 us
  transfers between devices with their start and end apart: 13, of which 11 were waited for; matrix products, arithmetic and copies ran while one was open for 29% of the time, Pallas kernels for 0%

profile of v1, /device:TPU:0, one launch (start us, length us, event | category | flops | bytes accessed | tf_op | source)
XLA Modules:
  0.0 954.8 jit_solution(11928807414023486540)
XLA Ops:
  15.3 8.5 all-reduce.25
  25.7 23.8 %all-gather.6.cloned.1.call-done = bf16[1,1024,1152]{1,2,0:T(8,128)(2,1)} async-done(((bf16[1,1024,288]{1,2,0:T(8,128)(2,1)}), bf16[1,1024,1152]{1,2,0:T(8,128)(2,1)}) %all-gather.6.cloned.1.call-update) | async-done | bytes 2359312 | tf_op jit(solution)/shard_map/all_gather | solution.py:111
  49.5 4.7 fusion.87
  78.2 114.2 %while.42 = (s32[]{:T(128)}, f32[4,72,72]{2,1,0:T(8,128)S(1)}, f32[16,4,64,72]{3,2,1,0:T(8,128)}, f32[16,4,72,72]{3,2,1,0:T(8,128)}, f32[16,4,64]{2,1,0:T(4,128)...) while((s32[]{:T(128)}, f32[4,72,72]{2,1,0:T(8,128)S(1)}, ...), condition=%wide.region_6.7_spmd.clone.clone, body=%wide.region_4.6_spmd.clone.clone.sunk | while | flops 60402944 | bytes 1701095 | solution.py:69
  202.1 8.2 add_convert_fusion
  211.1 3.6 fusion.147
  214.8 47.9 %reduce-scatter.9.cloned.1.call-done = f32[1024,288]{0,1:T(8,128)} async-done(((f32[1024,1152]{0,1:T(8,128)}), f32[1024,288]{0,1:T(8,128)}) %reduce-scatter.9.cloned.1.call-update) | async-done | bytes 1179664 | tf_op jit(solution)/shard_map/reduce_scatter | solution.py:115
  265.3 5.8 all-reduce.24
  276.2 22.7 %all-gather.8.cloned.1.call-done = bf16[1,1024,1152]{1,2,0:T(8,128)(2,1)} async-done(((bf16[1,1024,288]{1,2,0:T(8,128)(2,1)}), bf16[1,1024,1152]{1,2,0:T(8,128)(2,1)}) %all-gather.8.cloned.1.call-update) | async-done | bytes 2359312 | tf_op jit(solution)/shard_map/all_gather | solution.py:111
  298.9 7.3 fusion.79
  306.3 18.8 %all-gather.10.cloned.1.call-done = bf16[1,1024,1152]{1,2,0:T(8,128)(2,1)} async-done(((bf16[1,1024,288]{1,2,0:T(8,128)(2,1)}), bf16[1,1024,1152]{1,2,0:T(8,128)(2,1)}) %all-gather.10.cloned.1.call-update) | async-done | bytes 2359312 | tf_op jit(solution)/shard_map/all_gather | solution.py:119
  325.1 9.2 fusion.66
  335.7 4.9 fusion.148
  342.3 8.4 fusion.138
  350.9 37.8 %reduce-scatter.13.cloned.1.call-done = f32[1024,288]{0,1:T(8,128)} async-done(((f32[1024,1152]{0,1:T(8,128)}), f32[1024,288]{0,1:T(8,128)}) %reduce-scatter.13.cloned.1.call-update) | async-done | bytes 1179664 | tf_op jit(solution)/shard_map/reduce_scatter | solution.py:123
  391.7 5.9 all-reduce.23
  397.6 41.3 %reduce-scatter.11.cloned.1.call-done = f32[1024,288]{0,1:T(8,128)} async-done(((f32[1024,1152]{0,1:T(8,128)}), f32[1024,288]{0,1:T(8,128)}) %reduce-scatter.11.cloned.1.call-update) | async-done | bytes 1179664 | tf_op jit(solution)/shard_map/reduce_scatter | solution.py:115
  438.9 3.8 fusion.91
  444.0 7.1 convolution_convert_fusion.1
  452.4 8.0 convolution_convert_fusion
  460.7 7.4 all-gather.12.cloned.1.call-done
  468.2 3.6 fusion.70
  481.4 169.0 %while.41 = (s32[]{:T(128)}, f32[4,72,72]{2,1,0:T(8,128)S(1)}, f32[16,4,64,72]{3,2,1,0:T(8,128)}, bf16[16,4,64,72]{3,2,1,0:T(8,128)(2,1)S(1)}, bf16[16,4,64,72]{...) while((s32[]{:T(128)}, f32[4,72,72]{2,1,0:T(8,128)S(1)}, ...), condition=%wide.region_27.28_spmd.clone, body=%wide.region_18.27_spmd.clone.sunk | while | flops 135152128 | bytes 4529631 | solution.py:69
  656.0 4.0 convolution_convert_fusion.3
  674.4 4.5 convolution_convert_fusion.2
  680.4 4.3 fusion.149
  689.6 11.5 %all-reduce.20 = s32[8]{0:T(128)S(1)} all-reduce(s32[8]{0:T(128)S(1)} %dynamic-update-slice), channel_id=1, replica_groups=mesh['dp'=8,'tensor'=4] {'dp'}, use_global_device_ids=true, to_apply=%add.20 | all-reduce | flops 8 | bytes 64
  707.6 7.5 multiply_reduce_fusion.12
  722.9 71.8 %reduce-scatter.17.cloned.1.call-done = bf16[144,3,288]{2,0,1:T(8,128)(2,1)} async-done(((bf16[1152,3,288]{2,0,1:T(8,128)(2,1)}), bf16[144,3,288]{2,0,1:T(8,128)(2,1)}) %reduce-scatter.17.cloned.1.call-update) | async-done | bytes 248848 | tf_op jit(solution)/shard_map/reduce_scatter | solution.py:333
  796.6 47.6 %reduce-scatter.15.cloned.1.call-done = f32[1024,288]{0,1:T(8,128)} async-done(((f32[1024,1152]{0,1:T(8,128)}), f32[1024,288]{0,1:T(8,128)}) %reduce-scatter.15.cloned.1.call-update) | async-done | bytes 1179664 | tf_op jit(solution)/shard_map/reduce_scatter | solution.py:123
  849.3 10.2 %all-reduce.22 = (f32[1024]{0:T(1024)S(1)}, f32[1,1024]{1,0:T(1,128)S(1)}, f32[1152]{0:T(1024)S(1)}) all-reduce(f32[1024]{0:T(1024)S(1)} %get-tuple-element.607, f32[1,1024]{1,0:T(1,128)S(1)} %bitcast.367, f32[1152]{0:T(1024)S(1)} %convolution_reduce_fusion), channel_id=1, replica_groups=mesh['dp'=8,'tensor'=4] {'tensor'}, use_global_device_ids=true, to_apply=%region_32.33 | all-reduce | flops 3200 | bytes 25600 | tf_op jit(solution)/shard_map/psum | solution.py:128
  863.4 70.7 %all-reduce.28.cloned.1.call-done = f32[89888]{0:T(1024)} async-done(((f32[89888]{0:T(1024)}), f32[89888]{0:T(1024)}) %all-reduce.28.cloned.1.call-update) | async-done | bytes 359568
  (777 shorter events, 415.3 us)
Async XLA Ops:
  7.2 291.7 %copy-start = (bf16[1152,1152]{1,0:T(8,128)(2,1)S(1)}, bf16[1152,1152]{1,0:T(8,128)(2,1)}, u32[]{:S(2)}) copy-start(bf16[1152,1152]{1,0:T(8,128)(2,1)} %param.29) | copy-start | bytes 7962628
  7.2 42.3 %all-gather.6.cloned.1.call-start = ((), (), s32[]{:S(2)}) async-start(), calls=%async_computation.8 | async-start | bytes 2949120 | tf_op jit(solution)/shard_map/all_gather | solution.py:111
  11.0 3.5 copy-start.28
  11.0 4.2 copy-start.4
  14.5 10.6 %copy-start.30 = (bf16[4]{0:T(256)(128)(2,1)S(1)}, bf16[4]{0:T(256)(128)(2,1)}, u32[]{:S(2)}) copy-start(bf16[4]{0:T(256)(128)(2,1)} %param.26) | copy-start | bytes 28
  14.5 10.6 %copy-start.26 = (bf16[3,3,288]{2,1,0:T(4,128)(2,1)S(1)}, bf16[3,3,288]{2,1,0:T(4,128)(2,1)}, u32[]{:S(2)}) copy-start(bf16[3,3,288]{2,1,0:T(4,128)(2,1)} %param.27) | copy-start | bytes 15556
  25.0 237.7 %reduce-scatter.9.cloned.1.call-start = ((), (), s32[]{:S(2)}) async-start(), calls=%async_computation.9 | async-start | bytes 5898240 | tf_op jit(solution)/shard_map/reduce_scatter | solution.py:115
  198.7 3.3 copy-start.23
  198.7 3.3 copy-start.24
  202.0 9.1 copy-start.14
  214.7 48.0 %copy-start.25 = (f32[288]{0:T(512)S(1)}, f32[288]{0:T(512)}, u32[]{:S(2)}) copy-start(f32[288]{0:T(512)} %get-tuple-element.630) | copy-start | bytes 3460
  214.7 56.5 %copy-start.27 = (f32[288]{0:T(512)S(1)}, f32[288]{0:T(512)}, u32[]{:S(2)}) copy-start(f32[288]{0:T(512)} %get-tuple-element.626) | copy-start | bytes 3460
  214.7 84.2 %all-gather.8.cloned.1.call-start = ((), (), s32[]{:S(2)}) async-start(), calls=%async_computation.10 | async-start | bytes 2949120 | tf_op jit(solution)/shard_map/all_gather | solution.py:111
  273.6 51.5 %all-gather.10.cloned.1.call-start = ((), (), s32[]{:S(2)}) async-start(), calls=%async_computation.12 | async-start | bytes 2949120 | tf_op jit(solution)/shard_map/all_gather | solution.py:119
  275.7 112.9 %reduce-scatter.13.cloned.1.call-start = ((), (), s32[]{:S(2)}) async-start(), calls=%async_computation.13 | async-start | bytes 5898240 | tf_op jit(solution)/shard_map/reduce_scatter | solution.py:123
  340.6 98.3 %reduce-scatter.11.cloned.1.call-start = ((), (), s32[]{:S(2)}) async-start(), calls=%async_computation.11 | async-start | bytes 5898240 | tf_op jit(solution)/shard_map/reduce_scatter | solution.py:115
  350.8 39.3 %copy-start.3 = (f32[1,1024,288]{1,2,0:T(8,128)S(1)}, f32[1,1024,288]{1,2,0:T(8,128)}, u32[]{:S(2)}) copy-start(f32[1,1024,288]{1,2,0:T(8,128)} %get-tuple-element.688) | copy-start | bytes 3538948
  350.8 117.4 %all-gather.12.cloned.1.call-start = ((), (), s32[]{:S(2)}) async-start(), calls=%async_computation.14 | async-start | bytes 2949120 | tf_op jit(solution)/shard_map/all_gather | solution.py:119
  442.7 8.4 copy-start.8
  443.9 257.8 %reduce-scatter.21.cloned.1.call-start = ((), (), s32[]{:S(2)}) async-start(), calls=%async_computation.18 | async-start | bytes 2985984 | tf_op jit(solution)/shard_map/reduce_scatter | solution.py:333
  451.1 252.5 %reduce-scatter.23.cloned.1.call-start = ((), (), s32[]{:S(2)}) async-start(), calls=%async_computation.19 | async-start | bytes 2985984 | tf_op jit(solution)/shard_map/reduce_scatter | solution.py:333
  460.4 7.7 copy-start.15
  460.5 260.9 %reduce-scatter.19.cloned.1.call-start = ((), (), s32[]{:S(2)}) async-start(), calls=%async_computation.17 | async-start | bytes 995328 | tf_op jit(solution)/shard_map/reduce_scatter | solution.py:333
  650.4 5.6 copy-start.12
  660.0 134.7 %reduce-scatter.17.cloned.1.call-start = ((), (), s32[]{:S(2)}) async-start(), calls=%async_computation.16 | async-start | bytes 2985984 | tf_op jit(solution)/shard_map/reduce_scatter | solution.py:333
  669.7 4.7 copy-start.6
  678.9 165.2 %reduce-scatter.15.cloned.1.call-start = ((), (), s32[]{:S(2)}) async-start(), calls=%async_computation.15 | async-start | bytes 5898240 | tf_op jit(solution)/shard_map/reduce_scatter | solution.py:123
  687.6 17.9 %copy-start.13 = (f32[1024,288]{0,1:T(8,128)S(1)}, f32[1024,288]{0,1:T(8,128)}, u32[]{:S(2)}) copy-start(f32[1024,288]{0,1:T(8,128)} %fusion.70) | copy-start | bytes 3538948
  687.7 246.4 %all-reduce.28.cloned.1.call-start = ((), (), s32[]{:S(2)}) async-start(), calls=%async_computation.20 | async-start | bytes 720896
  707.6 7.6 copy-start.2
  846.4 15.5 %copy-start.9 = (f32[1,1024,288]{1,2,0:T(8,128)S(1)}, f32[1,1024,288]{1,2,0:T(8,128)}, u32[]{:S(2)}) copy-start(f32[1,1024,288]{1,2,0:T(8,128)} %copy-done.8) | copy-start | bytes 3538948
  939.8 8.2 copy-start.1
  (14 other events, 29.4 us)
Sparse Core Ops, SparseCore 0:
  25.1 24.3 all-gather.5
  214.8 47.8 reduce-scatter.8
  273.7 25.1 all-gather.7
  301.0 24.0 all-gather.9
  340.7 47.8 reduce-scatter.12
  391.0 47.8 reduce-scatter.10
  444.0 24.0 all-gather.11
  472.3 70.7 reduce-scatter.20
  546.8 70.2 reduce-scatter.22
  660.1 61.1 reduce-scatter.18
  725.4 69.2 reduce-scatter.16
  797.1 46.9 reduce-scatter.14
  862.0 71.9 all-reduce.27

commit v2 on v1

--- a/solution.py
+++ b/solution.py
@@ -1,16 +1,17 @@
-from functools import partial
+import functools
 import math
 
 import jax
 import jax.numpy as jnp
 from jax import lax
+from jax.experimental import pallas as pl
+from jax.experimental.pallas import tpu as pltpu
 from jax.sharding import PartitionSpec as P
 
 MODEL_DIM = 1152
 HD = 72
 NCLASS = 1000
 GRID = 32
-CH = 64
 
 
 TOP_PRECISION = lax.Precision.HIGHEST
@@ -24,76 +25,262 @@
     return jnp.concatenate([jnp.cos(angles), jnp.sin(angles)], axis=1)
 
 
-def span_pass(running_state, block):
-    query_matrix, key_matrix, value_matrix, log_forget = block
-    block_len = log_forget.shape[1]
-    decay_factors = jnp.cumsum(log_forget, axis=1)
-    causal_mask = (jnp.arange(block_len)[:, None] >= jnp.arange(block_len)[None, :])[None]
-    decay_gap = jnp.where(causal_mask, decay_factors[:, :, None] - decay_factors[:, None, :], 0.0)
-    score_matrix = jnp.einsum("mkd,mld->mkl", query_matrix, key_matrix, precision=TOP_PRECISION)
-    weighted_values = jnp.where(causal_mask, jnp.exp(decay_gap), 0.0) * score_matrix
-    within_block_part = jnp.einsum(
-        "dps,dsh->dph", weighted_values, value_matrix, precision=TOP_PRECISION
-    )
-    across_block_part = jnp.einsum(
-        "ugm,ump->ugp",
-        query_matrix * jnp.exp(decay_factors)[:, :, None],
-        running_state,
-        precision=TOP_PRECISION,
-    )
-    final_decay = decay_factors[:, -1:]
-    carried = key_matrix * jnp.exp(final_decay - decay_factors)[:, :, None]
-    running_state = running_state * jnp.exp(final_decay)[:, :, None] + jnp.einsum(
-        "nje,njf->nef", carried, value_matrix, precision=TOP_PRECISION
-    )
-    return (running_state, within_block_part + across_block_part)
-
-
-def gated_scan(query_matrix, key_matrix, value_matrix, log_forget, span):
-    latents, length, head_count, head_dim = query_matrix.shape
-    blocks = length // span
-
-    def arrange(array):
-        return (
-            array.reshape(latents, blocks, span, head_count, head_dim)
-            .transpose(1, 0, 3, 2, 4)
-            .reshape(blocks, latents * head_count, span, head_dim)
+SPAN = 256
+
+TN = (((0,), (0,)), ((), ()))
+NT = (((1,), (1,)), ((), ()))
+NN = (((1,), (0,)), ((), ()))
+NTT = (((0,), (1,)), ((), ()))
+
+
+def mm(left, right, form):
+    return lax.dot_general(left, right, form, preferred_element_type=jnp.float32)
+
+
+def low(values):
+    return values.astype(jnp.bfloat16)
+
+
+def shifted(rows, offset):
+    length = rows.shape[1]
+    return pltpu.roll(rows, (-offset) % length, 1)
+
+
+def edge_masks(length):
+    token = lax.broadcasted_iota(jnp.int32, (1, length), 1)
+    column = lax.rem(token, GRID)
+    return column > 0, column < GRID - 1, token >= GRID, token < length - GRID
+
+
+def neighbours(rows, masks):
+    left_ok, right_ok, _, _ = masks
+    return (
+        jnp.where(left_ok, shifted(rows, -1), 0.0),
+        rows,
+        jnp.where(right_ok, shifted(rows, 1), 0.0),
+    )
+
+
+def running_sum(rows, span, reverse=False, exclusive=False):
+    length = rows.shape[1]
+    place = lax.rem(lax.broadcasted_iota(jnp.int32, (1, length), 1), span)
+    total = rows
+    step = 1
+    if exclusive:
+        total = (
+            jnp.where(place < span - 1, shifted(total, 1), 0.0)
+            if reverse
+            else jnp.where(place >= 1, shifted(total, -1), 0.0)
         )
-
-    log_blocks = (
-        log_forget.reshape(latents, blocks, span, head_count)
-        .transpose(1, 0, 3, 2)
-        .reshape(blocks, latents * head_count, span)
-    )
-    initial = jnp.zeros((latents * head_count, head_dim, head_dim), query_matrix.dtype)
-    _, results = lax.scan(
-        jax.checkpoint(span_pass),
-        initial,
-        (arrange(query_matrix), arrange(key_matrix), arrange(value_matrix), log_blocks),
-    )
-    results = results.reshape(blocks, latents, head_count, span, head_dim).transpose(1, 0, 3, 2, 4)
-    return results.reshape(latents, length, head_count * head_dim)
-
-
-def depthwise(field, kernel, grid_side):
-    latents = field.shape[0]
-    channels = field.shape[2]
-    image = field.reshape(latents, grid_side, grid_side, channels)
-    padded = jnp.pad(image, ((0, 0), (1, 1), (1, 1), (0, 0)))
-    summed = jnp.zeros_like(image)
-    for row_off in range(3):
-        for col_off in range(3):
-            summed = (
-                summed
-                + padded[:, row_off : row_off + grid_side, col_off : col_off + grid_side, :]
-                * kernel[row_off, col_off]
-            )
-    return summed.reshape(latents, grid_side * grid_side, channels)
-
-
-def mixer_rows(query_matrix, key_matrix, value_matrix, log_forget, kernel, span, grid_side):
-    recurrent = gated_scan(query_matrix, key_matrix, value_matrix, log_forget, span)
-    return depthwise(recurrent, kernel, grid_side)
+    while step < span:
+        if reverse:
+            total = total + jnp.where(place < span - step, shifted(total, step), 0.0)
+        else:
+            total = total + jnp.where(place >= step, shifted(total, -step), 0.0)
+        step *= 2
+    return total
+
+
+def log_sigmoid(logit):
+    return jnp.minimum(logit, 0.0) - jnp.log(1.0 + jnp.exp(-jnp.abs(logit)))
+
+
+def conv_rows(rows, taps, masks, adjoint):
+    _, _, up_ok, down_ok = masks
+    left, middle, right = neighbours(rows, masks)
+    parts = []
+    for row in range(3):
+        if adjoint:
+            weights = [taps[:, 3 * (2 - row) + 2 - col : 3 * (2 - row) + 3 - col] for col in range(3)]
+        else:
+            weights = [taps[:, 3 * row + col : 3 * row + col + 1] for col in range(3)]
+        parts.append(left * weights[0] + middle * weights[1] + right * weights[2])
+    above = jnp.where(up_ok, shifted(parts[0], -GRID), 0.0)
+    below = jnp.where(down_ok, shifted(parts[2], GRID), 0.0)
+    return above + parts[1] + below
+
+
+def decay_block(row, column):
+    span = row.shape[1]
+    key_at = lax.broadcasted_iota(jnp.int32, (span, span), 0)
+    query_at = lax.broadcasted_iota(jnp.int32, (span, span), 1)
+    return jnp.where(query_at >= key_at, jnp.exp(jnp.minimum(row - column, 0.0)), 0.0)
+
+
+def mixer_kernel(heads, proj_ref, logit_ref, taps_ref, mixed_ref, rec_ref, states_ref, wide, cum_ref, col_ref):
+    part, length = rec_ref.shape
+    spans = length // SPAN
+    log_forget = log_sigmoid(logit_ref[...])
+    cum = running_sum(log_forget, SPAN)
+    cum_ref[...] = cum
+    col_ref[...] = jnp.transpose(cum)
+    wide[...] = proj_ref[...].astype(jnp.float32)
+    scale = HD ** (-0.5)
+
+    def one_span(at, states):
+        lanes = pl.ds(pl.multiple_of(at * SPAN, SPAN), SPAN)
+        after = []
+        for head in range(heads):
+            at_rows = [pl.ds(kind * part + head * HD, HD) for kind in range(3)]
+            query, key, value = (wide[rows, lanes] for rows in at_rows)
+            row = cum_ref[head : head + 1, lanes]
+            column = col_ref[lanes, head : head + 1]
+            last = row[:, SPAN - 1 : SPAN]
+            state = states[head]
+            states_ref[at, head] = state
+            weights = decay_block(row, column) * mm(low(key), low(query), TN)
+            out = mm(low(value), low(weights), NN)
+            out = out + mm(low(state), low(query * jnp.exp(row)), NN)
+            rec_ref[pl.ds(head * HD, HD), lanes] = out * scale
+            carried = low(key * jnp.exp(last - row))
+            after.append(state * jnp.exp(last) + mm(low(value), carried, NT))
+        return tuple(after)
+
+    lax.fori_loop(0, spans, one_span, tuple(jnp.zeros((HD, HD), jnp.float32) for _ in range(heads)))
+    masks = edge_masks(length)
+
+    def one_group(at, carry):
+        rows = pl.ds(pl.multiple_of(at * 16, 16), 16)
+        mixed_ref[rows, :] = low(conv_rows(rec_ref[rows, :], taps_ref[rows, :], masks, False))
+        return carry
+
+    lax.fori_loop(0, part // 16, one_group, 0)
+
+
+def mixer(proj, logit, taps, heads):
+    part = proj.shape[0] // 3
+    length = proj.shape[1]
+    spans = length // SPAN
+    return pl.pallas_call(
+        functools.partial(mixer_kernel, heads),
+        out_shape=(
+            jax.ShapeDtypeStruct((part, length), jnp.bfloat16),
+            jax.ShapeDtypeStruct((part, length), jnp.float32),
+            jax.ShapeDtypeStruct((spans, heads, HD, HD), jnp.float32),
+        ),
+        in_specs=[pl.BlockSpec(memory_space=pltpu.VMEM)] * 3,
+        out_specs=[pl.BlockSpec(memory_space=pltpu.VMEM)] * 3,
+        scratch_shapes=[
+            pltpu.VMEM((3 * part, length), jnp.float32),
+            pltpu.VMEM((8, length), jnp.float32),
+            pltpu.VMEM((length, 8), jnp.float32),
+        ],
+        compiler_params=pltpu.CompilerParams(vmem_limit_bytes=56 * 2**20),
+        name="mixer",
+    )(proj, logit, taps)
+
+
+def back_kernel(
+    heads, proj_ref, logit_ref, taps_ref, rec_ref, states_ref, grad_ref,
+    gproj_ref, gforget_ref, gtaps_ref, wide, gwide, cum_ref, col_ref, grec_ref, rows_ref,
+):
+    part, length = rec_ref.shape
+    spans = length // SPAN
+    logit = logit_ref[...]
+    cum = running_sum(log_sigmoid(logit), SPAN)
+    cum_ref[...] = cum
+    col_ref[...] = jnp.transpose(cum)
+    wide[...] = proj_ref[...].astype(jnp.float32)
+    masks = edge_masks(length)
+    scale = HD ** (-0.5)
+    lane = lax.broadcasted_iota(jnp.int32, (16, 16), 1)
+
+    def one_group(at, carry):
+        rows = pl.ds(pl.multiple_of(at * 16, 16), 16)
+        grad = grad_ref[rows, :].astype(jnp.float32)
+        grec_ref[rows, :] = conv_rows(grad, taps_ref[rows, :], masks, True) * scale
+        moved = neighbours(rec_ref[rows, :], masks)
+        _, _, up_ok, down_ok = masks
+        grads = (
+            jnp.where(down_ok, shifted(grad, GRID), 0.0),
+            grad,
+            jnp.where(up_ok, shifted(grad, -GRID), 0.0),
+        )
+        result = jnp.zeros((16, 16), jnp.float32)
+        for row in range(3):
+            for col in range(3):
+                one = jnp.sum(moved[col] * grads[row], axis=1, keepdims=True)
+                result = jnp.where(lane == 3 * row + col, one, result)
+        gtaps_ref[rows, :] = result
+        return carry
+
+    lax.fori_loop(0, part // 16, one_group, 0)
+    rows_ref[...] = jnp.zeros_like(rows_ref)
+    key_at = lax.broadcasted_iota(jnp.int32, (SPAN, SPAN), 0)
+    query_at = lax.broadcasted_iota(jnp.int32, (SPAN, SPAN), 1)
+    later = low(jnp.where(key_at >= query_at, 1.0, 0.0))
+
+    def one_span(step, back_states):
+        at = spans - 1 - step
+        lanes = pl.ds(pl.multiple_of(at * SPAN, SPAN), SPAN)
+        after = []
+        for head in range(heads):
+            at_rows = [pl.ds(kind * part + head * HD, HD) for kind in range(3)]
+            query, key, value = (wide[rows, lanes] for rows in at_rows)
+            grad = low(grec_ref[pl.ds(head * HD, HD), lanes])
+            row = cum_ref[head : head + 1, lanes]
+            column = col_ref[lanes, head : head + 1]
+            last = row[:, SPAN - 1 : SPAN]
+            state = states_ref[at, head]
+            back = back_states[head]
+            decay = decay_block(row, column)
+            score = mm(low(key), low(query), TN)
+            weights = decay * score
+            grad_weights = mm(low(value), grad, TN)
+            grad_score = grad_weights * decay
+            product = low(grad_weights * weights)
+            grad_score = low(grad_score)
+            in_decay = jnp.exp(row)
+            out_decay = jnp.exp(last - row)
+            query_in = mm(low(state), grad, TN) * in_decay
+            key_out = mm(low(back), low(value), TN) * out_decay
+            gwide[at_rows[0], lanes] = mm(low(key), grad_score, NN) + query_in
+            gwide[at_rows[1], lanes] = mm(low(query), grad_score, NT) + key_out
+            carried = low(key * out_decay)
+            gwide[at_rows[2], lanes] = mm(grad, low(weights), NT) + mm(low(back), carried, NN)
+            inside = mm(product, later, NN)
+            inside = jnp.sum(jnp.where(key_at < query_at, inside, 0.0), axis=0, keepdims=True)
+            span_decay = jnp.exp(last)
+            across = jnp.sum(back * state, keepdims=True) * span_decay
+            rows_ref[0, head : head + 1, lanes] = jnp.sum(query * query_in, axis=0, keepdims=True)
+            rows_ref[1, head : head + 1, lanes] = jnp.sum(key * key_out, axis=0, keepdims=True)
+            rows_ref[2, head : head + 1, lanes] = inside + across
+            after.append(back * span_decay + mm(grad, low(query * in_decay), NT))
+        return tuple(after)
+
+    lax.fori_loop(0, spans, one_span, tuple(jnp.zeros((HD, HD), jnp.float32) for _ in range(heads)))
+    grad_log = (
+        running_sum(rows_ref[0], SPAN, reverse=True)
+        + running_sum(rows_ref[1], SPAN, exclusive=True)
+        + rows_ref[2]
+    )
+    gforget_ref[...] = low(grad_log / (1.0 + jnp.exp(logit)))
+    gproj_ref[...] = low(gwide[...])
+
+
+def mixer_back(proj, logit, taps, rec, states, grad, heads):
+    part = proj.shape[0] // 3
+    length = proj.shape[1]
+    return pl.pallas_call(
+        functools.partial(back_kernel, heads),
+        out_shape=(
+            jax.ShapeDtypeStruct((3 * part, length), jnp.bfloat16),
+            jax.ShapeDtypeStruct((8, length), jnp.bfloat16),
+            jax.ShapeDtypeStruct((part, 16), jnp.float32),
+        ),
+        in_specs=[pl.BlockSpec(memory_space=pltpu.VMEM)] * 6,
+        out_specs=[pl.BlockSpec(memory_space=pltpu.VMEM)] * 3,
+        scratch_shapes=[
+            pltpu.VMEM((3 * part, length), jnp.float32),
+            pltpu.VMEM((3 * part, length), jnp.float32),
+            pltpu.VMEM((8, length), jnp.float32),
+            pltpu.VMEM((length, 8), jnp.float32),
+            pltpu.VMEM((part, length), jnp.float32),
+            pltpu.VMEM((3, 8, length), jnp.float32),
+        ],
+        compiler_params=pltpu.CompilerParams(vmem_limit_bytes=56 * 2**20),
+        name="mixer_back",
+    )(proj, logit, taps, rec, states, grad)
 
 
 def tanh_gelu(inputs):
@@ -177,31 +364,13 @@
     first_normalized = share_rows((unit_one * (1.0 + scale_one) + shift_one).astype(jnp.bfloat16))
     rows_one = first_normalized.reshape(row_count, MODEL_DIM)
     qkv_flat = query_key_value_weight.reshape(MODEL_DIM, 3 * part_width)
-    projected_rows = jnp.dot(rows_one, qkv_flat, preferred_element_type=jnp.float32).astype(
-        jnp.bfloat16
-    )
-    forget_logit = jnp.dot(
-        rows_one, gate_weight, preferred_element_type=jnp.float32
-    ) + gate_bias.astype(jnp.float32)
-
-    def head_view(columns):
-        return columns.astype(jnp.float32).reshape(latents, length, heads_here, HD)
-
-    query_matrix = head_view(projected_rows[:, :part_width]) * HD ** (-0.5)
-    key_matrix = head_view(projected_rows[:, part_width : 2 * part_width])
-    value_matrix = head_view(projected_rows[:, 2 * part_width :])
-    log_forget = jax.nn.log_sigmoid(forget_logit).reshape(latents, length, heads_here)
-    mixed_out, mixer_pull = jax.vjp(
-        partial(mixer_rows, span=CH, grid_side=GRID),
-        query_matrix,
-        key_matrix,
-        value_matrix,
-        log_forget,
-        conv_weight.astype(jnp.float32),
-    )
-    mixer_low = mixed_out.reshape(row_count, part_width).astype(jnp.bfloat16)
+    projected = low(mm(qkv_flat, rows_one, NTT))
+    forget_logit = mm(gate_weight, rows_one, NTT) + gate_bias.astype(jnp.float32)[:, None]
+    forget_logit = jnp.pad(forget_logit, ((0, 8 - heads_here), (0, 0)))
+    taps = jnp.pad(conv_weight.astype(jnp.float32).reshape(9, part_width).T, ((0, 0), (0, 7)))
+    mixed_low, recurrent, states = mixer(projected, forget_logit, taps, heads_here)
     attn_out = branch_total(
-        jnp.dot(mixer_low, out_weight, preferred_element_type=jnp.float32)
+        mm(mixed_low, out_weight, TN)
     ).reshape(latents, length, part_width)
     after_attn = tokens_value + gate_one * attn_out
     mean_two, std_inv_two = moments(after_attn, MODEL_DIM)
@@ -236,27 +405,18 @@
     grad_attn = spread_grads((grad_after * gate_one).astype(jnp.bfloat16)).reshape(
         row_count, MODEL_DIM
     )
-    grad_out_w = jnp.einsum("rp,rd->pd", mixer_low, grad_attn, preferred_element_type=jnp.float32)
-    grad_mixed = jnp.einsum(
-        "rd,pd->rp", grad_attn, out_weight, preferred_element_type=jnp.float32
-    ).reshape(latents, length, part_width)
-    grad_query, grad_key, grad_value, grad_log, grad_conv = mixer_pull(grad_mixed)
-    grad_projected = (
-        jnp.concatenate([grad_query * HD ** (-0.5), grad_key, grad_value], axis=2)
-        .reshape(row_count, 3 * part_width)
-        .astype(jnp.bfloat16)
-    )
-    grad_forget = (grad_log.reshape(row_count, heads_here) * jax.nn.sigmoid(-forget_logit)).astype(
-        jnp.bfloat16
-    )
-    grad_qkv = jnp.einsum(
-        "rd,rc->dc", rows_one, grad_projected, preferred_element_type=jnp.float32
-    ).reshape(MODEL_DIM, 3, part_width)
-    grad_gate_w = jnp.einsum("rd,rh->dh", rows_one, grad_forget, preferred_element_type=jnp.float32)
-    grad_gate_b = jnp.sum(grad_forget.astype(jnp.float32), axis=0)
+    grad_out_w = mm(mixed_low, grad_attn, NN)
+    grad_mixed = mm(out_weight, grad_attn, NT)
+    grad_projected, grad_forget, grad_taps = mixer_back(
+        projected, forget_logit, taps, recurrent, states, grad_mixed, heads_here
+    )
+    grad_forget = grad_forget[:heads_here]
+    grad_conv = grad_taps[:, :9].T
+    grad_qkv = mm(rows_one, grad_projected, NTT).reshape(MODEL_DIM, 3, part_width)
+    grad_gate_w = mm(rows_one, grad_forget, NTT)
+    grad_gate_b = jnp.sum(grad_forget.astype(jnp.float32), axis=1)
     grad_normed_one = input_total(
-        jnp.einsum("rc,dc->rd", grad_projected, qkv_flat, preferred_element_type=jnp.float32)
-        + jnp.einsum("rh,dh->rd", grad_forget, gate_weight, preferred_element_type=jnp.float32)
+        mm(grad_projected, qkv_flat, NTT) + mm(grad_forget, gate_weight, NTT)
     ).reshape(latents, length, part_width)
     grad_shift_one = jnp.sum(grad_normed_one, axis=1)
     grad_scale_one = jnp.sum(grad_normed_one * unit_one, axis=1)

time: 962 us -> 779 us (0.81)
  matrix products: 262 us -> 89.7 us
  waiting for transfers between devices: 391 us -> 542 us
  local copies, waits for them, and re-layouts: 147 us -> 22.3 us
  other arithmetic: 92.3 us -> 29.7 us
  Pallas kernels: 0 us -> 29.1 us
    dot_general x217 -> x9, matrix products: 207 us -> 35.2 us  [mm(): lax.dot_general(left, right, form, preferred_element_type=jnp.float32)]
    reduce_scatter x4, waiting for transfers between devices: 72.6 us -> 223 us  [dp_total(): lax.psum_scatter(low, 'dp', scatter_dimension=axis, tiled=True)]
    squeeze x80 -> x0, local copies, waits for them, and re-layouts: 46 us -> none  [gated_scan(): lax.scan(jax.checkpoint(span_pass), initial, (arrange(query_matrix), arra...]
    pallas_call x0 -> x2, Pallas kernels: none -> 29.1 us  [the longest x1 18.3 us: mixer_back(): pl.pallas_call(functools.partial(back_kernel, heads), out_shape=(jax.Shap...]
    another operation x80 -> x0, other arithmetic: 16.4 us -> none  [the longest x64 16.2 us: span_pass(): decay_factors = jnp.cumsum(log_forget, axis=1)]
    reduce_sum x35 -> x1, other arithmetic: 15 us -> 0.12 us  [shards(): grad_gate_b = jnp.sum(grad_forget.astype(jnp.float32), axis=1)]
    dynamic_slice x16 -> x0, local copies, waits for them, and re-layouts: 14.7 us -> none  [gated_scan(): lax.scan(jax.checkpoint(span_pass), initial, (arrange(query_matrix), arra...]
    unnamed x79 -> x51, local copies, waits for them, and re-layouts: 27.5 us -> 12.8 us
  transfers between devices with their start and end apart: 13 -> 13, of which waited for: 11 -> 13; matrix products, arithmetic and copies ran while one was open for 29% -> 9% of each run, Pallas kernels for 0% -> 2%
where the time goes in v2:
time: 779 us; the launch traced here: 772 us
  waiting for transfers between devices  542 us (70%)
  matrix products  89.7 us (12%)
  blocking collectives  42 us (5%)
  other arithmetic  29.7 us (4%)
  Pallas kernels  29.1 us (4%)
  local copies, waits for them, and re-layouts  22.3 us (3%)
  between operations  16.6 us (2%)
    reduce_scatter x4, waiting for transfers between devices, dp_total(): lax.psum_scatter(low, 'dp', scatter_dimension=axis, tiled=True)  223 us
    reduce_scatter x2, waiting for transfers between devices, branch_total(): lax.psum_scatter(partial_rows, 'tensor', scatter_dimension=1, tiled=True)  89.2 us
    reduce_scatter x2, waiting for transfers between devices, input_total(): lax.psum_scatter(partial_rows, 'tensor', scatter_dimension=1, tiled=True)  85.2 us
    unnamed x14, waiting for transfers between devices  71 us
    all_gather x2, waiting for transfers between devices, share_rows(): return lax.all_gather(local_rows, 'tensor', axis=2, tiled=True)  46.6 us
    dot_general x9, matrix products, mm(): lax.dot_general(left, right, form, preferred_element_type=jnp.float32)  35.2 us
    all_gather x2, waiting for transfers between devices, spread_grads(): return lax.all_gather(local_grads, 'tensor', axis=2, tiled=True)  26.1 us
    pallas_call x1, Pallas kernels, mixer_back(): pl.pallas_call(functools.partial(back_kernel, heads), out_shape=(jax.Shap...  18.3 us
  transfers between devices with their start and end apart: 13, of which 13 were waited for; matrix products, arithmetic and copies ran while one was open for 9% of the time, Pallas kernels for 2%

profile of v2, /device:TPU:0, one launch (start us, length us, event | category | flops | bytes accessed | tf_op | source)
XLA Modules:
  0.0 772.4 jit_solution(6706689539633858503)
XLA Ops:
  14.8 8.5 %all-reduce.7 = (f32[1,1024]{1,0:T(1,128)S(1)}, f32[1,1024]{1,0:T(1,128)S(1)}) all-reduce(f32[1,1024]{1,0:T(1,128)S(1)} %bitcast.149, f32[1,1024]{1,0:T(1,128)S(1)} %bitcast.148), channel_id=1, replica_groups=mesh['dp'=8,'tensor'=4] {'tensor'}, use_global_device_ids=true, to_apply=%region_3.4 | all-reduce | flops 2048 | bytes 16384 | tf_op jit(solution)/shard_map/psum | solution.py:291
  25.4 23.6 %all-gather.6.cloned.1.call-done = bf16[1,1024,1152]{1,2,0:T(8,128)(2,1)} async-done(((bf16[1,1024,288]{1,2,0:T(8,128)(2,1)}), bf16[1,1024,1152]{1,2,0:T(8,128)(2,1)}) %all-gather.6.cloned.1.call-update) | async-done | bytes 2359312 | tf_op jit(solution)/shard_map/all_gather | solution.py:298
  51.8 5.2 convert_bitcast_fusion.proj_ref
  57.1 10.8 %mixer.1 = (bf16[288,1024]{1,0:T(8,128)(2,1)}, f32[288,1024]{1,0:T(8,128)}, f32[4,4,72,72]{3,2,1,0:T(8,128)}) custom-call(bf16[864,1024]{1,0:T(8,128)(2,1)} %convert_bitcast_fusion.proj_ref, f32[8,1024]{1,0:T(8,128)} %pad.10.logit_ref, f32[288,16]{1,0:T(8,128)} %pad_convert_fusion.taps_ref), custom_call_target="tpu_custom_call" | custom-call | tf_op jit(solution)/shard_map/mixer/pallas_call | solution.py:154
  67.9 4.6 fusion.87
  72.6 48.0 %reduce-scatter.9.cloned.1.call-done = f32[1024,288]{0,1:T(8,128)} async-done(((f32[1024,1152]{0,1:T(8,128)}), f32[1024,288]{0,1:T(8,128)}) %reduce-scatter.9.cloned.1.call-update) | async-done | bytes 1179664 | tf_op jit(solution)/shard_map/reduce_scatter | solution.py:302
  123.1 5.8 all-reduce.6
  133.7 23.0 %all-gather.8.cloned.1.call-done = bf16[1,1024,1152]{1,2,0:T(8,128)(2,1)} async-done(((bf16[1,1024,288]{1,2,0:T(8,128)(2,1)}), bf16[1,1024,1152]{1,2,0:T(8,128)(2,1)}) %all-gather.8.cloned.1.call-update) | async-done | bytes 2359312 | tf_op jit(solution)/shard_map/all_gather | solution.py:298
  156.8 7.3 fusion.19
  164.1 18.8 %all-gather.10.cloned.1.call-done = bf16[1,1024,1152]{1,2,0:T(8,128)(2,1)} async-done(((bf16[1,1024,288]{1,2,0:T(8,128)(2,1)}), bf16[1,1024,1152]{1,2,0:T(8,128)(2,1)}) %all-gather.10.cloned.1.call-update) | async-done | bytes 2359312 | tf_op jit(solution)/shard_map/all_gather | solution.py:306
  182.9 9.2 %fusion.6 = bf16[1024,1152]{1,0:T(8,128)(2,1)S(1)} fusion(f32[1024,1152]{1,0:T(8,128)} %fusion.19, bf16[1152,1152]{1,0:T(8,128)(2,1)} %param.26, bf16[1,1024,1152]{1,2,0:T(8,128)(2,1)} %all-gather.10.cloned.1.call-done), kind=kOutput, calls=%fused_computation.11 | convolution fusion | flops 2741501952 | bytes 12091392 | tf_op jit(solution)/shard_map/rd,fd->rf/dot_general | solution.py:393
  193.5 4.9 fusion.88
  200.2 8.4 %fusion.82 = f32[1024,1152]{0,1:T(8,128)} fusion(bf16[1152,1152]{1,0:T(8,128)(2,1)S(1)} %copy-done.17, f32[1024,1152]{1,0:T(8,128)} %fusion.19), kind=kOutput, calls=%fused_computation.131 | convolution fusion | flops 2728525824 | bytes 12091392 | tf_op jit(solution)/shard_map/dot_general | solution.py:384
  208.7 37.8 %reduce-scatter.13.cloned.1.call-done = f32[1024,288]{0,1:T(8,128)} async-done(((f32[1024,1152]{0,1:T(8,128)}), f32[1024,288]{0,1:T(8,128)}) %reduce-scatter.13.cloned.1.call-update) | async-done | bytes 1179664 | tf_op jit(solution)/shard_map/reduce_scatter | solution.py:310
  249.6 5.9 all-reduce.5
  255.5 41.3 %reduce-scatter.11.cloned.1.call-done = f32[1024,288]{0,1:T(8,128)} async-done(((f32[1024,1152]{0,1:T(8,128)}), f32[1024,288]{0,1:T(8,128)}) %reduce-scatter.11.cloned.1.call-update) | async-done | bytes 1179664 | tf_op jit(solution)/shard_map/reduce_scatter | solution.py:302
  296.8 3.8 fusion.33
  301.7 7.1 convolution_convert_fusion.1
  310.9 7.3 convolution_convert_fusion
  318.7 7.2 all-gather.12.cloned.1.call-done
  325.9 4.0 convolution_convert_fusion.3
  333.7 18.3 %mixer_back.1 = (bf16[864,1024]{1,0:T(8,128)(2,1)}, bf16[8,1024]{1,0:T(8,128)(2,1)}, f32[288,16]{1,0:T(8,128)}) custom-call(bf16[864,1024]{1,0:T(8,128)(2,1)} %convert_bitcast_fusion.proj_ref, f32[8,1024]{1,0:T(8,128)} %pad.10.logit_ref, f32[288,16]{1,0:T(8,128)} %pad_convert_fusion.taps_ref, f32[288,1024]{1,0:T(8,128)} %get-tuple-element.19.rec_ref, ...), custom_call_target="tpu_custom_call" | custom-call | tf_op jit(solution)/shard_map/mixer_back/pallas_call | solution.py:264
  352.0 6.1 convolution_convert_fusion.2
  358.1 4.8 fusion.89
  367.9 11.4 %all-reduce.2 = s32[8]{0:T(128)S(1)} all-reduce(s32[8]{0:T(128)S(1)} %dynamic-update-slice), channel_id=1, replica_groups=mesh['dp'=8,'tensor'=4] {'dp'}, use_global_device_ids=true, to_apply=%add.2 | all-reduce | flops 8 | bytes 64
  379.9 20.6 %reduce-scatter.21.cloned.1.call-done = bf16[144,1152]{1,0:T(8,128)(2,1)} async-done(((bf16[1152,1152]{1,0:T(8,128)(2,1)}), bf16[144,1152]{1,0:T(8,128)(2,1)}) %reduce-scatter.21.cloned.1.call-update) | async-done | bytes 331792 | tf_op jit(solution)/shard_map/reduce_scatter | solution.py:493
  402.4 71.4 %reduce-scatter.23.cloned.1.call-done = bf16[1152,144]{0,1:T(8,128)(2,1)} async-done(((bf16[1152,1152]{0,1:T(8,128)(2,1)}), bf16[1152,144]{0,1:T(8,128)(2,1)}) %reduce-scatter.23.cloned.1.call-update) | async-done | bytes 331792 | tf_op jit(solution)/shard_map/reduce_scatter | solution.py:493
  479.0 58.9 %reduce-scatter.19.cloned.1.call-done = bf16[288,144]{0,1:T(8,128)(2,1)} async-done(((bf16[288,1152]{0,1:T(8,128)(2,1)}), bf16[288,144]{0,1:T(8,128)(2,1)}) %reduce-scatter.19.cloned.1.call-update) | async-done | bytes 82960 | tf_op jit(solution)/shard_map/reduce_scatter | solution.py:493
  539.5 72.5 %reduce-scatter.17.cloned.1.call-done = bf16[144,3,288]{2,0,1:T(8,128)(2,1)} async-done(((bf16[1152,3,288]{2,0,1:T(8,128)(2,1)}), bf16[144,3,288]{2,0,1:T(8,128)(2,1)}) %reduce-scatter.17.cloned.1.call-update) | async-done | bytes 248848 | tf_op jit(solution)/shard_map/reduce_scatter | solution.py:493
  613.9 47.5 %reduce-scatter.15.cloned.1.call-done = f32[1024,288]{0,1:T(8,128)} async-done(((f32[1024,1152]{0,1:T(8,128)}), f32[1024,288]{0,1:T(8,128)}) %reduce-scatter.15.cloned.1.call-update) | async-done | bytes 1179664 | tf_op jit(solution)/shard_map/reduce_scatter | solution.py:310
  666.5 10.4 %all-reduce.4 = (f32[1024]{0:T(1024)S(1)}, f32[1,1024]{1,0:T(1,128)S(1)}, f32[1152]{0:T(1024)S(1)}) all-reduce(f32[1024]{0:T(1024)S(1)} %get-tuple-element.75, f32[1,1024]{1,0:T(1,128)S(1)} %bitcast.150, f32[1152]{0:T(1024)S(1)} %convolution_reduce_fusion), channel_id=1, replica_groups=mesh['dp'=8,'tensor'=4] {'tensor'}, use_global_device_ids=true, to_apply=%region_19.20 | all-reduce | flops 3200 | bytes 25600 | tf_op jit(solution)/shard_map/psum | solution.py:315
  680.8 70.8 %all-reduce.10.cloned.1.call-done = f32[89888]{0:T(1024)} async-done(((f32[89888]{0:T(1024)}), f32[89888]{0:T(1024)}) %all-reduce.10.cloned.1.call-update) | async-done | bytes 359568
  (146 shorter events, 70.4 us)
Async XLA Ops:
  7.2 149.6 %copy-start = (bf16[1152,1152]{1,0:T(8,128)(2,1)S(1)}, bf16[1152,1152]{1,0:T(8,128)(2,1)}, u32[]{:S(2)}) copy-start(bf16[1152,1152]{1,0:T(8,128)(2,1)} %param.25) | copy-start | bytes 7962628
  7.2 41.8 %all-gather.6.cloned.1.call-start = ((), (), s32[]{:S(2)}) async-start(), calls=%async_computation.8 | async-start | bytes 2949120 | tf_op jit(solution)/shard_map/all_gather | solution.py:298
  10.8 3.7 copy-start.16
  10.8 3.8 copy-start.3
  11.0 13.5 %copy-start.19 = (bf16[4]{0:T(256)(128)(2,1)S(1)}, bf16[4]{0:T(256)(128)(2,1)}, u32[]{:S(2)}) copy-start(bf16[4]{0:T(256)(128)(2,1)} %param.22) | copy-start | bytes 28
  11.0 13.6 %copy-start.15 = (bf16[3,3,288]{2,1,0:T(4,128)(2,1)S(1)}, bf16[3,3,288]{2,1,0:T(4,128)(2,1)}, u32[]{:S(2)}) copy-start(bf16[3,3,288]{2,1,0:T(4,128)(2,1)} %param.23) | copy-start | bytes 15556
  14.5 34.4 %copy-start.14 = (bf16[1152,4]{0,1:T(4,128)(2,1)S(1)}, bf16[1152,4]{0,1:T(4,128)(2,1)}, u32[]{:S(2)}) copy-start(bf16[1152,4]{0,1:T(4,128)(2,1)} %param.21) | copy-start | bytes 27652
  24.5 96.1 %reduce-scatter.9.cloned.1.call-start = ((), (), s32[]{:S(2)}) async-start(), calls=%async_computation.9 | async-start | bytes 5898240 | tf_op jit(solution)/shard_map/reduce_scatter | solution.py:302
  49.0 2.9 copy-start.4
  57.1 10.8 %copy-start.10 = (bf16[288,1152]{1,0:T(8,128)(2,1)S(1)}, bf16[288,1152]{1,0:T(8,128)(2,1)}, u32[]{:S(2)}) copy-start(bf16[288,1152]{1,0:T(8,128)(2,1)} %param.24) | copy-start | bytes 1990660
  72.6 84.2 %all-gather.8.cloned.1.call-start = ((), (), s32[]{:S(2)}) async-start(), calls=%async_computation.10 | async-start | bytes 2949120 | tf_op jit(solution)/shard_map/all_gather | solution.py:298
  131.4 51.6 %all-gather.10.cloned.1.call-start = ((), (), s32[]{:S(2)}) async-start(), calls=%async_computation.12 | async-start | bytes 2949120 | tf_op jit(solution)/shard_map/all_gather | solution.py:306
  133.5 113.0 %reduce-scatter.13.cloned.1.call-start = ((), (), s32[]{:S(2)}) async-start(), calls=%async_computation.13 | async-start | bytes 5898240 | tf_op jit(solution)/shard_map/reduce_scatter | solution.py:310
  198.5 98.3 %reduce-scatter.11.cloned.1.call-start = ((), (), s32[]{:S(2)}) async-start(), calls=%async_computation.11 | async-start | bytes 5898240 | tf_op jit(solution)/shard_map/reduce_scatter | solution.py:302
  208.6 39.3 %copy-start.2 = (f32[1,1024,288]{1,2,0:T(8,128)S(1)}, f32[1,1024,288]{1,2,0:T(8,128)}, u32[]{:S(2)}) copy-start(f32[1,1024,288]{1,2,0:T(8,128)} %get-tuple-element.101) | copy-start | bytes 3538948
  208.7 117.2 %all-gather.12.cloned.1.call-start = ((), (), s32[]{:S(2)}) async-start(), calls=%async_computation.14 | async-start | bytes 2949120 | tf_op jit(solution)/shard_map/all_gather | solution.py:306
  300.6 8.3 %copy-start.6 = (f32[1,1024,288]{1,2,0:T(8,128)}, f32[1,1024,288]{1,2,0:T(8,128)S(1)}, u32[]{:S(2)}) copy-start(f32[1,1024,288]{1,2,0:T(8,128)S(1)} %get-tuple-element.107) | copy-start | bytes 3538948
  301.7 98.9 %reduce-scatter.21.cloned.1.call-start = ((), (), s32[]{:S(2)}) async-start(), calls=%async_computation.18 | async-start | bytes 2985984 | tf_op jit(solution)/shard_map/reduce_scatter | solution.py:493
  308.8 2.0 copy-start.18
  308.9 164.9 %reduce-scatter.23.cloned.1.call-start = ((), (), s32[]{:S(2)}) async-start(), calls=%async_computation.19 | async-start | bytes 2985984 | tf_op jit(solution)/shard_map/reduce_scatter | solution.py:493
  318.2 7.7 copy-start.9
  318.2 11.8 %copy-start.11 = (bf16[288,1152]{1,0:T(8,128)(2,1)S(1)}, bf16[288,1152]{1,0:T(8,128)(2,1)}, u32[]{:S(2)}) copy-start(bf16[288,1152]{1,0:T(8,128)(2,1)} %param.24) | copy-start | bytes 1990660
  318.2 219.7 %reduce-scatter.19.cloned.1.call-start = ((), (), s32[]{:S(2)}) async-start(), calls=%async_computation.17 | async-start | bytes 995328 | tf_op jit(solution)/shard_map/reduce_scatter | solution.py:493
  329.9 282.1 %reduce-scatter.17.cloned.1.call-start = ((), (), s32[]{:S(2)}) async-start(), calls=%async_computation.16 | async-start | bytes 2985984 | tf_op jit(solution)/shard_map/reduce_scatter | solution.py:493
  333.7 18.3 %copy-start.5 = (bf16[1,1024,1152]{1,2,0:T(8,128)(2,1)S(1)}, bf16[1,1024,1152]{1,2,0:T(8,128)(2,1)}, u32[]{:S(2)}) copy-start(bf16[1,1024,1152]{1,2,0:T(8,128)(2,1)} %all-gather.6.cloned.1.call-done) | copy-start | bytes 7077892
  358.1 4.9 copy-start.13
  358.1 303.2 %reduce-scatter.15.cloned.1.call-start = ((), (), s32[]{:S(2)}) async-start(), calls=%async_computation.15 | async-start | bytes 5898240 | tf_op jit(solution)/shard_map/reduce_scatter | solution.py:310
  365.9 109.8 %copy-start.12 = (f32[288,16]{1,0:T(8,128)S(1)}, f32[288,16]{1,0:T(8,128)}, u32[]{:S(2)}) copy-start(f32[288,16]{1,0:T(8,128)} %get-tuple-element.23) | copy-start | bytes 55300
  365.9 385.7 %all-reduce.10.cloned.1.call-start = ((), (), s32[]{:S(2)}) async-start(), calls=%async_computation.20 | async-start | bytes 720896
  661.3 1.8 copy-start.8
  663.6 15.7 %copy-start.7 = (f32[1,1024,288]{1,2,0:T(8,128)S(1)}, f32[1,1024,288]{1,2,0:T(8,128)}, u32[]{:S(2)}) copy-start(f32[1,1024,288]{1,2,0:T(8,128)} %copy-done.6) | copy-start | bytes 3538948
  757.4 8.2 %copy-start.1 = (bf16[1152,1152]{1,0:T(8,128)(2,1)S(1)}, bf16[1152,1152]{1,0:T(8,128)(2,1)}, u32[]{:S(2)}) copy-start(bf16[1152,1152]{1,0:T(8,128)(2,1)} %param.25) | copy-start | bytes 7962628
  (3 other events, 3.9 us)
Sparse Core Ops, SparseCore 0:
  24.6 24.3 all-gather.5
  72.7 47.8 reduce-scatter.8
  131.5 25.2 all-gather.7
  158.8 24.0 all-gather.9
  198.6 47.8 reduce-scatter.12
  248.9 47.8 reduce-scatter.10
  301.8 24.0 all-gather.11
  330.0 70.4 reduce-scatter.20
  404.2 69.5 reduce-scatter.22
  477.5 60.3 reduce-scatter.18
  542.0 69.9 reduce-scatter.16
  614.4 46.8 reduce-scatter.14
  679.4 72.0 all-reduce.9

commit v3 on v2

--- a/solution.py
+++ b/solution.py
@@ -30,7 +30,6 @@
 TN = (((0,), (0,)), ((), ()))
 NT = (((1,), (1,)), ((), ()))
 NN = (((1,), (0,)), ((), ()))
-NTT = (((0,), (1,)), ((), ()))
 
 
 def mm(left, right, form):
@@ -172,7 +171,7 @@
 
 def back_kernel(
     heads, proj_ref, logit_ref, taps_ref, rec_ref, states_ref, grad_ref,
-    gproj_ref, gforget_ref, gtaps_ref, wide, gwide, cum_ref, col_ref, grec_ref, rows_ref,
+    gproj_ref, gtaps_ref, wide, gwide, cum_ref, col_ref, grec_ref, rows_ref,
 ):
     part, length = rec_ref.shape
     spans = length // SPAN
@@ -254,7 +253,8 @@
         + running_sum(rows_ref[1], SPAN, exclusive=True)
         + rows_ref[2]
     )
-    gforget_ref[...] = low(grad_log / (1.0 + jnp.exp(logit)))
+    gwide[3 * part :, :] = jnp.zeros((gwide.shape[0] - 3 * part, length), jnp.float32)
+    gwide[3 * part : 3 * part + heads, :] = (grad_log / (1.0 + jnp.exp(logit)))[:heads]
     gproj_ref[...] = low(gwide[...])
 
 
@@ -264,15 +264,14 @@
     return pl.pallas_call(
         functools.partial(back_kernel, heads),
         out_shape=(
-            jax.ShapeDtypeStruct((3 * part, length), jnp.bfloat16),
-            jax.ShapeDtypeStruct((8, length), jnp.bfloat16),
+            jax.ShapeDtypeStruct((WIDE_ROWS, length), jnp.bfloat16),
             jax.ShapeDtypeStruct((part, 16), jnp.float32),
         ),
         in_specs=[pl.BlockSpec(memory_space=pltpu.VMEM)] * 6,
-        out_specs=[pl.BlockSpec(memory_space=pltpu.VMEM)] * 3,
+        out_specs=[pl.BlockSpec(memory_space=pltpu.VMEM)] * 2,
         scratch_shapes=[
             pltpu.VMEM((3 * part, length), jnp.float32),
-            pltpu.VMEM((3 * part, length), jnp.float32),
+            pltpu.VMEM((WIDE_ROWS, length), jnp.float32),
             pltpu.VMEM((8, length), jnp.float32),
             pltpu.VMEM((length, 8), jnp.float32),
             pltpu.VMEM((part, length), jnp.float32),
@@ -283,41 +282,635 @@
     )(proj, logit, taps, rec, states, grad)
 
 
-def tanh_gelu(inputs):
-    return jax.nn.gelu(inputs, approximate=True)
-
-
-def moments(rows, model_width):
-    totals = lax.psum((jnp.sum(rows, axis=-1), jnp.sum(rows * rows, axis=-1)), "tensor")
-    mean_row = totals[0][..., None] / model_width
-    var_row = totals[1][..., None] / model_width - mean_row * mean_row
-    return (mean_row, lax.rsqrt(var_row + norm_eps))
-
-
-def share_rows(local_rows):
-    return lax.all_gather(local_rows, "tensor", axis=2, tiled=True)
-
-
-def branch_total(partial_rows):
-    return lax.psum_scatter(partial_rows, "tensor", scatter_dimension=1, tiled=True)
-
-
-def spread_grads(local_grads):
-    return lax.all_gather(local_grads, "tensor", axis=2, tiled=True)
-
-
-def input_total(partial_rows):
-    return lax.psum_scatter(partial_rows, "tensor", scatter_dimension=1, tiled=True)
-
-
-def norm_back(grad_normed, normalized, inv_std, scale_row, model_width):
-    scaled = grad_normed * (1.0 + scale_row)
-    totals = lax.psum((jnp.sum(scaled, axis=-1), jnp.sum(scaled * normalized, axis=-1)), "tensor")
-    return inv_std * (
-        scaled
-        - totals[0][..., None] / model_width
-        - normalized * totals[1][..., None] / model_width
+MESH = pl.DeviceIdType.MESH
+CHUNK = 256
+VMEM_LIMIT = 58 * 2**20
+VMEM_SPEC = pl.BlockSpec(memory_space=pltpu.VMEM)
+WIDE_ROWS = 896
+
+
+def places():
+    me = lax.axis_index("tensor")
+    across = lax.rem(me + 2, 4)
+    beside = me + 1 - 2 * lax.rem(me, 2)
+    corner = lax.rem(beside + 2, 4)
+    return me, across, beside, corner
+
+
+def greet(peers):
+    barrier = pltpu.get_barrier_semaphore()
+    for peer in peers:
+        pl.semaphore_signal(barrier, inc=1, device_id={"tensor": peer}, device_id_type=MESH)
+    pl.semaphore_wait(barrier, len(peers))
+
+
+def send(source, target, sems, at, peer):
+    copy = pltpu.make_async_remote_copy(
+        src_ref=source,
+        dst_ref=target,
+        send_sem=sems.at[0, at],
+        recv_sem=sems.at[1, at],
+        device_id={"tensor": peer},
+        device_id_type=MESH,
     )
+    copy.start()
+    return copy
+
+
+def shard(at, part):
+    return pl.ds(pl.multiple_of(at * part, 32), part)
+
+
+class Spread:
+    def __init__(self, where, buffer, sems, part):
+        self.me, self.across, self.beside, _ = where
+        self.buffer, self.sems, self.part = buffer, sems, part
+        self.far, self.near, self.on = {}, {}, {}
+
+    def view(self, owner, lanes):
+        return self.buffer.at[shard(owner, self.part), lanes]
+
+    def start(self, k, lanes, source=None):
+        block = self.view(self.me, lanes)
+        source = block if source is None else source
+        self.far[k] = send(source, block, self.sems, 3 * k, self.across)
+        self.near[k] = send(source, block, self.sems, 3 * k + 1, self.beside)
+
+    def relay(self, k, lanes):
+        self.far[k].wait_recv()
+        block = self.view(self.across, lanes)
+        self.on[k] = send(block, block, self.sems, 3 * k + 2, self.beside)
+
+    def end(self, k):
+        self.near[k].wait_recv()
+        self.on[k].wait_recv()
+
+    def finish(self):
+        for copies in (self.far, self.near, self.on):
+            for copy in copies.values():
+                copy.wait_send()
+
+
+class Reduce:
+    def __init__(self, where, part, bufs, sems):
+        self.me, self.across, self.beside, self.corner = where
+        self.part = part
+        self.pair_out, self.pair_in, self.far_out, self.far_in, self.keep = bufs
+        self.sems = sems
+        self.pair, self.far = {}, {}
+
+    def start(self, k, lanes, term):
+        for index, owner in enumerate((self.corner, self.beside)):
+            self.pair_out[index, :, lanes] = low(term(owner))
+            self.pair[k, index] = send(
+                self.pair_out.at[index, :, lanes],
+                self.pair_in.at[index, :, lanes],
+                self.sems,
+                3 * k + index,
+                self.beside,
+            )
+            self.keep[index, :, lanes] = term((self.across, self.me)[index])
+
+    def relay(self, k, lanes, remote=True):
+        self.pair[k, 0].wait_recv()
+        block = low(self.keep[0, :, lanes] + self.pair_in[0, :, lanes].astype(jnp.float32))
+        self.far_out[:, lanes] = block
+        if remote:
+            self.far[k] = send(
+                self.far_out.at[:, lanes], self.far_in.at[:, lanes], self.sems, 3 * k + 2, self.across
+            )
+
+    def near_sum(self, k, lanes):
+        self.pair[k, 1].wait_recv()
+        return self.keep[1, :, lanes] + self.pair_in[1, :, lanes].astype(jnp.float32)
+
+    def end(self, k, lanes):
+        total = self.near_sum(k, lanes)
+        self.far[k].wait_recv()
+        return total + self.far_in[:, lanes].astype(jnp.float32)
+
+    def finish(self):
+        for copies in (self.pair, self.far):
+            for copy in copies.values():
+                copy.wait_send()
+
+
+class Rows:
+    def __init__(self, where, buffer, sems):
+        self.me, self.peers = where[0], where[1:]
+        self.buffer, self.sems = buffer, sems
+        self.copies = {}
+
+    def start(self, k, lanes, first, second):
+        self.buffer[self.me, 0:1, lanes] = first
+        self.buffer[self.me, 1:2, lanes] = second
+        block = self.buffer.at[self.me, :, lanes]
+        self.copies[k] = [
+            send(block, block, self.sems, 3 * k + index, peer) for index, peer in enumerate(self.peers)
+        ]
+
+    def end(self, k, lanes):
+        for copy in self.copies[k]:
+            copy.wait_recv()
+        total = sum(self.buffer[index, :, lanes] for index in range(4))
+        return total[0:1], total[1:2]
+
+    def finish(self):
+        for copies in self.copies.values():
+            for copy in copies:
+                copy.wait_send()
+
+
+def reduce_scratch(part, length):
+    return [
+        pltpu.VMEM((2, part, length), jnp.bfloat16),
+        pltpu.VMEM((2, part, length), jnp.bfloat16),
+        pltpu.VMEM((part, length), jnp.bfloat16),
+        pltpu.VMEM((part, length), jnp.bfloat16),
+        pltpu.VMEM((2, part, length), jnp.float32),
+    ]
+
+
+def copy_sems(count):
+    return pltpu.SemaphoreType.DMA((2, count))
+
+
+def column_sums(rows):
+    return jnp.sum(rows, axis=1, keepdims=True)
+
+
+def row_sums(rows):
+    return jnp.sum(rows, axis=0, keepdims=True)
+
+
+def open_kernel(
+    x_ref, cot_ref, silu_ref, ada_ref, bias_ref, qkv_ref, gate_ref, gate_bias_ref,
+    normed_ref, proj_ref, logit_ref, stats_ref, mods_ref, gmlp_ref, wback_ref,
+    raw, rows, wide, raw_sems, row_sems,
+):
+    part, length = x_ref.shape
+    width = 4 * part
+    chunks = length // CHUNK
+    lanes = [pl.ds(k * CHUNK, CHUNK) for k in range(chunks)]
+    where = places()
+    me, _, _, _ = where
+    greet(where[1:])
+    spread = Spread(where, raw, raw_sems, part)
+    for k in range(chunks):
+        spread.start(k, lanes[k], x_ref.at[:, lanes[k]])
+    raw[shard(me, part), :] = x_ref[...]
+
+    row_at = lax.broadcasted_iota(jnp.int32, (8, part), 0)
+    mods = bias_ref[:, :part]
+    silu = silu_ref[...]
+    for index in range(6):
+        product = mm(silu, ada_ref[index * part : (index + 1) * part, :], NT)
+        mods = mods + jnp.where(row_at == index, product, 0.0)
+    rows[me] = bias_ref[...]
+    rows[me, :, :part] = mods
+    row_copies = [
+        send(rows.at[me], rows.at[me], row_sems, index, peer) for index, peer in enumerate(where[1:])
+    ]
+    own_mods = jnp.transpose(rows[me])[:part]
+    mods_ref[...] = own_mods
+    gmlp_ref[...] = low(cot_ref[...].astype(jnp.float32) * own_mods[:, 5:6])
+    projected = qkv_ref.shape[0]
+    wide[:projected, :] = qkv_ref[...]
+    wide[projected:, :] = gate_ref[...]
+    wback_ref[...] = jnp.transpose(wide[...])
+    for copy in row_copies:
+        copy.wait_recv()
+    columns = [jnp.transpose(rows[index])[:part] for index in range(4)]
+
+    def one_chunk(k):
+        spread.end(k)
+        blocks = [raw[index * part : (index + 1) * part, lanes[k]].astype(jnp.float32) for index in range(4)]
+        mean = sum(row_sums(block) for block in blocks) / width
+        square = sum(row_sums(block * block) for block in blocks) / width
+        inv_std = lax.rsqrt(square - mean * mean + norm_eps)
+        stats_ref[0:1, lanes[k]] = mean
+        stats_ref[1:2, lanes[k]] = inv_std
+        for index in range(4):
+            unit = (blocks[index] - mean) * inv_std
+            normed = unit * (1.0 + columns[index][:, 1:2]) + columns[index][:, 0:1]
+            normed_ref[index * part : (index + 1) * part, lanes[k]] = low(normed)
+        product = mm(wide[...], normed_ref[:, lanes[k]], NN)
+        proj_ref[:, lanes[k]] = low(product[:projected])
+        logit_ref[:, lanes[k]] = product[projected : projected + 8] + gate_bias_ref[...]
+
+    stats_ref[2:, :] = jnp.zeros((6, length), jnp.float32)
+    for k in range(chunks):
+        spread.relay(k, lanes[k])
+        if k > 0:
+            one_chunk(k - 1)
+    one_chunk(chunks - 1)
+    spread.finish()
+    for copy in row_copies:
+        copy.wait_send()
+
+
+def open_layer(x, cot, silu, ada, bias, qkv, gate, gate_bias):
+    part, length = x.shape
+    width = 4 * part
+    chunks = length // CHUNK
+    shape = jax.ShapeDtypeStruct
+    return pl.pallas_call(
+        open_kernel,
+        out_shape=(
+            shape((width, length), jnp.bfloat16),
+            shape((3 * part, length), jnp.bfloat16),
+            shape((8, length), jnp.float32),
+            shape((8, length), jnp.float32),
+            shape((part, 8), jnp.float32),
+            shape((part, length), jnp.bfloat16),
+            shape((width, WIDE_ROWS), jnp.bfloat16),
+        ),
+        in_specs=[VMEM_SPEC] * 8,
+        out_specs=[VMEM_SPEC] * 7,
+        scratch_shapes=[
+            pltpu.VMEM((width, length), jnp.bfloat16),
+            pltpu.VMEM((4, 8, bias.shape[1]), jnp.float32),
+            pltpu.VMEM((WIDE_ROWS, width), jnp.bfloat16),
+            copy_sems(3 * chunks),
+            copy_sems(3),
+        ],
+        compiler_params=pltpu.CompilerParams(
+            collective_id=1, has_side_effects=True, vmem_limit_bytes=VMEM_LIMIT
+        ),
+        name="open_layer",
+    )(x, cot, silu, ada, bias, qkv, gate, gate_bias)
+
+
+GELU_SLOPE = math.sqrt(2.0 / math.pi)
+GELU_CUBE = 0.044715
+
+
+def middle_kernel(
+    mix_ref, x_ref, mods_ref, gmlp_ref, gmlp_far_ref, cot_ref, out_w_ref, up_ref, down_ref,
+    attn_ref, after_ref, mlp_keep_ref, mlp_send_ref, gafter_ref, gattn_ref, gmix_ref, gup_ref, gdown_ref,
+    gout_ref, sums_ref,
+    out_t, turned, gmlp, gact, normed, act, gup_rows, unit,
+    a_pair_out, a_pair_in, a_far_out, a_far_in, a_keep,
+    g_pair_out, g_pair_in, g_far_out, g_far_in, g_keep,
+    first_rows, second_rows,
+    gm_sems, a_sems, n_sems, g_sems, t_sems, m_sems, first_sems, second_sems,
+):
+    part, length = x_ref.shape
+    width = 4 * part
+    hidden = up_ref.shape[1]
+    chunks = length // CHUNK
+    lanes = [pl.ds(k * CHUNK, CHUNK) for k in range(chunks)]
+    where = places()
+    me, across, beside, _ = where
+    first_rows[...] = jnp.zeros_like(first_rows)
+    second_rows[...] = jnp.zeros_like(second_rows)
+    greet(where[1:])
+    own, other = shard(me, part), shard(across, part)
+    gm_copies = [
+        send(gmlp_ref, gmlp.at[own, :], gm_sems, 0, beside),
+        send(gmlp_far_ref, gmlp.at[other, :], gm_sems, 1, beside),
+    ]
+    gmlp[own, :] = gmlp_ref[...]
+    gmlp[other, :] = gmlp_far_ref[...]
+    gate_one, scale_two, shift_two = mods_ref[:, 2:3], mods_ref[:, 4:5], mods_ref[:, 3:4]
+
+    attn_sum = Reduce(where, part, (a_pair_out, a_pair_in, a_far_out, a_far_in, a_keep), a_sems)
+    grad_sum = Reduce(where, part, (g_pair_out, g_pair_in, g_far_out, g_far_in, g_keep), g_sems)
+    norm_spread = Spread(where, normed, n_sems, part)
+    grad_spread = Spread(where, gattn_ref, t_sems, part)
+    moments = Rows(where, first_rows, first_sems)
+    means = Rows(where, second_rows, second_sems)
+
+    out_t[...] = jnp.transpose(out_w_ref[...])
+    sums_ref[...] = jnp.zeros_like(sums_ref)
+
+    def attn_start(k):
+        mixed = mix_ref[:, lanes[k]]
+        attn_sum.start(k, lanes[k], lambda owner: mm(out_t[shard(owner, part), :], mixed, NN))
+
+    def attn_end(k):
+        attn = attn_sum.end(k, lanes[k])
+        attn_ref[:, lanes[k]] = attn
+        after = x_ref[:, lanes[k]].astype(jnp.float32) + gate_one * attn
+        after_ref[:, lanes[k]] = after
+        moments.start(k, lanes[k], row_sums(after), row_sums(after * after))
+
+    inverse = [None] * chunks
+
+    def norm_chunk(k):
+        total, squares = moments.end(k, lanes[k])
+        mean = total / width
+        inverse[k] = lax.rsqrt(squares / width - mean * mean + norm_eps)
+        rows = (after_ref[:, lanes[k]] - mean) * inverse[k]
+        unit[:, lanes[k]] = rows
+        normed[own, lanes[k]] = low(rows * (1.0 + scale_two) + shift_two)
+        norm_spread.start(k, lanes[k])
+
+    def grad_act_chunk(k):
+        gact[:, lanes[k]] = mm(down_ref[...], gmlp[:, lanes[k]], NN)
+
+    def hidden_chunk(k):
+        norm_spread.end(k)
+        block = normed[:, lanes[k]]
+
+        def one_block(at, carry):
+            rows = pl.ds(pl.multiple_of(at * part, 32), part)
+            up = mm(turned[rows, :], block, NN)
+            square = up * up
+            bend = jnp.tanh(GELU_SLOPE * up * (1.0 + GELU_CUBE * square))
+            half = 0.5 * (1.0 + bend)
+            act[rows, lanes[k]] = low(up * half)
+            slope = half + 0.5 * up * (1.0 - bend * bend) * GELU_SLOPE * (1.0 + 3.0 * GELU_CUBE * square)
+            gup_rows[rows, lanes[k]] = low(gact[rows, lanes[k]] * slope)
+            return carry
+
+        lax.fori_loop(0, hidden // part, one_block, 0)
+
+    def grad_start(k):
+        block = gup_rows[:, lanes[k]]
+        grad_sum.start(k, lanes[k], lambda owner: mm(up_ref[shard(owner, part), :], block, NN))
+
+    def grad_end(k):
+        grad = grad_sum.end(k, lanes[k])
+        rows = unit[:, lanes[k]]
+        sums_ref[:, 3:4] += column_sums(grad)
+        sums_ref[:, 4:5] += column_sums(grad * rows)
+        scaled = grad * (1.0 + scale_two)
+        gafter_ref[:, lanes[k]] = scaled
+        means.start(k, lanes[k], row_sums(scaled), row_sums(scaled * rows))
+
+    def after_chunk(k):
+        total, along = means.end(k, lanes[k])
+        scaled = gafter_ref[:, lanes[k]]
+        back = inverse[k] * (scaled - total / width - unit[:, lanes[k]] * (along / width))
+        grad = cot_ref[:, lanes[k]].astype(jnp.float32) + back
+        gafter_ref[:, lanes[k]] = grad
+        gattn_ref[own, lanes[k]] = low(grad * gate_one)
+        grad_spread.start(k, lanes[k])
+        sums_ref[:, 2:3] += column_sums(grad * attn_ref[:, lanes[k]])
+
+    def mixed_chunk(k):
+        grad_spread.end(k)
+        gmix_ref[:, lanes[k]] = mm(out_w_ref[...], gattn_ref[:, lanes[k]], NN)
+
+    def weight_grad(target, left, right, half):
+        rows = target.shape[0] // 2
+        target[half * rows : (half + 1) * rows, :] = low(mm(left[half * rows : (half + 1) * rows, :], right[...], NT))
+
+    mlp_sum = Reduce(where, part, (a_pair_out, a_pair_in, mlp_send_ref, None, a_keep), m_sems)
+
+    def mlp_start(k):
+        block = act[:, lanes[k]]
+        mlp_sum.start(k, lanes[k], lambda owner: mm(turned[shard(owner, part), :], block, NN))
+
+    def mlp_end(k):
+        mlp_sum.relay(k, lanes[k], remote=False)
+        mlp_keep_ref[:, lanes[k]] = mlp_sum.near_sum(k, lanes[k])
+
+    attn_start(0)
+    attn_start(1)
+    attn_sum.relay(0, lanes[0])
+    attn_start(2)
+    attn_sum.relay(1, lanes[1])
+    attn_start(3)
+    attn_sum.relay(2, lanes[2])
+    turned[...] = jnp.transpose(up_ref[...])
+    attn_sum.relay(3, lanes[3])
+    attn_end(0)
+    for copy in gm_copies:
+        copy.wait_recv()
+    grad_act_chunk(0)
+    attn_end(1)
+    norm_chunk(0)
+    grad_act_chunk(1)
+    attn_end(2)
+    norm_chunk(1)
+    grad_act_chunk(2)
+    attn_end(3)
+    norm_chunk(2)
+    norm_spread.relay(0, lanes[0])
+    grad_act_chunk(3)
+    norm_chunk(3)
+    norm_spread.relay(1, lanes[1])
+    hidden_chunk(0)
+    grad_start(0)
+    norm_spread.relay(2, lanes[2])
+    hidden_chunk(1)
+    grad_sum.relay(0, lanes[0])
+    grad_start(1)
+    norm_spread.relay(3, lanes[3])
+    hidden_chunk(2)
+    grad_sum.relay(1, lanes[1])
+    grad_start(2)
+    grad_end(0)
+    hidden_chunk(3)
+    grad_sum.relay(2, lanes[2])
+    after_chunk(0)
+    grad_start(3)
+    grad_end(1)
+    grad_sum.relay(3, lanes[3])
+    after_chunk(1)
+    grad_end(2)
+    weight_grad(gdown_ref, gmlp, act, 0)
+    grad_spread.relay(0, lanes[0])
+    after_chunk(2)
+    grad_end(3)
+    weight_grad(gdown_ref, gmlp, act, 1)
+    after_chunk(3)
+    grad_spread.relay(1, lanes[1])
+    mixed_chunk(0)
+    attn_sum.finish()
+    turned[...] = jnp.transpose(down_ref[...])
+    weight_grad(gup_ref, normed, gup_rows, 0)
+    grad_spread.relay(2, lanes[2])
+    mixed_chunk(1)
+    weight_grad(gup_ref, normed, gup_rows, 1)
+    grad_spread.relay(3, lanes[3])
+    mixed_chunk(2)
+    mlp_start(0)
+    mlp_start(1)
+    mlp_end(0)
+    mixed_chunk(3)
+    mlp_start(2)
+    mlp_end(1)
+    mlp_start(3)
+    mlp_end(2)
+    gout_ref[...] = low(mm(gattn_ref[...], mix_ref[...], NT))
+    mlp_end(3)
+    for copy in gm_copies:
+        copy.wait_send()
+    for group in (norm_spread, grad_spread, grad_sum, mlp_sum, moments, means):
+        group.finish()
+
+
+def middle_layer(mix, x, mods, gmlp, gmlp_far, cot, out_w, up, down):
+    part, length = x.shape
+    width = 4 * part
+    hidden = up.shape[1]
+    chunks = length // CHUNK
+    shape = jax.ShapeDtypeStruct
+    return pl.pallas_call(
+        middle_kernel,
+        out_shape=(
+            shape((part, length), jnp.float32),
+            shape((part, length), jnp.float32),
+            shape((part, length), jnp.float32),
+            shape((part, length), jnp.bfloat16),
+            shape((part, length), jnp.float32),
+            shape((width, length), jnp.bfloat16),
+            shape((part, length), jnp.float32),
+            shape((width, hidden), jnp.bfloat16),
+            shape((width, hidden), jnp.bfloat16),
+            shape((width, part), jnp.bfloat16),
+            shape((part, 8), jnp.float32),
+        ),
+        in_specs=[VMEM_SPEC] * 9,
+        out_specs=[VMEM_SPEC] * 11,
+        scratch_shapes=[
+            pltpu.VMEM((width, part), jnp.bfloat16),
+            pltpu.VMEM((hidden, width), jnp.bfloat16),
+            pltpu.VMEM((width, length), jnp.bfloat16),
+            pltpu.VMEM((hidden, length), jnp.float32),
+            pltpu.VMEM((width, length), jnp.bfloat16),
+            pltpu.VMEM((hidden, length), jnp.bfloat16),
+            pltpu.VMEM((hidden, length), jnp.bfloat16),
+            pltpu.VMEM((part, length), jnp.float32),
+            *reduce_scratch(part, length),
+            *reduce_scratch(part, length),
+            pltpu.VMEM((4, 8, length), jnp.float32),
+            pltpu.VMEM((4, 8, length), jnp.float32),
+            copy_sems(2),
+            *[copy_sems(3 * chunks)] * 7,
+        ],
+        compiler_params=pltpu.CompilerParams(
+            collective_id=2, has_side_effects=True, vmem_limit_bytes=VMEM_LIMIT
+        ),
+        name="middle_layer",
+    )(mix, x, mods, gmlp, gmlp_far, cot, out_w, up, down)
+
+
+def close_kernel(
+    gproj_ref, wback_ref, normed_ref, x_ref, stats_ref, mods_ref, gafter_ref, after_ref, cot_ref,
+    mlp_keep_ref, mlp_far_ref, sums_ref,
+    gtokens_ref, out_ref, gqkv_ref, gmods_ref,
+    pair_out, pair_in, far_out, far_in, keep, mean_rows, sum_sems, mean_sems,
+):
+    part, length = x_ref.shape
+    width = 4 * part
+    chunks = length // CHUNK
+    lanes = [pl.ds(k * CHUNK, CHUNK) for k in range(chunks)]
+    where = places()
+    mean_rows[...] = jnp.zeros_like(mean_rows)
+    greet(where[1:])
+    total_sum = Reduce(where, part, (pair_out, pair_in, far_out, far_in, keep), sum_sems)
+    means = Rows(where, mean_rows, mean_sems)
+    scale_one, gate_two = mods_ref[:, 1:2], mods_ref[:, 5:6]
+    gmods_ref[...] = sums_ref[...]
+
+    def start(k):
+        block = gproj_ref[:, lanes[k]]
+        total_sum.start(k, lanes[k], lambda owner: mm(wback_ref[shard(owner, part), :], block, NN))
+
+    def unit_of(k):
+        return (x_ref[:, lanes[k]].astype(jnp.float32) - stats_ref[0:1, lanes[k]]) * stats_ref[1:2, lanes[k]]
+
+    def end(k):
+        grad = total_sum.end(k, lanes[k])
+        unit = unit_of(k)
+        gmods_ref[:, 0:1] += column_sums(grad)
+        gmods_ref[:, 1:2] += column_sums(grad * unit)
+        scaled = grad * (1.0 + scale_one)
+        gtokens_ref[:, lanes[k]] = scaled
+        means.start(k, lanes[k], row_sums(scaled), row_sums(scaled * unit))
+
+    def tokens(k):
+        total, along = means.end(k, lanes[k])
+        back = gtokens_ref[:, lanes[k]] - total / width - unit_of(k) * (along / width)
+        gtokens_ref[:, lanes[k]] = gafter_ref[:, lanes[k]] + stats_ref[1:2, lanes[k]] * back
+
+    def outputs(k):
+        mlp = mlp_keep_ref[:, lanes[k]] + mlp_far_ref[:, lanes[k]].astype(jnp.float32)
+        out_ref[:, lanes[k]] = low(after_ref[:, lanes[k]] + gate_two * mlp)
+        gmods_ref[:, 5:6] += column_sums(cot_ref[:, lanes[k]].astype(jnp.float32) * mlp)
+
+    def weight_grad(quarter):
+        rows = pl.ds(quarter * part, part)
+        gqkv_ref[rows, :] = low(mm(normed_ref[rows, :], gproj_ref[...], NT))
+
+    start(0)
+    start(1)
+    total_sum.relay(0, lanes[0])
+    start(2)
+    total_sum.relay(1, lanes[1])
+    start(3)
+    total_sum.relay(2, lanes[2])
+    outputs(0)
+    total_sum.relay(3, lanes[3])
+    for k in range(chunks):
+        if k > 0:
+            outputs(k)
+        weight_grad(k)
+        end(k)
+        if k > 0:
+            tokens(k - 1)
+    tokens(chunks - 1)
+    total_sum.finish()
+    means.finish()
+
+
+def close_layer(gproj, wback, normed, x, stats, mods, gafter, after, cot, mlp_keep, mlp_far, sums):
+    part, length = x.shape
+    width = 4 * part
+    chunks = length // CHUNK
+    shape = jax.ShapeDtypeStruct
+    return pl.pallas_call(
+        close_kernel,
+        out_shape=(
+            shape((part, length), jnp.float32),
+            shape((part, length), jnp.bfloat16),
+            shape((width, WIDE_ROWS), jnp.bfloat16),
+            shape((part, 8), jnp.float32),
+        ),
+        in_specs=[VMEM_SPEC] * 12,
+        out_specs=[VMEM_SPEC] * 4,
+        scratch_shapes=[
+            *reduce_scratch(part, length),
+            pltpu.VMEM((4, 8, length), jnp.float32),
+            copy_sems(3 * chunks),
+            copy_sems(3 * chunks),
+        ],
+        compiler_params=pltpu.CompilerParams(
+            collective_id=3, has_side_effects=True, vmem_limit_bytes=VMEM_LIMIT
+        ),
+        name="close_layer",
+    )(gproj, wback, normed, x, stats, mods, gafter, after, cot, mlp_keep, mlp_far, sums)
+
+
+def dp_total(partial, shard_count):
+    rows, columns = partial.shape
+    own = rows // shard_count
+    spots = shard_count // 2
+    at = lax.axis_index("dp")
+    spot, side = at // 2, lax.rem(at, 2)
+    blocks = partial.reshape(spots, 2, own, columns)
+    outgoing = lax.dynamic_index_in_dim(blocks, 1 - side, axis=1, keepdims=False)
+    kept = lax.dynamic_index_in_dim(blocks, side, axis=1, keepdims=False)
+    arrived = lax.ppermute(outgoing, "dp", [(index, index ^ 1) for index in range(shard_count)])
+    half = low(kept.astype(jnp.float32) + arrived.astype(jnp.float32))
+    if spots > 4:
+        groups = [[2 * index + bit for index in range(spots)] for bit in range(2)]
+        total = lax.psum_scatter(
+            half.reshape(spots * own, columns), "dp", scatter_dimension=0, axis_index_groups=groups, tiled=True
+        )
+        return total.astype(jnp.float32)
+    total = lax.dynamic_index_in_dim(half, spot, axis=0, keepdims=False).astype(jnp.float32)
+    for step in range(1, spots):
+        block = lax.dynamic_index_in_dim(half, lax.rem(spot + step, spots), axis=0, keepdims=False)
+        moved = lax.ppermute(
+            block, "dp", [(index, (index + 2 * step) % shard_count) for index in range(shard_count)]
+        )
+        total = total + moved.astype(jnp.float32)
+    return total
 
 
 def shards(
@@ -336,181 +929,99 @@
     down_weight,
     cotangent,
 ):
-    latents, length, part_width = latent_tokens.shape
-    row_count = latents * length
-    heads_here = gate_weight.shape[1]
-    onehot = labels[:, None] == jnp.arange(NCLASS, dtype=jnp.int32)[None, :]
-    cond = jnp.dot(
-        onehot.astype(jnp.bfloat16), class_table, preferred_element_type=jnp.float32
-    ) + embed_time(timesteps, MODEL_DIM)
-    silu_value, silu_pull = jax.vjp(jax.nn.silu, cond)
-    silu_cond = silu_value.astype(jnp.bfloat16)
-    ada_flat = ada_weight.reshape(MODEL_DIM, 6 * part_width)
-    mods = (
-        jnp.dot(silu_cond, ada_flat, preferred_element_type=jnp.float32).reshape(
-            latents, 6, part_width
-        )
-        + ada_bias.astype(jnp.float32)[None]
-    )
-    shift_one = mods[:, 0:1]
-    scale_one = mods[:, 1:2]
-    gate_one = mods[:, 2:3]
-    shift_two = mods[:, 3:4]
-    scale_two = mods[:, 4:5]
-    gate_two = mods[:, 5:6]
-    tokens_value = latent_tokens.astype(jnp.float32)
-    mean_one, std_inv_one = moments(tokens_value, MODEL_DIM)
-    unit_one = (tokens_value - mean_one) * std_inv_one
-    first_normalized = share_rows((unit_one * (1.0 + scale_one) + shift_one).astype(jnp.bfloat16))
-    rows_one = first_normalized.reshape(row_count, MODEL_DIM)
-    qkv_flat = query_key_value_weight.reshape(MODEL_DIM, 3 * part_width)
-    projected = low(mm(qkv_flat, rows_one, NTT))
-    forget_logit = mm(gate_weight, rows_one, NTT) + gate_bias.astype(jnp.float32)[:, None]
-    forget_logit = jnp.pad(forget_logit, ((0, 8 - heads_here), (0, 0)))
-    taps = jnp.pad(conv_weight.astype(jnp.float32).reshape(9, part_width).T, ((0, 0), (0, 7)))
-    mixed_low, recurrent, states = mixer(projected, forget_logit, taps, heads_here)
-    attn_out = branch_total(
-        mm(mixed_low, out_weight, TN)
-    ).reshape(latents, length, part_width)
-    after_attn = tokens_value + gate_one * attn_out
-    mean_two, std_inv_two = moments(after_attn, MODEL_DIM)
-    unit_two = (after_attn - mean_two) * std_inv_two
-    normed_two = share_rows((unit_two * (1.0 + scale_two) + shift_two).astype(jnp.bfloat16))
-    rows_two = normed_two.reshape(row_count, MODEL_DIM)
-    up_rows = jnp.dot(rows_two, up_weight, preferred_element_type=jnp.float32)
-    act_rows, gelu_pull = jax.vjp(tanh_gelu, up_rows)
-    act_low = act_rows.astype(jnp.bfloat16)
-    mlp_out = branch_total(
-        jnp.dot(act_low, down_weight, preferred_element_type=jnp.float32)
-    ).reshape(latents, length, part_width)
-    layer_out = (after_attn + gate_two * mlp_out).astype(jnp.bfloat16)
-    grad_result = cotangent.astype(jnp.float32)
-    grad_gate_two = jnp.sum(grad_result * mlp_out, axis=1)
-    grad_mlp = spread_grads((grad_result * gate_two).astype(jnp.bfloat16)).reshape(
-        row_count, MODEL_DIM
-    )
-    grad_down = jnp.einsum("rf,rd->fd", act_low, grad_mlp, preferred_element_type=jnp.float32)
-    grad_act = jnp.einsum("rd,fd->rf", grad_mlp, down_weight, preferred_element_type=jnp.float32)
-    grad_up_rows = gelu_pull(grad_act)[0].astype(jnp.bfloat16)
-    grad_up = jnp.einsum("rd,rf->df", rows_two, grad_up_rows, preferred_element_type=jnp.float32)
-    grad_normed_two = input_total(
-        jnp.einsum("rf,df->rd", grad_up_rows, up_weight, preferred_element_type=jnp.float32)
-    ).reshape(latents, length, part_width)
-    grad_shift_two = jnp.sum(grad_normed_two, axis=1)
-    grad_scale_two = jnp.sum(grad_normed_two * unit_two, axis=1)
-    grad_after = grad_result + norm_back(
-        grad_normed_two, unit_two, std_inv_two, scale_two, MODEL_DIM
-    )
-    grad_gate_one = jnp.sum(grad_after * attn_out, axis=1)
-    grad_attn = spread_grads((grad_after * gate_one).astype(jnp.bfloat16)).reshape(
-        row_count, MODEL_DIM
-    )
-    grad_out_w = mm(mixed_low, grad_attn, NN)
-    grad_mixed = mm(out_weight, grad_attn, NT)
-    grad_projected, grad_forget, grad_taps = mixer_back(
-        projected, forget_logit, taps, recurrent, states, grad_mixed, heads_here
-    )
-    grad_forget = grad_forget[:heads_here]
-    grad_conv = grad_taps[:, :9].T
-    grad_qkv = mm(rows_one, grad_projected, NTT).reshape(MODEL_DIM, 3, part_width)
-    grad_gate_w = mm(rows_one, grad_forget, NTT)
-    grad_gate_b = jnp.sum(grad_forget.astype(jnp.float32), axis=1)
-    grad_normed_one = input_total(
-        mm(grad_projected, qkv_flat, NTT) + mm(grad_forget, gate_weight, NTT)
-    ).reshape(latents, length, part_width)
-    grad_shift_one = jnp.sum(grad_normed_one, axis=1)
-    grad_scale_one = jnp.sum(grad_normed_one * unit_one, axis=1)
-    grad_tokens = grad_after + norm_back(
-        grad_normed_one, unit_one, std_inv_one, scale_one, MODEL_DIM
-    )
-    grad_mods = jnp.stack(
-        [
-            grad_shift_one,
-            grad_scale_one,
-            grad_gate_one,
-            grad_shift_two,
-            grad_scale_two,
-            grad_gate_two,
-        ],
-        axis=1,
-    ).astype(jnp.bfloat16)
-    mods_flat = grad_mods.reshape(latents, 6 * part_width)
-    grad_silu = jnp.einsum("bc,dc->bd", mods_flat, ada_flat, preferred_element_type=jnp.float32)
+    _, length, part = latent_tokens.shape
+    heads = gate_weight.shape[1]
+    hidden = up_weight.shape[1]
     shard_count = lax.psum(1, "dp")
     shard_at = lax.axis_index("dp")
     own_width = MODEL_DIM // shard_count
+    x = latent_tokens[0].T
+    cot = cotangent[0].T
+    qkv = jnp.transpose(query_key_value_weight, (1, 2, 0)).reshape(3 * part, MODEL_DIM)
+    ada = jnp.transpose(ada_weight, (1, 2, 0)).reshape(6 * part, MODEL_DIM)
+    gate = jnp.pad(gate_weight.T, ((0, WIDE_ROWS - 3 * part - heads), (0, 0)))
+    gate_column = jnp.pad(gate_bias.astype(jnp.float32), (0, 8 - heads))[:, None]
+    bias_rows = jnp.pad(ada_bias.astype(jnp.float32), ((0, 2), (0, -part % 128)))
+    taps = jnp.pad(conv_weight.astype(jnp.float32).reshape(9, part).T, ((0, 0), (0, 7)))
+
+    cond = lax.dynamic_slice_in_dim(class_table, labels[0], 1, axis=0).astype(jnp.float32) + embed_time(
+        timesteps, MODEL_DIM
+    )
+    silu_cond = low(jax.nn.silu(cond))
+    normed_one, projected, forget_logit, stats, mods, grad_mlp, wide_back = open_layer(
+        x, cot, jnp.broadcast_to(silu_cond, (8, MODEL_DIM)), ada, bias_rows, qkv, gate, gate_column
+    )
+    swap_chips = [(0, 2), (1, 3), (2, 0), (3, 1)]
+    grad_mlp_far = lax.ppermute(grad_mlp, "tensor", swap_chips)
+    mixed_low, recurrent, states = mixer(projected, forget_logit, taps, heads)
+    (
+        _,
+        after_attn,
+        mlp_keep,
+        mlp_send,
+        grad_after,
+        _,
+        grad_mixed,
+        grad_up,
+        grad_down,
+        grad_out_w,
+        sums_two,
+    ) = middle_layer(mixed_low, x, mods, grad_mlp, grad_mlp_far, cot, out_weight, up_weight, down_weight)
+    mlp_far = lax.ppermute(mlp_send, "tensor", swap_chips)
+    grad_down = dp_total(grad_down, shard_count)
+    grad_up = dp_total(grad_up, shard_count)
+    grad_out_w = dp_total(grad_out_w, shard_count)
+    grad_projected, grad_taps = mixer_back(projected, forget_logit, taps, recurrent, states, grad_mixed, heads)
+    grad_tokens, layer_out, grad_wide, grad_mod_columns = close_layer(
+        grad_projected, wide_back, normed_one, x, stats, mods, grad_after, after_attn, cot, mlp_keep, mlp_far, sums_two
+    )
+    grad_wide = dp_total(grad_wide, shard_count)
+
+    grad_mods = low(grad_mod_columns.T[:6])
+    mods_flat = grad_mods.reshape(1, 6 * part)
+    grad_silu = mm(mods_flat, ada, NN)
+    grad_gate_b = jnp.sum(grad_projected[3 * part : 3 * part + heads].astype(jnp.float32), axis=1)
     small = jnp.concatenate(
         [
-            mods_flat.astype(jnp.float32).reshape(latents * 6 * part_width),
-            lax.psum(grad_silu, "tensor").reshape(latents * MODEL_DIM),
-            cond.reshape(latents * MODEL_DIM),
-            grad_gate_w.reshape(MODEL_DIM * heads_here),
+            mods_flat.astype(jnp.float32).reshape(6 * part),
+            lax.psum(grad_silu, "tensor").reshape(MODEL_DIM),
+            cond.reshape(MODEL_DIM),
             grad_gate_b,
-            grad_conv.reshape(9 * part_width),
+            grad_taps[:, :9].T.reshape(9 * part),
         ]
     )
     every = lax.all_gather(small, "dp", axis=0, tiled=False)
     every_labels = lax.all_gather(labels, "dp", axis=0, tiled=True)
-    all_latents = every_labels.shape[0]
-    sizes = [
-        latents * 6 * part_width,
-        latents * MODEL_DIM,
-        latents * MODEL_DIM,
-        MODEL_DIM * heads_here,
-        heads_here,
-        9 * part_width,
-    ]
+    sizes = [6 * part, MODEL_DIM, MODEL_DIM, heads, 9 * part]
     starts = [sum(sizes[:index]) for index in range(len(sizes) + 1)]
-    every_mods, every_silu, every_cond, every_gate_w, every_gate_b, every_conv = (
-        every[:, low:high] for low, high in zip(starts[:-1], starts[1:])
+    every_mods, every_silu, every_cond, every_gate_b, every_conv = (
+        every[:, begin:end] for begin, end in zip(starts[:-1], starts[1:])
     )
-    every_mods = every_mods.reshape(all_latents, 6 * part_width)
-    grad_ada_b = jnp.sum(every_mods, axis=0).reshape(6, part_width)
+    grad_ada_b = jnp.sum(every_mods, axis=0).reshape(6, part)
     grad_gate_b = jnp.sum(every_gate_b, axis=0)
-    grad_conv = jnp.sum(every_conv, axis=0).reshape(3, 3, part_width)
+    grad_conv = jnp.sum(every_conv, axis=0).reshape(3, 3, part)
 
     def own_columns(rows):
-        rows = rows.reshape(all_latents, MODEL_DIM)
         return lax.dynamic_slice_in_dim(rows, shard_at * own_width, own_width, axis=1)
 
     own_silu, own_pull = jax.vjp(jax.nn.silu, own_columns(every_cond))
     own_cond = own_pull(own_columns(every_silu))[0]
-    grad_ada_w = jnp.einsum(
-        "bd,bc->dc",
-        own_silu.astype(jnp.bfloat16),
-        every_mods.astype(jnp.bfloat16),
-        preferred_element_type=jnp.float32,
-    ).reshape(own_width, 6, part_width)
+    grad_ada_w = mm(low(own_silu), low(every_mods), TN).reshape(own_width, 6, part)
     every_onehot = every_labels[:, None] == jnp.arange(NCLASS, dtype=jnp.int32)[None, :]
     grad_class = jnp.dot(every_onehot.astype(jnp.float32).T, own_cond, precision=TOP_PRECISION)
-    own_gate_w = lax.dynamic_slice_in_dim(
-        every_gate_w.reshape(shard_count, MODEL_DIM, heads_here), shard_at * own_width, own_width, axis=1
-    )
-    grad_gate_w = jnp.sum(own_gate_w, axis=0)
-
-    def dp_total(partial, axis):
-        low = partial.astype(jnp.bfloat16)
-        return lax.psum_scatter(low, "dp", scatter_dimension=axis, tiled=True).astype(jnp.float32)
-
-    grad_qkv, grad_out_w, grad_up, grad_down = (
-        dp_total(grad_qkv, 0),
-        dp_total(grad_out_w, 1),
-        dp_total(grad_up, 0),
-        dp_total(grad_down, 1),
-    )
     return (
-        layer_out,
-        grad_tokens,
+        layer_out.T[None],
+        grad_tokens.T[None],
         grad_class,
         grad_ada_w,
         grad_ada_b,
-        grad_qkv,
-        grad_gate_w,
+        grad_wide[:, : 3 * part].reshape(own_width, 3, part),
+        grad_wide[:, 3 * part : 3 * part + heads],
         grad_gate_b,
         grad_conv,
-        grad_out_w,
+        grad_out_w.T,
         grad_up,
-        grad_down,
+        grad_down.T,
     )
 
 

time: 779 us -> 420 us (0.54)
  waiting for transfers between devices: 542 us -> 108 us
  Pallas kernels: 29.1 us -> 179 us
  matrix products: 89.7 us -> 4.69 us
  starting transfers between devices: 1.33 us -> 49.5 us
  blocking collectives: 42 us -> 18.9 us
  other arithmetic: 29.7 us -> 15.1 us
    reduce_scatter x8 -> x0, waiting for transfers between devices: 398 us -> none  [the longest x4 223 us: dp_total(): lax.psum_scatter(low, 'dp', scatter_dimension=axis, tiled=True)]
    pallas_call x0 -> x3, Pallas kernels: none -> 150 us  [the longest x1 87.3 us: middle_layer(): pl.pallas_call(middle_kernel, out_shape=(shape((part, length), jnp.float3...]
    all_gather x4 -> x0, waiting for transfers between devices: 72.7 us -> none  [the longest x2 46.6 us: share_rows(): return lax.all_gather(local_rows, 'tensor', axis=2, tiled=True)]
    dot_general x10 -> x0, matrix products: 53.1 us -> none  [the longest x1 9.17 us: shards(): jnp.einsum('rd,fd->rf', grad_mlp, down_weight, preferred_element_type=jnp...]
    ppermute x0 -> x18, starting transfers between devices: none -> 49.4 us  [the longest x12 42 us: dp_total(): lax.ppermute(block, 'dp', [(index, (index + 2 * step) % shard_count) for...]
    ppermute x0 -> x18, waiting for transfers between devices: none -> 40.3 us  [the longest x12 35.2 us: dp_total(): lax.ppermute(block, 'dp', [(index, (index + 2 * step) % shard_count) for...]
    dot_general x9 -> x2, matrix products: 35.2 us -> 3.35 us  [mm(): lax.dot_general(left, right, form, preferred_element_type=jnp.float32)]
    psum x4 -> x1, blocking collectives: 30.6 us -> 6.63 us  [shards(): lax.psum(grad_silu, 'tensor').reshape(MODEL_DIM)]
  transfers between devices with their start and end apart: 13 -> 19, of which waited for: 13 -> 6; matrix products, arithmetic and copies ran while one was open for 9% -> 7% of each run, Pallas kernels for 2% -> 14%
where the time goes in v3:
time: 420 us; the launch traced here: 415 us
  Pallas kernels  179 us (43%)
  waiting for transfers between devices  108 us (26%)
  starting transfers between devices  49.5 us (12%)
  local copies, waits for them, and re-layouts  22.7 us (5%)
  blocking collectives  18.9 us (4%)
  between operations  16.5 us (4%)
  other arithmetic  15.1 us (4%)
  matrix products  4.69 us (1%)
    pallas_call x1, Pallas kernels, middle_layer(): pl.pallas_call(middle_kernel, out_shape=(shape((part, length), jnp.float3...  87.3 us
    unnamed x2, waiting for transfers between devices  67.8 us
    ppermute x12, starting transfers between devices, dp_total(): lax.ppermute(block, 'dp', [(index, (index + 2 * step) % shard_count) for...  42 us
    ppermute x12, waiting for transfers between devices, dp_total(): lax.ppermute(block, 'dp', [(index, (index + 2 * step) % shard_count) for...  35.2 us
    pallas_call x1, Pallas kernels, open_layer(): pl.pallas_call(open_kernel, out_shape=(shape((width, length), jnp.bfloat1...  32 us
    pallas_call x1, Pallas kernels, close_layer(): pl.pallas_call(close_kernel, out_shape=(shape((part, length), jnp.float32...  30.8 us
    pallas_call x1, Pallas kernels, mixer_back(): pl.pallas_call(functools.partial(back_kernel, heads), out_shape=(jax.Shap...  18.3 us
    unnamed x1, blocking collectives  12.3 us
  transfers between devices with their start and end apart: 19, of which 6 were waited for; matrix products, arithmetic and copies ran while one was open for 7% of the time, Pallas kernels for 14%

profile of v3, /device:TPU:0, one launch (start us, length us, event | category | flops | bytes accessed | tf_op | source)
XLA Modules:
  0.0 414.6 jit_solution(115666432285327927)
XLA Ops:
  8.6 1.4 fusion.38
  10.1 1.3 pad_convert_fusion.1.bias_ref
  12.7 1.3 pad.23.gate_ref
  14.7 32.0 %open_layer.1 = (bf16[1152,1024]{1,0:T(8,128)(2,1)}, bf16[864,1024]{1,0:T(8,128)(2,1)}, f32[8,1024]{1,0:T(8,128)}, f32[8,1024]{1,0:T(8,128)}, f32[288,8]{1,0:T(8...) custom-call(bf16[288,1024]{1,0:T(8,128)(2,1)} %bitcast.115, bf16[288,1024]{1,0:T(8,128)(2,1)} %bitcast.118, ...), custom_call_target="tpu_custom_call" | custom-call | tf_op jit(solution)/shard_map/open_layer/pallas_call | solution.py:517
  46.7 1.7 collective-permute-start
  49.7 12.3 %all-reduce.4 = s32[8]{0:T(128)} all-reduce(s32[8]{0:T(128)S(1)} %dynamic-update-slice), channel_id=1, replica_groups=mesh['dp'=8,'tensor'=4] {'dp'}, use_global_device_ids=true, to_apply=%add.4 | all-reduce | flops 8 | bytes 64
  63.5 10.7 %mixer.1 = (bf16[288,1024]{1,0:T(8,128)(2,1)}, f32[288,1024]{1,0:T(8,128)}, f32[4,4,72,72]{3,2,1,0:T(8,128)}) custom-call(bf16[864,1024]{1,0:T(8,128)(2,1)} %get-tuple-element.37.proj_ref, f32[8,1024]{1,0:T(8,128)} %get-tuple-element.38.logit_ref, f32[288,16]{1,0:T(8,128)} %pad_convert_fusion.taps_ref), custom_call_target="tpu_custom_call" | custom-call | tf_op jit(solution)/shard_map/mixer/pallas_call | solution.py:153
  75.1 87.3 %middle_layer.1 = (f32[288,1024]{1,0:T(8,128)}, f32[288,1024]{1,0:T(8,128)}, f32[288,1024]{1,0:T(8,128)}, bf16[288,1024]{1,0:T(8,128)(2,1)}, f32[288,1024]{1,0:T...) custom-call(bf16[288,1024]{1,0:T(8,128)(2,1)} %get-tuple-element.41., ...), custom_call_target="tpu_custom_call" | custom-call | tf_op jit(solution)/shard_map/middle_layer/pallas_call | solution.py:752
  163.1 18.3 %mixer_back.1 = (bf16[896,1024]{1,0:T(8,128)(2,1)}, f32[288,16]{1,0:T(8,128)}) custom-call(bf16[864,1024]{1,0:T(8,128)(2,1)} %get-tuple-element.37.proj_ref, f32[8,1024]{1,0:T(8,128)} %get-tuple-element.38.logit_ref, f32[288,16]{1,0:T(8,128)} %pad_convert_fusion.taps_ref, f32[288,1024]{1,0:T(8,128)} %get-tuple-element.39.rec_ref, ...), custom_call_target="tpu_custom_call" | custom-call | tf_op jit(solution)/shard_map/mixer_back/pallas_call | solution.py:264
  184.1 1.6 collective-permute-start.6
  185.6 2.5 dynamic-slice_bitcast_fusion.1
  189.8 1.5 collective-permute-start.14
  192.2 5.0 %collective-permute-done.6 = bf16[4,144,288]{2,1,0:T(8,128)(2,1)S(1)} collective-permute-done((bf16[4,144,288]{2,1,0:T(8,128)(2,1)S(1)}, bf16[4,144,288]{2,1,0:T(8,128)(2,1)S(1)}, u32[]{:S(2)}, u32[]{:S(2)}) %collective-permute-start.6) | collective-permute-done | bytes 331808 | tf_op jit(solution)/shard_map/ppermute | solution.py:898
  197.6 1.7 collective-permute-start.8
  199.8 30.8 %close_layer.1 = (f32[288,1024]{1,0:T(8,128)}, bf16[288,1024]{1,0:T(8,128)(2,1)}, bf16[1152,896]{1,0:T(8,128)(2,1)}, f32[288,8]{1,0:T(8,128)}) custom-call(bf16[896,1024]{1,0:T(8,128)(2,1)} %get-tuple-element.45.gproj_ref, bf16[1152,896]{1,0:T(8,128)(2,1)} %get-tuple-element.46.wback_ref, bf16[1152,1024]{1,0:T(8,128)(2,1)} %get-tuple-element.47.normed_ref, ...), custom_call_target="tpu_custom_call" | custom-call | tf_op jit(solution)/shard_map/close_layer/pallas_call | solution.py:866
  231.7 2.9 fusion.5
  234.8 6.6 %psum.7 = f32[1152]{0:T(1024)S(1)} all-reduce(f32[1152]{0:T(1024)S(1)} %fusion.5), channel_id=1, replica_groups=mesh['dp'=8,'tensor'=4] {'tensor'}, use_global_device_ids=true, to_apply=%region_0.1 | all-reduce | flops 1152 | bytes 9216 | tf_op jit(solution)/shard_map/psum | solution.py:987
  244.6 1.5 collective-permute-start.2
  246.1 67.8 %all-reduce.8.cloned.1.call-done = f32[53024]{0:T(1024)} async-done(((f32[53024]{0:T(1024)}), f32[53024]{0:T(1024)}) %all-reduce.8.cloned.1.call-update) | async-done | bytes 212112
  316.3 1.3 copy.78
  319.6 1.3 fusion.19
  321.0 2.2 fusion.3
  323.3 2.4 collective-permute-start.13
  327.5 1.8 fusion.2
  329.4 2.6 collective-permute-start.17
  332.6 1.5 fusion.4
  335.4 13.6 %collective-permute-start.15 = (bf16[144,1152]{1,0:T(8,128)(2,1)S(1)}, bf16[144,1152]{1,0:T(8,128)(2,1)S(1)}, u32[]{:S(2)}, u32[]{:S(2)}) collective-permute-start(bf16[144,1152]{1,0:T(8,128)(2,1)S(1)} %get-tuple-element.124), channel_id=1, source_target_pairs={{0,8},{4,12},{8,16},{12,20},{16,24},{20,28},{24,0},{28,4},{1,9},{5... | collective-permute-start | bytes 995336 | tf_op jit(solution)/shard_map/ppermute | solution.py:909
  349.0 20.7 %collective-permute-done.12 = bf16[144,1152]{1,0:T(8,128)(2,1)S(1)} collective-permute-done((bf16[144,1152]{1,0:T(8,128)(2,1)S(1)}, bf16[144,1152]{1,0:T(8,128)(2,1)S(1)}, u32[]{:S(2)}, u32[]{:S(2)}) %collective-permute-start.12) | collective-permute-done | bytes 331808 | tf_op jit(solution)/shard_map/ppermute | solution.py:909
  369.7 2.8 collective-permute-start.4
  373.5 15.7 %collective-permute-start.3 = (bf16[144,896]{1,0:T(8,128)(2,1)S(1)}, bf16[144,896]{1,0:T(8,128)(2,1)S(1)}, u32[]{:S(2)}, u32[]{:S(2)}) collective-permute-start(bf16[144,896]{1,0:T(8,128)(2,1)S(1)} %get-tuple-element.130), channel_id=1, source_target_pairs={{0,8},{4,12},{8,16},{12,20},{16,24},{20,28},{24,0},{28,4},{1,9},{5... | collective-permute-start | bytes 774152 | tf_op jit(solution)/shard_map/ppermute | solution.py:909
  389.2 6.5 %collective-permute-done.16 = bf16[144,1152]{1,0:T(8,128)(2,1)S(1)} collective-permute-done((bf16[144,1152]{1,0:T(8,128)(2,1)S(1)}, bf16[144,1152]{1,0:T(8,128)(2,1)S(1)}, u32[]{:S(2)}, u32[]{:S(2)}) %collective-permute-start.16) | collective-permute-done | bytes 331808 | tf_op jit(solution)/shard_map/ppermute | solution.py:909
  396.8 6.7 %collective-permute-done.4 = bf16[144,896]{1,0:T(8,128)(2,1)S(1)} collective-permute-done((bf16[144,896]{1,0:T(8,128)(2,1)S(1)}, bf16[144,896]{1,0:T(8,128)(2,1)S(1)}, u32[]{:S(2)}, u32[]{:S(2)}) %collective-permute-start.4) | collective-permute-done | bytes 258080 | tf_op jit(solution)/shard_map/ppermute | solution.py:909
  (100 shorter events, 30.5 us)
Async XLA Ops:
  7.2 306.7 %all-reduce.8.cloned.1.call-start = ((), (), s32[]{:S(2)}) async-start(), calls=%async_computation | async-start | bytes 425984
  14.7 33.7 %copy-start.12 = (u32[32]{0:T(128)S(1)}, u32[32]{0:T(128)}, u32[]{:S(2)}) copy-start(u32[32]{0:T(128)} %constant.137) | copy-start | bytes 388
  14.7 47.3 %copy-start.10 = (bf16[3,3,288]{2,1,0:T(4,128)(2,1)S(1)}, bf16[3,3,288]{2,1,0:T(4,128)(2,1)}, u32[]{:S(2)}) copy-start(bf16[3,3,288]{2,1,0:T(4,128)(2,1)} %param.23) | copy-start | bytes 15556
  46.7 27.6 %collective-permute-start = (bf16[288,1024]{1,0:T(8,128)(2,1)}, bf16[288,1024]{1,0:T(8,128)(2,1)S(1)}, u32[]{:S(2)}, u32[]{:S(2)}) collective-permute-start(bf16[288,1024]{1,0:T(8,128)(2,1)} %get-tuple-element.43.gmlp_ref), channel_id=1, source_target_pairs={{0,2},{1,3},{2,0},{3,1},{4,6},{5,7},{6,4},{7,5},{8,10},{9,11},{10,... | collective-permute-start | bytes 1769480 | tf_op jit(solution)/shard_map/ppermute | solution.py:955
  74.3 0.8 copy-start.7
  162.4 36.9 %collective-permute-start.1 = (bf16[288,1024]{1,0:T(8,128)(2,1)}, bf16[288,1024]{1,0:T(8,128)(2,1)}, u32[]{:S(2)}, u32[]{:S(2)}) collective-permute-start(bf16[288,1024]{1,0:T(8,128)(2,1)} %get-tuple-element.52), channel_id=1, source_target_pairs={{0,2},{1,3},{2,0},{3,1},{4,6},{5,7},{6,4},{7,5},{8,10},{9,11},{10,... | collective-permute-start | bytes 1769480 | tf_op jit(solution)/shard_map/ppermute | solution.py:970
  163.1 20.9 %copy-start.5 = (bf16[1152,288]{1,0:T(8,128)(2,1)S(1)}, bf16[1152,288]{1,0:T(8,128)(2,1)}, u32[]{:S(2)}) copy-start(bf16[1152,288]{1,0:T(8,128)(2,1)} %get-tuple-element.59) | copy-start | bytes 1990660
  183.0 5.6 %copy-start = (bf16[1152,1152]{1,0:T(8,128)(2,1)S(1)}, bf16[1152,1152]{1,0:T(8,128)(2,1)}, u32[]{:S(2)}) copy-start(bf16[1152,1152]{1,0:T(8,128)(2,1)} %get-tuple-element.61) | copy-start | bytes 7962628
  184.1 13.1 %collective-permute-start.6 = (bf16[4,144,288]{2,1,0:T(8,128)(2,1)S(1)}, bf16[4,144,288]{2,1,0:T(8,128)(2,1)S(1)}, u32[]{:S(2)}, u32[]{:S(2)}) collective-permute-start(bf16[4,144,288]{2,1,0:T(8,128)(2,1)S(1)} %dynamic-slice_bitcast_fusion.3), channel_id=1, source_target_pairs={{0,4},{4,0},{8,12},{12,8},{16,20},{20,16},{24,28},{28,24},{1,5},{5... | collective-permute-start | bytes 995336 | tf_op jit(solution)/shard_map/ppermute | solution.py:898
  188.1 132.8 %collective-permute-start.10 = (bf16[4,144,1152]{2,1,0:T(8,128)(2,1)}, bf16[4,144,1152]{2,1,0:T(8,128)(2,1)}, u32[]{:S(2)}, u32[]{:S(2)}) collective-permute-start(bf16[4,144,1152]{2,1,0:T(8,128)(2,1)} %dynamic-slice_bitcast_fusion.1), channel_id=1, source_target_pairs={{0,4},{4,0},{8,12},{12,8},{16,20},{20,16},{24,28},{28,24},{1,5},{5... | collective-permute-start | bytes 3981320 | tf_op jit(solution)/shard_map/ppermute | solution.py:898
  189.8 137.7 %collective-permute-start.14 = (bf16[4,144,1152]{2,1,0:T(8,128)(2,1)}, bf16[4,144,1152]{2,1,0:T(8,128)(2,1)}, u32[]{:S(2)}, u32[]{:S(2)}) collective-permute-start(bf16[4,144,1152]{2,1,0:T(8,128)(2,1)} %dynamic-slice_bitcast_fusion), channel_id=1, source_target_pairs={{0,4},{4,0},{8,12},{12,8},{16,20},{20,16},{24,28},{28,24},{1,5},{5... | collective-permute-start | bytes 3981320 | tf_op jit(solution)/shard_map/ppermute | solution.py:898
  197.4 45.4 %collective-permute-start.9 = (bf16[144,288]{1,0:T(8,128)(2,1)S(1)}, bf16[144,288]{1,0:T(8,128)(2,1)S(1)}, u32[]{:S(2)}, u32[]{:S(2)}) collective-permute-start(bf16[144,288]{1,0:T(8,128)(2,1)S(1)} %get-tuple-element.134), channel_id=1, source_target_pairs={{0,24},{4,28},{8,0},{12,4},{16,8},{20,12},{24,16},{28,20},{1,25},{... | collective-permute-start | bytes 248840 | tf_op jit(solution)/shard_map/ppermute | solution.py:909
  197.6 45.2 %collective-permute-start.8 = (bf16[144,288]{1,0:T(8,128)(2,1)S(1)}, bf16[144,288]{1,0:T(8,128)(2,1)S(1)}, u32[]{:S(2)}, u32[]{:S(2)}) collective-permute-start(bf16[144,288]{1,0:T(8,128)(2,1)S(1)} %get-tuple-element.135), channel_id=1, source_target_pairs={{0,16},{4,20},{8,24},{12,28},{16,0},{20,4},{24,8},{28,12},{1,17},{... | collective-permute-start | bytes 248840 | tf_op jit(solution)/shard_map/ppermute | solution.py:909
  199.3 43.5 %collective-permute-start.7 = (bf16[144,288]{1,0:T(8,128)(2,1)S(1)}, bf16[144,288]{1,0:T(8,128)(2,1)S(1)}, u32[]{:S(2)}, u32[]{:S(2)}) collective-permute-start(bf16[144,288]{1,0:T(8,128)(2,1)S(1)} %get-tuple-element.133), channel_id=1, source_target_pairs={{0,8},{4,12},{8,16},{12,20},{16,24},{20,28},{24,0},{28,4},{1,9},{5... | collective-permute-start | bytes 248840 | tf_op jit(solution)/shard_map/ppermute | solution.py:909
  231.7 9.8 %copy-start.9 = (f32[1152]{0:T(1024)S(1)}, f32[1152]{0:T(1024)}, u32[]{:S(2)}) copy-start(f32[1152]{0:T(1024)} %get-tuple-element.122) | copy-start | bytes 13828
  231.7 11.9 %copy-start.2 = (bf16[1152,896]{1,0:T(8,128)(2,1)S(1)}, bf16[1152,896]{1,0:T(8,128)(2,1)}, u32[]{:S(2)}) copy-start(bf16[1152,896]{1,0:T(8,128)(2,1)} %get-tuple-element.58) | copy-start | bytes 6193156
  242.1 0.7 copy-start.6
  244.6 87.4 %collective-permute-start.2 = (bf16[4,144,896]{2,1,0:T(8,128)(2,1)}, bf16[4,144,896]{2,1,0:T(8,128)(2,1)}, u32[]{:S(2)}, u32[]{:S(2)}) collective-permute-start(bf16[4,144,896]{2,1,0:T(8,128)(2,1)} %dynamic-slice_bitcast_fusion.2), channel_id=1, source_target_pairs={{0,4},{4,0},{8,12},{12,8},{16,20},{20,16},{24,28},{28,24},{1,5},{5... | collective-permute-start | bytes 3096584 | tf_op jit(solution)/shard_map/ppermute | solution.py:898
  316.3 3.4 copy-start.11
  321.0 6.5 %copy-start.1 = (bf16[1152,1152]{1,0:T(8,128)(2,1)S(1)}, bf16[1152,1152]{1,0:T(8,128)(2,1)}, u32[]{:S(2)}) copy-start(bf16[1152,1152]{1,0:T(8,128)(2,1)} %get-tuple-element.61) | copy-start | bytes 7962628
  323.3 12.1 %collective-permute-start.13 = (bf16[144,1152]{1,0:T(8,128)(2,1)S(1)}, bf16[144,1152]{1,0:T(8,128)(2,1)S(1)}, u32[]{:S(2)}, u32[]{:S(2)}) collective-permute-start(bf16[144,1152]{1,0:T(8,128)(2,1)S(1)} %get-tuple-element.128), channel_id=1, source_target_pairs={{0,24},{4,28},{8,0},{12,4},{16,8},{20,12},{24,16},{28,20},{1,25},{... | collective-permute-start | bytes 995336 | tf_op jit(solution)/shard_map/ppermute | solution.py:909
  325.7 44.0 %collective-permute-start.12 = (bf16[144,1152]{1,0:T(8,128)(2,1)S(1)}, bf16[144,1152]{1,0:T(8,128)(2,1)S(1)}, u32[]{:S(2)}, u32[]{:S(2)}) collective-permute-start(bf16[144,1152]{1,0:T(8,128)(2,1)S(1)} %get-tuple-element.129), channel_id=1, source_target_pairs={{0,16},{4,20},{8,24},{12,28},{16,0},{20,4},{24,8},{28,12},{1,17},{... | collective-permute-start | bytes 995336 | tf_op jit(solution)/shard_map/ppermute | solution.py:909
  326.2 43.5 %collective-permute-start.11 = (bf16[144,1152]{1,0:T(8,128)(2,1)S(1)}, bf16[144,1152]{1,0:T(8,128)(2,1)S(1)}, u32[]{:S(2)}, u32[]{:S(2)}) collective-permute-start(bf16[144,1152]{1,0:T(8,128)(2,1)S(1)} %get-tuple-element.127), channel_id=1, source_target_pairs={{0,8},{4,12},{8,16},{12,20},{16,24},{20,28},{24,0},{28,4},{1,9},{5... | collective-permute-start | bytes 995336 | tf_op jit(solution)/shard_map/ppermute | solution.py:909
  327.5 5.1 %copy-start.3 = (bf16[1152,896]{1,0:T(8,128)(2,1)S(1)}, bf16[1152,896]{1,0:T(8,128)(2,1)}, u32[]{:S(2)}) copy-start(bf16[1152,896]{1,0:T(8,128)(2,1)} %get-tuple-element.58) | copy-start | bytes 6193156
  329.4 44.2 %collective-permute-start.17 = (bf16[144,1152]{1,0:T(8,128)(2,1)S(1)}, bf16[144,1152]{1,0:T(8,128)(2,1)S(1)}, u32[]{:S(2)}, u32[]{:S(2)}) collective-permute-start(bf16[144,1152]{1,0:T(8,128)(2,1)S(1)} %get-tuple-element.125), channel_id=1, source_target_pairs={{0,24},{4,28},{8,0},{12,4},{16,8},{20,12},{24,16},{28,20},{1,25},{... | collective-permute-start | bytes 995336 | tf_op jit(solution)/shard_map/ppermute | solution.py:909
  332.0 63.8 %collective-permute-start.16 = (bf16[144,1152]{1,0:T(8,128)(2,1)S(1)}, bf16[144,1152]{1,0:T(8,128)(2,1)S(1)}, u32[]{:S(2)}, u32[]{:S(2)}) collective-permute-start(bf16[144,1152]{1,0:T(8,128)(2,1)S(1)} %get-tuple-element.126), channel_id=1, source_target_pairs={{0,16},{4,20},{8,24},{12,28},{16,0},{20,4},{24,8},{28,12},{1,17},{... | collective-permute-start | bytes 995336 | tf_op jit(solution)/shard_map/ppermute | solution.py:909
  335.4 60.4 %collective-permute-start.15 = (bf16[144,1152]{1,0:T(8,128)(2,1)S(1)}, bf16[144,1152]{1,0:T(8,128)(2,1)S(1)}, u32[]{:S(2)}, u32[]{:S(2)}) collective-permute-start(bf16[144,1152]{1,0:T(8,128)(2,1)S(1)} %get-tuple-element.124), channel_id=1, source_target_pairs={{0,8},{4,12},{8,16},{12,20},{16,24},{20,28},{24,0},{28,4},{1,9},{5... | collective-permute-start | bytes 995336 | tf_op jit(solution)/shard_map/ppermute | solution.py:909
  369.7 27.1 %collective-permute-start.5 = (bf16[144,896]{1,0:T(8,128)(2,1)S(1)}, bf16[144,896]{1,0:T(8,128)(2,1)S(1)}, u32[]{:S(2)}, u32[]{:S(2)}) collective-permute-start(bf16[144,896]{1,0:T(8,128)(2,1)S(1)} %get-tuple-element.131), channel_id=1, source_target_pairs={{0,24},{4,28},{8,0},{12,4},{16,8},{20,12},{24,16},{28,20},{1,25},{... | collective-permute-start | bytes 774152 | tf_op jit(solution)/shard_map/ppermute | solution.py:909
  369.7 33.8 %collective-permute-start.4 = (bf16[144,896]{1,0:T(8,128)(2,1)S(1)}, bf16[144,896]{1,0:T(8,128)(2,1)S(1)}, u32[]{:S(2)}, u32[]{:S(2)}) collective-permute-start(bf16[144,896]{1,0:T(8,128)(2,1)S(1)} %get-tuple-element.132), channel_id=1, source_target_pairs={{0,16},{4,20},{8,24},{12,28},{16,0},{20,4},{24,8},{28,12},{1,17},{... | collective-permute-start | bytes 774152 | tf_op jit(solution)/shard_map/ppermute | solution.py:909
  373.5 30.0 %collective-permute-start.3 = (bf16[144,896]{1,0:T(8,128)(2,1)S(1)}, bf16[144,896]{1,0:T(8,128)(2,1)S(1)}, u32[]{:S(2)}, u32[]{:S(2)}) collective-permute-start(bf16[144,896]{1,0:T(8,128)(2,1)S(1)} %get-tuple-element.130), channel_id=1, source_target_pairs={{0,8},{4,12},{8,16},{12,20},{16,24},{20,28},{24,0},{28,4},{1,9},{5... | collective-permute-start | bytes 774152 | tf_op jit(solution)/shard_map/ppermute | solution.py:909
  403.6 2.1 copy-start.8
  403.7 2.8 copy-start.4
Sparse Core Ops, SparseCore 0:
  242.9 70.9 all-reduce.7

commit v4 on v3

--- a/solution.py
+++ b/solution.py
@@ -165,6 +165,7 @@
             pltpu.VMEM((length, 8), jnp.float32),
         ],
         compiler_params=pltpu.CompilerParams(vmem_limit_bytes=56 * 2**20),
+        cost_estimate=work_for(11),
         name="mixer",
     )(proj, logit, taps)
 
@@ -278,6 +279,7 @@
             pltpu.VMEM((3, 8, length), jnp.float32),
         ],
         compiler_params=pltpu.CompilerParams(vmem_limit_bytes=56 * 2**20),
+        cost_estimate=work_for(18),
         name="mixer_back",
     )(proj, logit, taps, rec, states, grad)
 
@@ -287,6 +289,10 @@
 VMEM_LIMIT = 58 * 2**20
 VMEM_SPEC = pl.BlockSpec(memory_space=pltpu.VMEM)
 WIDE_ROWS = 896
+
+
+def work_for(microseconds):
+    return pl.CostEstimate(flops=int(microseconds * 1e9), bytes_accessed=0, transcendentals=0)
 
 
 def places():
@@ -537,6 +543,7 @@
         compiler_params=pltpu.CompilerParams(
             collective_id=1, has_side_effects=True, vmem_limit_bytes=VMEM_LIMIT
         ),
+        cost_estimate=work_for(25),
         name="open_layer",
     )(x, cot, silu, ada, bias, qkv, gate, gate_bias)
 
@@ -785,27 +792,58 @@
         compiler_params=pltpu.CompilerParams(
             collective_id=2, has_side_effects=True, vmem_limit_bytes=VMEM_LIMIT
         ),
+        cost_estimate=work_for(80),
         name="middle_layer",
     )(mix, x, mods, gmlp, gmlp_far, cot, out_w, up, down)
 
 
+def send_dp(source, target, sems, at, peer):
+    copy = pltpu.make_async_remote_copy(
+        src_ref=source,
+        dst_ref=target,
+        send_sem=sems.at[0, at],
+        recv_sem=sems.at[1, at],
+        device_id={"dp": peer},
+        device_id_type=MESH,
+    )
+    copy.start()
+    return copy
+
+
 def close_kernel(
+    shard_count,
     gproj_ref, wback_ref, normed_ref, x_ref, stats_ref, mods_ref, gafter_ref, after_ref, cot_ref,
-    mlp_keep_ref, mlp_far_ref, sums_ref,
-    gtokens_ref, out_ref, gqkv_ref, gmods_ref,
-    pair_out, pair_in, far_out, far_in, keep, mean_rows, sum_sems, mean_sems,
+    mlp_keep_ref, mlp_far_ref, sums_ref, gtaps_ref, cond_ref, label_ref, ada_ref,
+    gtokens_ref, out_ref, gqkv_ref, gclass_ref, gada_ref, gsmall_ref,
+    pair_out, pair_in, far_out, far_in, keep, mean_rows, silu_rows, gmods, ada, parcels, latent_in, mods_out, mods_in,
+    gcond, silu_own, mods_own, label_own,
+    sum_sems, mean_sems, silu_sems, dp_sems, ada_sem,
 ):
     part, length = x_ref.shape
     width = 4 * part
+    own = width // shard_count
     chunks = length // CHUNK
     lanes = [pl.ds(k * CHUNK, CHUNK) for k in range(chunks)]
     where = places()
+    spot = lax.axis_index("dp")
     mean_rows[...] = jnp.zeros_like(mean_rows)
-    greet(where[1:])
+    silu_rows[...] = jnp.zeros_like(silu_rows)
+    parcels[...] = jnp.zeros_like(parcels)
+    mods_out[...] = jnp.zeros_like(mods_out)
+    barrier = pltpu.get_barrier_semaphore()
+    for peer in where[1:]:
+        pl.semaphore_signal(barrier, inc=1, device_id={"tensor": peer}, device_id_type=MESH)
+    for step in range(1, shard_count):
+        pl.semaphore_signal(
+            barrier, inc=1, device_id={"dp": lax.rem(spot + step, shard_count)}, device_id_type=MESH
+        )
+    pl.semaphore_wait(barrier, shard_count + 2)
+    ada_copy = pltpu.make_async_copy(ada_ref, ada, ada_sem)
+    ada_copy.start()
     total_sum = Reduce(where, part, (pair_out, pair_in, far_out, far_in, keep), sum_sems)
     means = Rows(where, mean_rows, mean_sems)
     scale_one, gate_two = mods_ref[:, 1:2], mods_ref[:, 5:6]
-    gmods_ref[...] = sums_ref[...]
+    gmods[...] = sums_ref[...]
 
     def start(k):
         block = gproj_ref[:, lanes[k]]
@@ -817,8 +855,8 @@
     def end(k):
         grad = total_sum.end(k, lanes[k])
         unit = unit_of(k)
-        gmods_ref[:, 0:1] += column_sums(grad)
-        gmods_ref[:, 1:2] += column_sums(grad * unit)
+        gmods[:, 0:1] += column_sums(grad)
+        gmods[:, 1:2] += column_sums(grad * unit)
         scaled = grad * (1.0 + scale_one)
         gtokens_ref[:, lanes[k]] = scaled
         means.start(k, lanes[k], row_sums(scaled), row_sums(scaled * unit))
@@ -831,7 +869,7 @@
     def outputs(k):
         mlp = mlp_keep_ref[:, lanes[k]] + mlp_far_ref[:, lanes[k]].astype(jnp.float32)
         out_ref[:, lanes[k]] = low(after_ref[:, lanes[k]] + gate_two * mlp)
-        gmods_ref[:, 5:6] += column_sums(cot_ref[:, lanes[k]].astype(jnp.float32) * mlp)
+        gmods[:, 5:6] += column_sums(cot_ref[:, lanes[k]].astype(jnp.float32) * mlp)
 
     def weight_grad(quarter):
         rows = pl.ds(quarter * part, part)
@@ -853,37 +891,121 @@
         end(k)
         if k > 0:
             tokens(k - 1)
+
+    rows = jnp.transpose(gmods[...])
+    low_rows = low(rows)
+    row_at = lax.broadcasted_iota(jnp.int32, (8, width), 0)
+    ada_copy.wait()
+    product = jnp.zeros((8, width), jnp.float32)
+    for index in range(6):
+        product = product + jnp.where(row_at == index, mm(low_rows, ada[index * part : (index + 1) * part, :], NN), 0.0)
+    me = where[0]
+    silu_rows[me, 0:1, :] = row_sums(product)
+    silu_copies = [
+        send(silu_rows.at[me], silu_rows.at[me], silu_sems, index, peer) for index, peer in enumerate(where[1:])
+    ]
+    taps = jnp.transpose(gtaps_ref[...])
+    forget = gproj_ref[3 * part : 3 * part + 8, :].astype(jnp.float32)
+    forget = jnp.transpose(jnp.broadcast_to(column_sums(forget), (8, 128)))[0:1]
+    small = jnp.concatenate([rows[:6], taps[:9], jnp.zeros((1, part), jnp.float32)], axis=0)
+    mods_out[:, :part] = low(small)
+    mods_out[:, part : part + 8] = low(jnp.broadcast_to(forget, (16, 8)))
+    mods_in[spot] = mods_out[...]
+    dp_copies = []
+    for step in range(1, shard_count):
+        peer = lax.rem(spot + step, shard_count)
+        dp_copies.append(send_dp(mods_out, mods_in.at[spot], dp_sems, step, peer))
     tokens(chunks - 1)
+    for copy in silu_copies:
+        copy.wait_recv()
+    grad_silu = sum(silu_rows[index, 0:1, :] for index in range(4))
+    cond = cond_ref[0:1, :]
+    sigmoid = 1.0 / (1.0 + jnp.exp(-cond))
+    grad_cond = grad_silu * (sigmoid * (1.0 + cond * (1.0 - sigmoid)))
+    silu = low(cond * sigmoid).astype(jnp.float32)
+    for index in range(shard_count):
+        columns = slice(index * own, (index + 1) * own)
+        parcels[index, 0:1, :own] = grad_cond[:, columns]
+        parcels[index, 1:2, :own] = silu[:, columns]
+        parcels[index, 2:3, :] = jnp.broadcast_to(label_ref[...], (1, parcels.shape[2]))
+    latent_in[spot] = parcels[spot]
+    for step in range(1, shard_count):
+        peer = lax.rem(spot + step, shard_count)
+        dp_copies.append(send_dp(parcels.at[peer], latent_in.at[spot], dp_sems, shard_count + step, peer))
+    for copy in dp_copies:
+        copy.wait_recv()
+    totals = jnp.zeros(mods_out.shape, jnp.float32)
+    for index in range(shard_count):
+        arrived = mods_in[index].astype(jnp.float32)
+        totals = totals + arrived
+        for row in range(6):
+            mods_own[row, index : index + 1, :] = arrived[row : row + 1, :part]
+        gcond[index : index + 1, :] = latent_in[index, 0:1, :own]
+        silu_own[index : index + 1, :] = latent_in[index, 1:2, :own]
+        label_own[index : index + 1, :] = latent_in[index, 2:3, :128]
+    gsmall_ref[...] = totals
+    class_at = lax.broadcasted_iota(jnp.int32, (shard_count, NCLASS), 1).astype(jnp.float32)
+    onehot = jnp.where(label_own[:, 0:1] == class_at, 1.0, 0.0)
+    gclass_ref[...] = lax.dot_general(
+        gcond[...], onehot, TN, precision=TOP_PRECISION, preferred_element_type=jnp.float32
+    )
+    for row in range(6):
+        gada_ref[row] = mm(low(silu_own[...]), low(mods_own[row]), TN)
+    for copy in dp_copies + silu_copies:
+        copy.wait_send()
     total_sum.finish()
     means.finish()
 
 
-def close_layer(gproj, wback, normed, x, stats, mods, gafter, after, cot, mlp_keep, mlp_far, sums):
+def close_layer(
+    gproj, wback, normed, x, stats, mods, gafter, after, cot, mlp_keep, mlp_far, sums, gtaps, cond, label, ada,
+    shard_count,
+):
     part, length = x.shape
     width = 4 * part
+    own = width // shard_count
     chunks = length // CHUNK
+    padded = part + -part % 128
+    own_padded = own + -own % 128
     shape = jax.ShapeDtypeStruct
     return pl.pallas_call(
-        close_kernel,
+        functools.partial(close_kernel, shard_count),
         out_shape=(
             shape((part, length), jnp.float32),
             shape((part, length), jnp.bfloat16),
             shape((width, WIDE_ROWS), jnp.bfloat16),
-            shape((part, 8), jnp.float32),
+            shape((own, NCLASS), jnp.float32),
+            shape((6, own, part), jnp.float32),
+            shape((16, padded), jnp.float32),
         ),
-        in_specs=[VMEM_SPEC] * 12,
-        out_specs=[VMEM_SPEC] * 4,
+        in_specs=[VMEM_SPEC] * 15 + [pl.BlockSpec(memory_space=pl.ANY)],
+        out_specs=[VMEM_SPEC] * 6,
         scratch_shapes=[
             *reduce_scratch(part, length),
             pltpu.VMEM((4, 8, length), jnp.float32),
+            pltpu.VMEM((4, 8, width), jnp.float32),
+            pltpu.VMEM((part, 8), jnp.float32),
+            pltpu.VMEM(ada.shape, jnp.bfloat16),
+            pltpu.VMEM((shard_count, 8, own_padded), jnp.float32),
+            pltpu.VMEM((shard_count, 8, own_padded), jnp.float32),
+            pltpu.VMEM((16, padded), jnp.bfloat16),
+            pltpu.VMEM((shard_count, 16, padded), jnp.bfloat16),
+            pltpu.VMEM((shard_count, own), jnp.float32),
+            pltpu.VMEM((shard_count, own), jnp.float32),
+            pltpu.VMEM((6, shard_count, part), jnp.float32),
+            pltpu.VMEM((shard_count, 128), jnp.float32),
             copy_sems(3 * chunks),
             copy_sems(3 * chunks),
+            copy_sems(3),
+            copy_sems(2 * shard_count),
+            pltpu.SemaphoreType.DMA,
         ],
         compiler_params=pltpu.CompilerParams(
             collective_id=3, has_side_effects=True, vmem_limit_bytes=VMEM_LIMIT
         ),
+        cost_estimate=work_for(30),
         name="close_layer",
-    )(gproj, wback, normed, x, stats, mods, gafter, after, cot, mlp_keep, mlp_far, sums)
+    )(gproj, wback, normed, x, stats, mods, gafter, after, cot, mlp_keep, mlp_far, sums, gtaps, cond, label, ada)
 
 
 def dp_total(partial, shard_count):
@@ -931,9 +1053,7 @@
 ):
     _, length, part = latent_tokens.shape
     heads = gate_weight.shape[1]
-    hidden = up_weight.shape[1]
     shard_count = lax.psum(1, "dp")
-    shard_at = lax.axis_index("dp")
     own_width = MODEL_DIM // shard_count
     x = latent_tokens[0].T
     cot = cotangent[0].T
@@ -972,53 +1092,21 @@
     grad_up = dp_total(grad_up, shard_count)
     grad_out_w = dp_total(grad_out_w, shard_count)
     grad_projected, grad_taps = mixer_back(projected, forget_logit, taps, recurrent, states, grad_mixed, heads)
-    grad_tokens, layer_out, grad_wide, grad_mod_columns = close_layer(
-        grad_projected, wide_back, normed_one, x, stats, mods, grad_after, after_attn, cot, mlp_keep, mlp_far, sums_two
+    grad_tokens, layer_out, grad_wide, grad_class, grad_ada_w, small = close_layer(
+        grad_projected, wide_back, normed_one, x, stats, mods, grad_after, after_attn, cot, mlp_keep, mlp_far,
+        sums_two, grad_taps, cond, labels.astype(jnp.float32)[None], ada, shard_count,
     )
     grad_wide = dp_total(grad_wide, shard_count)
-
-    grad_mods = low(grad_mod_columns.T[:6])
-    mods_flat = grad_mods.reshape(1, 6 * part)
-    grad_silu = mm(mods_flat, ada, NN)
-    grad_gate_b = jnp.sum(grad_projected[3 * part : 3 * part + heads].astype(jnp.float32), axis=1)
-    small = jnp.concatenate(
-        [
-            mods_flat.astype(jnp.float32).reshape(6 * part),
-            lax.psum(grad_silu, "tensor").reshape(MODEL_DIM),
-            cond.reshape(MODEL_DIM),
-            grad_gate_b,
-            grad_taps[:, :9].T.reshape(9 * part),
-        ]
-    )
-    every = lax.all_gather(small, "dp", axis=0, tiled=False)
-    every_labels = lax.all_gather(labels, "dp", axis=0, tiled=True)
-    sizes = [6 * part, MODEL_DIM, MODEL_DIM, heads, 9 * part]
-    starts = [sum(sizes[:index]) for index in range(len(sizes) + 1)]
-    every_mods, every_silu, every_cond, every_gate_b, every_conv = (
-        every[:, begin:end] for begin, end in zip(starts[:-1], starts[1:])
-    )
-    grad_ada_b = jnp.sum(every_mods, axis=0).reshape(6, part)
-    grad_gate_b = jnp.sum(every_gate_b, axis=0)
-    grad_conv = jnp.sum(every_conv, axis=0).reshape(3, 3, part)
-
-    def own_columns(rows):
-        return lax.dynamic_slice_in_dim(rows, shard_at * own_width, own_width, axis=1)
-
-    own_silu, own_pull = jax.vjp(jax.nn.silu, own_columns(every_cond))
-    own_cond = own_pull(own_columns(every_silu))[0]
-    grad_ada_w = mm(low(own_silu), low(every_mods), TN).reshape(own_width, 6, part)
-    every_onehot = every_labels[:, None] == jnp.arange(NCLASS, dtype=jnp.int32)[None, :]
-    grad_class = jnp.dot(every_onehot.astype(jnp.float32).T, own_cond, precision=TOP_PRECISION)
     return (
         layer_out.T[None],
         grad_tokens.T[None],
-        grad_class,
-        grad_ada_w,
-        grad_ada_b,
+        grad_class.T,
+        jnp.transpose(grad_ada_w, (1, 0, 2)),
+        small[:6, :part],
         grad_wide[:, : 3 * part].reshape(own_width, 3, part),
         grad_wide[:, 3 * part : 3 * part + heads],
-        grad_gate_b,
-        grad_conv,
+        small[15, part : part + heads],
+        small[6:15, :part].reshape(3, 3, part),
         grad_out_w.T,
         grad_up,
         grad_down.T,

time: 420 us -> 328 us (0.78)
  waiting for transfers between devices: 108 us -> 54.3 us
  blocking collectives: 18.9 us -> 0 us
  between operations: 16.5 us -> 2.27 us
  Pallas kernels: 179 us -> 190 us
  starting transfers between devices: 49.5 us -> 42 us
  matrix products: 4.69 us -> 0 us
    unnamed x2 -> x0, waiting for transfers between devices: 67.8 us -> none
    unnamed x1 -> x0, blocking collectives: 12.3 us -> none
    pallas_call x1, Pallas kernels: 30.8 us -> 40.7 us  [close_layer(): pl.pallas_call(functools.partial(close_kernel, shard_count), out_shape=(s...]
    ppermute x12, starting transfers between devices: 42 us -> 34.2 us  [dp_total(): lax.ppermute(block, 'dp', [(index, (index + 2 * step) % shard_count) for...]
    psum x1 -> x0, blocking collectives: 6.63 us -> none  [shards(): lax.psum(grad_silu, 'tensor').reshape(MODEL_DIM)]
    ppermute x12, waiting for transfers between devices: 35.2 us -> 41.1 us  [dp_total(): lax.ppermute(block, 'dp', [(index, (index + 2 * step) % shard_count) for...]
    ppermute x4, waiting for transfers between devices: 5.04 us -> 10.8 us  [dp_total(): lax.ppermute(outgoing, 'dp', [(index, index ^ 1) for index in range(shard...]
    dot_general x3 -> x0, matrix products: 4.69 us -> none  [the longest x2 3.35 us: mm(): lax.dot_general(left, right, form, preferred_element_type=jnp.float32)]
  transfers between devices with their start and end apart: 19 -> 18, of which waited for: 6 -> 7; matrix products, arithmetic and copies ran while one was open for 7% -> 6% of each run, Pallas kernels for 14% -> 22%
where the time goes in v4:
time: 328 us; the launch traced here: 322 us
  Pallas kernels  190 us (58%)
  waiting for transfers between devices  54.3 us (17%)
  starting transfers between devices  42 us (13%)
  local copies, waits for them, and re-layouts  21.5 us (7%)
  other arithmetic  12.4 us (4%)
    pallas_call x1, Pallas kernels, middle_layer(): pl.pallas_call(middle_kernel, out_shape=(shape((part, length), jnp.float3...  87.6 us
    ppermute x12, waiting for transfers between devices, dp_total(): lax.ppermute(block, 'dp', [(index, (index + 2 * step) % shard_count) for...  41.1 us
    pallas_call x1, Pallas kernels, close_layer(): pl.pallas_call(functools.partial(close_kernel, shard_count), out_shape=(s...  40.7 us
    ppermute x12, starting transfers between devices, dp_total(): lax.ppermute(block, 'dp', [(index, (index + 2 * step) % shard_count) for...  34.2 us
    pallas_call x1, Pallas kernels, open_layer(): pl.pallas_call(open_kernel, out_shape=(shape((width, length), jnp.bfloat1...  32 us
    pallas_call x1, Pallas kernels, mixer_back(): pl.pallas_call(functools.partial(back_kernel, heads), out_shape=(jax.Shap...  18.4 us
    pallas_call x1, Pallas kernels, mixer(): pl.pallas_call(functools.partial(mixer_kernel, heads), out_shape=(jax.Sha...  10.9 us
    ppermute x4, waiting for transfers between devices, dp_total(): lax.ppermute(outgoing, 'dp', [(index, index ^ 1) for index in range(shard...  10.8 us
  transfers between devices with their start and end apart: 18, of which 7 were waited for; matrix products, arithmetic and copies ran while one was open for 6% of the time, Pallas kernels for 22%

profile of v4, /device:TPU:0, one launch (start us, length us, event | category | flops | bytes accessed | tf_op | source)
XLA Modules:
  0.0 322.0 jit_solution(14990230928346155625)
XLA Ops:
  2.0 1.3 pad_convert_fusion.1.bias_ref
  4.7 1.3 pad.23.gate_ref
  6.0 1.4 convert_reduce_fusion
  8.0 32.0 %open_layer.1 = (bf16[1152,1024]{1,0:T(8,128)(2,1)}, bf16[864,1024]{1,0:T(8,128)(2,1)}, f32[8,1024]{1,0:T(8,128)}, f32[8,1024]{1,0:T(8,128)}, f32[288,8]{1,0:T(8...) custom-call(bf16[288,1024]{1,0:T(8,128)(2,1)} %bitcast.124, bf16[288,1024]{1,0:T(8,128)(2,1)} %bitcast.127, ...), custom_call_target="tpu_custom_call" | custom-call | flops 24999999488 | tf_op jit(solution)/shard_map/open_layer/pallas_call | solution.py:523
  40.0 1.7 collective-permute-start
  42.6 10.9 %mixer.1 = (bf16[288,1024]{1,0:T(8,128)(2,1)}, f32[288,1024]{1,0:T(8,128)}, f32[4,4,72,72]{3,2,1,0:T(8,128)}) custom-call(bf16[864,1024]{1,0:T(8,128)(2,1)} %get-tuple-element.39.proj_ref, f32[8,1024]{1,0:T(8,128)} %get-tuple-element.40.logit_ref, f32[288,16]{1,0:T(8,128)} %pad_convert_fusion.taps_ref), custom_call_target="tpu_custom_call" | custom-call | flops 11000000512 | tf_op jit(solution)/shard_map/mixer/pallas_call | solution.py:153
  53.5 2.4 collective-permute-done.gmlp_far_ref
  56.8 87.6 %middle_layer.1 = (f32[288,1024]{1,0:T(8,128)}, f32[288,1024]{1,0:T(8,128)}, f32[288,1024]{1,0:T(8,128)}, bf16[288,1024]{1,0:T(8,128)(2,1)}, f32[288,1024]{1,0:T...) custom-call(bf16[288,1024]{1,0:T(8,128)(2,1)} %get-tuple-element.43., ...), custom_call_target="tpu_custom_call" | custom-call | flops 80000000000 | tf_op jit(solution)/shard_map/middle_layer/pallas_call | solution.py:759
  144.4 1.5 collective-permute-start.1
  146.9 1.5 collective-permute-start.6
  148.5 2.5 dynamic-slice_bitcast_fusion.1
  151.5 18.4 %mixer_back.1 = (bf16[896,1024]{1,0:T(8,128)(2,1)}, f32[288,16]{1,0:T(8,128)}) custom-call(bf16[864,1024]{1,0:T(8,128)(2,1)} %get-tuple-element.39.proj_ref, f32[8,1024]{1,0:T(8,128)} %get-tuple-element.40.logit_ref, f32[288,16]{1,0:T(8,128)} %pad_convert_fusion.taps_ref, f32[288,1024]{1,0:T(8,128)} %get-tuple-element.41.rec_ref, ...), custom_call_target="tpu_custom_call" | custom-call | flops 17999998976 | tf_op jit(solution)/shard_map/mixer_back/pallas_call | solution.py:265
  170.1 3.6 %collective-permute-start.9 = (bf16[144,288]{1,0:T(8,128)(2,1)S(1)}, bf16[144,288]{1,0:T(8,128)(2,1)S(1)}, u32[]{:S(2)}, u32[]{:S(2)}) collective-permute-start(bf16[144,288]{1,0:T(8,128)(2,1)S(1)} %get-tuple-element.102), channel_id=1, source_target_pairs={{0,24},{4,28},{8,0},{12,4},{16,8},{20,12},{24,16},{28,20},{1,25},{... | collective-permute-start | bytes 248840 | tf_op jit(solution)/shard_map/ppermute | solution.py:1031
  175.9 1.3 collective-permute-done.9
  177.2 1.5 collective-permute-start.14
  178.7 4.3 %collective-permute-done.8 = bf16[144,288]{1,0:T(8,128)(2,1)S(1)} collective-permute-done((bf16[144,288]{1,0:T(8,128)(2,1)S(1)}, bf16[144,288]{1,0:T(8,128)(2,1)S(1)}, u32[]{:S(2)}, u32[]{:S(2)}) %collective-permute-start.8) | collective-permute-done | bytes 82976 | tf_op jit(solution)/shard_map/ppermute | solution.py:1031
  184.6 40.7 %close_layer.1 = (f32[288,1024]{1,0:T(8,128)}, bf16[288,1024]{1,0:T(8,128)(2,1)}, bf16[1152,896]{1,0:T(8,128)(2,1)}, f32[144,1000]{1,0:T(8,128)}, f32[6,144,288]{2,1,0:T(8,128)}, /*index=5*/f32[16,384]{1,0:T(8,128)}) custom-call(bf16[896,1024]{1,0:T(8,128)(2,1)} %get-tuple-element.47.gproj_ref, bf16[1152,896]{1,0:T(8,128)(2,1)} %get-tuple-element.48.wback_ref, ...), custom_call_target="tpu_custom_call" | custom-call | flops 30000001024 | tf_op jit(solution)/shard_map/close_layer/pallas_call | solution.py:971
  225.3 1.3 slice.15
  227.3 2.3 dynamic-slice_bitcast_fusion.2
  232.4 2.0 fusion.1
  234.6 2.7 collective-permute-start.13
  238.2 1.8 fusion
  240.1 2.9 collective-permute-start.17
  243.1 10.8 %collective-permute-done.2 = bf16[4,144,896]{2,1,0:T(8,128)(2,1)} collective-permute-done((bf16[4,144,896]{2,1,0:T(8,128)(2,1)}, bf16[4,144,896]{2,1,0:T(8,128)(2,1)}, u32[]{:S(2)}, u32[]{:S(2)}) %collective-permute-start.2) | collective-permute-done | bytes 1032224 | tf_op jit(solution)/shard_map/ppermute | solution.py:1020
  253.8 1.4 collective-permute-start.16
  255.2 1.5 fusion.2
  256.8 3.0 collective-permute-start.15
  259.8 20.7 %collective-permute-done.12 = bf16[144,1152]{1,0:T(8,128)(2,1)S(1)} collective-permute-done((bf16[144,1152]{1,0:T(8,128)(2,1)S(1)}, bf16[144,1152]{1,0:T(8,128)(2,1)S(1)}, u32[]{:S(2)}, u32[]{:S(2)}) %collective-permute-start.12) | collective-permute-done | bytes 331808 | tf_op jit(solution)/shard_map/ppermute | solution.py:1031
  280.6 4.1 %collective-permute-start.4 = (bf16[144,896]{1,0:T(8,128)(2,1)S(1)}, bf16[144,896]{1,0:T(8,128)(2,1)S(1)}, u32[]{:S(2)}, u32[]{:S(2)}) collective-permute-start(bf16[144,896]{1,0:T(8,128)(2,1)S(1)} %get-tuple-element.100), channel_id=1, source_target_pairs={{0,16},{4,20},{8,24},{12,28},{16,0},{20,4},{24,8},{28,12},{1,17},{... | collective-permute-start | bytes 774152 | tf_op jit(solution)/shard_map/ppermute | solution.py:1031
  285.7 14.4 %collective-permute-start.3 = (bf16[144,896]{1,0:T(8,128)(2,1)S(1)}, bf16[144,896]{1,0:T(8,128)(2,1)S(1)}, u32[]{:S(2)}, u32[]{:S(2)}) collective-permute-start(bf16[144,896]{1,0:T(8,128)(2,1)S(1)} %get-tuple-element.98), channel_id=1, source_target_pairs={{0,8},{4,12},{8,16},{12,20},{16,24},{20,28},{24,0},{28,4},{1,9},{5... | collective-permute-start | bytes 774152 | tf_op jit(solution)/shard_map/ppermute | solution.py:1031
  300.0 6.5 %collective-permute-done.16 = bf16[144,1152]{1,0:T(8,128)(2,1)S(1)} collective-permute-done((bf16[144,1152]{1,0:T(8,128)(2,1)S(1)}, bf16[144,1152]{1,0:T(8,128)(2,1)S(1)}, u32[]{:S(2)}, u32[]{:S(2)}) %collective-permute-start.16) | collective-permute-done | bytes 331808 | tf_op jit(solution)/shard_map/ppermute | solution.py:1031
  307.6 8.3 %collective-permute-done.4 = bf16[144,896]{1,0:T(8,128)(2,1)S(1)} collective-permute-done((bf16[144,896]{1,0:T(8,128)(2,1)S(1)}, bf16[144,896]{1,0:T(8,128)(2,1)S(1)}, u32[]{:S(2)}, u32[]{:S(2)}) %collective-permute-start.4) | collective-permute-done | bytes 258080 | tf_op jit(solution)/shard_map/ppermute | solution.py:1031
  (67 shorter events, 22.1 us)
Async XLA Ops:
  8.0 33.7 %copy-start.7 = (bf16[3,3,288]{2,1,0:T(4,128)(2,1)S(1)}, bf16[3,3,288]{2,1,0:T(4,128)(2,1)}, u32[]{:S(2)}) copy-start(bf16[3,3,288]{2,1,0:T(4,128)(2,1)} %param.23) | copy-start | bytes 15556
  40.0 15.9 %collective-permute-start = (bf16[288,1024]{1,0:T(8,128)(2,1)}, bf16[288,1024]{1,0:T(8,128)(2,1)S(1)}, u32[]{:S(2)}, u32[]{:S(2)}) collective-permute-start(bf16[288,1024]{1,0:T(8,128)(2,1)} %get-tuple-element.45.gmlp_ref), channel_id=1, source_target_pairs={{0,2},{1,3},{2,0},{3,1},{4,6},{5,7},{6,4},{7,5},{8,10},{9,11},{10,... | collective-permute-start | bytes 1769480 | tf_op jit(solution)/shard_map/ppermute | solution.py:1075
  55.9 0.8 copy-start.8
  144.4 39.4 %collective-permute-start.1 = (bf16[288,1024]{1,0:T(8,128)(2,1)}, bf16[288,1024]{1,0:T(8,128)(2,1)S(1)}, u32[]{:S(2)}, u32[]{:S(2)}) collective-permute-start(bf16[288,1024]{1,0:T(8,128)(2,1)} %get-tuple-element.54), channel_id=1, source_target_pairs={{0,2},{1,3},{2,0},{3,1},{4,6},{5,7},{6,4},{7,5},{8,10},{9,11},{10,... | collective-permute-start | bytes 1769480 | tf_op jit(solution)/shard_map/ppermute | solution.py:1090
  146.9 23.0 %collective-permute-start.6 = (bf16[4,144,288]{2,1,0:T(8,128)(2,1)S(1)}, bf16[4,144,288]{2,1,0:T(8,128)(2,1)S(1)}, u32[]{:S(2)}, u32[]{:S(2)}) collective-permute-start(bf16[4,144,288]{2,1,0:T(8,128)(2,1)S(1)} %dynamic-slice_bitcast_fusion.3), channel_id=1, source_target_pairs={{0,4},{4,0},{8,12},{12,8},{16,20},{20,16},{24,28},{28,24},{1,5},{5... | collective-permute-start | bytes 995336 | tf_op jit(solution)/shard_map/ppermute | solution.py:1020
  151.0 81.5 %collective-permute-start.10 = (bf16[4,144,1152]{2,1,0:T(8,128)(2,1)}, bf16[4,144,1152]{2,1,0:T(8,128)(2,1)}, u32[]{:S(2)}, u32[]{:S(2)}) collective-permute-start(bf16[4,144,1152]{2,1,0:T(8,128)(2,1)} %dynamic-slice_bitcast_fusion.1), channel_id=1, source_target_pairs={{0,4},{4,0},{8,12},{12,8},{16,20},{20,16},{24,28},{28,24},{1,5},{5... | collective-permute-start | bytes 3981320 | tf_op jit(solution)/shard_map/ppermute | solution.py:1020
  151.5 18.4 %copy-start.4 = (bf16[1152,288]{1,0:T(8,128)(2,1)S(1)}, bf16[1152,288]{1,0:T(8,128)(2,1)}, u32[]{:S(2)}) copy-start(bf16[1152,288]{1,0:T(8,128)(2,1)} %get-tuple-element.63) | copy-start | bytes 1990660
  151.5 23.3 %copy-start = (bf16[1152,1152]{1,0:T(8,128)(2,1)S(1)}, bf16[1152,1152]{1,0:T(8,128)(2,1)}, u32[]{:S(2)}) copy-start(bf16[1152,1152]{1,0:T(8,128)(2,1)} %get-tuple-element.65) | copy-start | bytes 7962628
  170.1 7.2 %collective-permute-start.9 = (bf16[144,288]{1,0:T(8,128)(2,1)S(1)}, bf16[144,288]{1,0:T(8,128)(2,1)S(1)}, u32[]{:S(2)}, u32[]{:S(2)}) collective-permute-start(bf16[144,288]{1,0:T(8,128)(2,1)S(1)} %get-tuple-element.102), channel_id=1, source_target_pairs={{0,24},{4,28},{8,0},{12,4},{16,8},{20,12},{24,16},{28,20},{1,25},{... | collective-permute-start | bytes 248840 | tf_op jit(solution)/shard_map/ppermute | solution.py:1031
  173.7 9.3 %collective-permute-start.8 = (bf16[144,288]{1,0:T(8,128)(2,1)S(1)}, bf16[144,288]{1,0:T(8,128)(2,1)S(1)}, u32[]{:S(2)}, u32[]{:S(2)}) collective-permute-start(bf16[144,288]{1,0:T(8,128)(2,1)S(1)} %get-tuple-element.103), channel_id=1, source_target_pairs={{0,16},{4,20},{8,24},{12,28},{16,0},{20,4},{24,8},{28,12},{1,17},{... | collective-permute-start | bytes 248840 | tf_op jit(solution)/shard_map/ppermute | solution.py:1031
  173.7 9.3 %collective-permute-start.7 = (bf16[144,288]{1,0:T(8,128)(2,1)S(1)}, bf16[144,288]{1,0:T(8,128)(2,1)S(1)}, u32[]{:S(2)}, u32[]{:S(2)}) collective-permute-start(bf16[144,288]{1,0:T(8,128)(2,1)S(1)} %get-tuple-element.101), channel_id=1, source_target_pairs={{0,8},{4,12},{8,16},{12,20},{16,24},{20,28},{24,0},{28,4},{1,9},{5... | collective-permute-start | bytes 248840 | tf_op jit(solution)/shard_map/ppermute | solution.py:1031
  177.2 61.0 %collective-permute-start.14 = (bf16[4,144,1152]{2,1,0:T(8,128)(2,1)}, bf16[4,144,1152]{2,1,0:T(8,128)(2,1)}, u32[]{:S(2)}, u32[]{:S(2)}) collective-permute-start(bf16[4,144,1152]{2,1,0:T(8,128)(2,1)} %dynamic-slice_bitcast_fusion), channel_id=1, source_target_pairs={{0,4},{4,0},{8,12},{12,8},{16,20},{20,16},{24,28},{28,24},{1,5},{5... | collective-permute-start | bytes 3981320 | tf_op jit(solution)/shard_map/ppermute | solution.py:1020
  183.8 0.8 copy-start.9
  229.6 24.2 %collective-permute-start.2 = (bf16[4,144,896]{2,1,0:T(8,128)(2,1)}, bf16[4,144,896]{2,1,0:T(8,128)(2,1)}, u32[]{:S(2)}, u32[]{:S(2)}) collective-permute-start(bf16[4,144,896]{2,1,0:T(8,128)(2,1)} %dynamic-slice_bitcast_fusion.2), channel_id=1, source_target_pairs={{0,4},{4,0},{8,12},{12,8},{16,20},{20,16},{24,28},{28,24},{1,5},{5... | collective-permute-start | bytes 3096584 | tf_op jit(solution)/shard_map/ppermute | solution.py:1020
  234.6 22.2 %collective-permute-start.13 = (bf16[144,1152]{1,0:T(8,128)(2,1)S(1)}, bf16[144,1152]{1,0:T(8,128)(2,1)S(1)}, u32[]{:S(2)}, u32[]{:S(2)}) collective-permute-start(bf16[144,1152]{1,0:T(8,128)(2,1)S(1)} %get-tuple-element.96), channel_id=1, source_target_pairs={{0,24},{4,28},{8,0},{12,4},{16,8},{20,12},{24,16},{28,20},{1,25},{... | collective-permute-start | bytes 995336 | tf_op jit(solution)/shard_map/ppermute | solution.py:1031
  237.3 43.3 %collective-permute-start.12 = (bf16[144,1152]{1,0:T(8,128)(2,1)S(1)}, bf16[144,1152]{1,0:T(8,128)(2,1)S(1)}, u32[]{:S(2)}, u32[]{:S(2)}) collective-permute-start(bf16[144,1152]{1,0:T(8,128)(2,1)S(1)} %get-tuple-element.97), channel_id=1, source_target_pairs={{0,16},{4,20},{8,24},{12,28},{16,0},{20,4},{24,8},{28,12},{1,17},{... | collective-permute-start | bytes 995336 | tf_op jit(solution)/shard_map/ppermute | solution.py:1031
  237.3 43.3 %collective-permute-start.11 = (bf16[144,1152]{1,0:T(8,128)(2,1)S(1)}, bf16[144,1152]{1,0:T(8,128)(2,1)S(1)}, u32[]{:S(2)}, u32[]{:S(2)}) collective-permute-start(bf16[144,1152]{1,0:T(8,128)(2,1)S(1)} %get-tuple-element.95), channel_id=1, source_target_pairs={{0,8},{4,12},{8,16},{12,20},{16,24},{20,28},{24,0},{28,4},{1,9},{5... | collective-permute-start | bytes 995336 | tf_op jit(solution)/shard_map/ppermute | solution.py:1031
  238.2 17.0 %copy-start.1 = (bf16[1152,896]{1,0:T(8,128)(2,1)S(1)}, bf16[1152,896]{1,0:T(8,128)(2,1)}, u32[]{:S(2)}) copy-start(bf16[1152,896]{1,0:T(8,128)(2,1)} %get-tuple-element.62) | copy-start | bytes 6193156
  240.1 45.5 %collective-permute-start.17 = (bf16[144,1152]{1,0:T(8,128)(2,1)S(1)}, bf16[144,1152]{1,0:T(8,128)(2,1)S(1)}, u32[]{:S(2)}, u32[]{:S(2)}) collective-permute-start(bf16[144,1152]{1,0:T(8,128)(2,1)S(1)} %get-tuple-element.93), channel_id=1, source_target_pairs={{0,24},{4,28},{8,0},{12,4},{16,8},{20,12},{24,16},{28,20},{1,25},{... | collective-permute-start | bytes 995336 | tf_op jit(solution)/shard_map/ppermute | solution.py:1031
  253.8 52.8 %collective-permute-start.16 = (bf16[144,1152]{1,0:T(8,128)(2,1)S(1)}, bf16[144,1152]{1,0:T(8,128)(2,1)S(1)}, u32[]{:S(2)}, u32[]{:S(2)}) collective-permute-start(bf16[144,1152]{1,0:T(8,128)(2,1)S(1)} %get-tuple-element.94), channel_id=1, source_target_pairs={{0,16},{4,20},{8,24},{12,28},{16,0},{20,4},{24,8},{28,12},{1,17},{... | collective-permute-start | bytes 995336 | tf_op jit(solution)/shard_map/ppermute | solution.py:1031
  256.8 49.8 %collective-permute-start.15 = (bf16[144,1152]{1,0:T(8,128)(2,1)S(1)}, bf16[144,1152]{1,0:T(8,128)(2,1)S(1)}, u32[]{:S(2)}, u32[]{:S(2)}) collective-permute-start(bf16[144,1152]{1,0:T(8,128)(2,1)S(1)} %get-tuple-element.92), channel_id=1, source_target_pairs={{0,8},{4,12},{8,16},{12,20},{16,24},{20,28},{24,0},{28,4},{1,9},{5... | collective-permute-start | bytes 995336 | tf_op jit(solution)/shard_map/ppermute | solution.py:1031
  280.6 27.1 %collective-permute-start.5 = (bf16[144,896]{1,0:T(8,128)(2,1)S(1)}, bf16[144,896]{1,0:T(8,128)(2,1)S(1)}, u32[]{:S(2)}, u32[]{:S(2)}) collective-permute-start(bf16[144,896]{1,0:T(8,128)(2,1)S(1)} %get-tuple-element.99), channel_id=1, source_target_pairs={{0,24},{4,28},{8,0},{12,4},{16,8},{20,12},{24,16},{28,20},{1,25},{... | collective-permute-start | bytes 774152 | tf_op jit(solution)/shard_map/ppermute | solution.py:1031
  280.6 35.3 %collective-permute-start.4 = (bf16[144,896]{1,0:T(8,128)(2,1)S(1)}, bf16[144,896]{1,0:T(8,128)(2,1)S(1)}, u32[]{:S(2)}, u32[]{:S(2)}) collective-permute-start(bf16[144,896]{1,0:T(8,128)(2,1)S(1)} %get-tuple-element.100), channel_id=1, source_target_pairs={{0,16},{4,20},{8,24},{12,28},{16,0},{20,4},{24,8},{28,12},{1,17},{... | collective-permute-start | bytes 774152 | tf_op jit(solution)/shard_map/ppermute | solution.py:1031
  285.7 30.2 %collective-permute-start.3 = (bf16[144,896]{1,0:T(8,128)(2,1)S(1)}, bf16[144,896]{1,0:T(8,128)(2,1)S(1)}, u32[]{:S(2)}, u32[]{:S(2)}) collective-permute-start(bf16[144,896]{1,0:T(8,128)(2,1)S(1)} %get-tuple-element.98), channel_id=1, source_target_pairs={{0,8},{4,12},{8,16},{12,20},{16,24},{20,28},{24,0},{28,4},{1,9},{5... | collective-permute-start | bytes 774152 | tf_op jit(solution)/shard_map/ppermute | solution.py:1031
  316.0 2.1 copy-start.6
  316.1 2.8 copy-start.3
  318.1 1.8 copy-start.5
  318.9 1.8 copy-start.2
